TPU v7x, 32 devices: a whole 2x2x4 slice. The times are simulated.
32 devices in a mesh: seq: 8 (over y, x, core), wt: 4 (over z).
Axes of the slice: x: 2, y: 2, z: 4, core: 2. Of those that a mesh axis runs over, the one named last changes fastest.
Arguments:
- tokens: bfloat16 [8192, 1024], P(('wt', 'seq')), may hold values from -6 to 6
- cotangent: bfloat16 [8192, 1024], P(('wt', 'seq')), may hold values from -6 to 6
- w_qkv: bfloat16 [1024, 3072], P('wt'), may hold values from -0.1875 to 0.1875
- qv_bias: float32 [2, 1024], replicated, may hold values from -3 to 3
- w_out: bfloat16 [1024, 1024], P('wt'), may hold values from -1 to 1
- out_bias: float32 [1024], replicated, may hold values from -3 to 3
- norm1_gain: float32 [1024], replicated, may hold values from 0.1 to 1.9
- norm1_bias: float32 [1024], replicated, may hold values from -1.75 to 1.75
- w_fc1: bfloat16 [1024, 4096], P('wt'), may hold values from -0.1875 to 0.1875
- fc1_bias: float32 [4096], replicated, may hold values from -3 to 3
- w_fc2: bfloat16 [4096, 1024], P('wt'), may hold values from -0.09375 to 0.09375
- fc2_bias: float32 [1024], replicated, may hold values from -3 to 3
- norm2_gain: float32 [1024], replicated, may hold values from 0.1 to 1.9
- norm2_bias: float32 [1024], replicated, may hold values from -1.75 to 1.75
- doc_lengths: int32 [4, 4], P('wt'), may hold values from 1 to 1024, as said below
- adapter_ids: int32 [4, 4], P('wt'), may hold values from 0 to 7
- attn_down: bfloat16 [4, 8, 1024, 16], replicated, may hold values from -0.1875 to 0.1875
- attn_up: bfloat16 [4, 8, 16, 1024], replicated, may hold values from -1.5 to 1.5
- fc1_down: bfloat16 [8, 1024, 16], replicated, may hold values from -0.1875 to 0.1875
- fc1_up: bfloat16 [8, 16, 4096], replicated, may hold values from -1.5 to 1.5
- fc2_down: bfloat16 [8, 4096, 16], replicated, may hold values from -0.09375 to 0.09375
- fc2_up: bfloat16 [8, 16, 1024], replicated, may hold values from -1.5 to 1.5
Outputs:
- output: float32 [8192, 1024], P(('wt', 'seq'))
- input_grad: float32 [8192, 1024], P(('wt', 'seq'))
- grad_attn_down: float32 [4, 8, 1024, 16], replicated
- grad_attn_up: float32 [4, 8, 16, 1024], replicated
- grad_fc1_down: float32 [8, 1024, 16], replicated
- grad_fc1_up: float32 [8, 16, 4096], replicated
- grad_fc2_down: float32 [8, 4096, 16], replicated
- grad_fc2_up: float32 [8, 16, 1024], replicated
Inputs may be any that keep to these rules, and one draw needn't show every extreme that they name: `doc_lengths`: row s lists in order the lengths of the 4 documents of group s and sums to 2048; in every row exactly one document has 1024 tokens and every other document has fewer.
All inputs are finite; a program needn't handle non-finite values.
Results may differ from a plain program's by a relative error of at most 0.018.
The roundings to bfloat16 on the way count: a program that leaves them out, or rounds other values in their place, can miss the bound.
Values may be sent and summed in bfloat16 or wider, within the bound.
A program may use at most 128 MiB of HBM per device.

v0:
```python
import jax
import jax.numpy as jnp
from jax import lax
from jax.sharding import PartitionSpec as P

HEADS = 16
HEAD_DIM = 64


def layer_norm(value, gain, shift):
    mean = jnp.mean(value, axis=-1, keepdims=True)
    centred = value - mean
    spread = jnp.mean(centred * centred, axis=-1, keepdims=True)
    return centred * lax.rsqrt(spread + 1e-05) * gain + shift


def gelu_exact(value):
    return jax.nn.gelu(value, approximate=False)


def times_transposed(grad, weight):
    return lax.dot_general(
        grad, weight, (((1,), (1,)), ((), ())), preferred_element_type=jnp.float32
    )


def left_inner(left, right):
    return lax.dot_general(
        left, right, (((0,), (0,)), ((), ())), preferred_element_type=jnp.float32
    )


def stack_down(down):
    return jnp.transpose(down, (1, 0, 2)).reshape(down.shape[1], down.shape[0] * down.shape[2])


def stack_up(up):
    return up.reshape(up.shape[0] * up.shape[1], up.shape[2])


def unstack_down(stacked, adapter_count, rank_size):
    return jnp.transpose(stacked.reshape(stacked.shape[0], adapter_count, rank_size), (1, 0, 2))


def unstack_up(stacked, adapter_count, rank_size):
    return stacked.reshape(adapter_count, rank_size, stacked.shape[1])


def segment_of(positions, starts):
    return jnp.sum((positions[:, None] >= starts[None, :]).astype(jnp.int32), axis=1) - 1


def shards(
    tokens,
    cotangent,
    w_qkv,
    qv_bias,
    w_out,
    out_bias,
    norm1_gain,
    norm1_bias,
    w_fc1,
    fc1_bias,
    w_fc2,
    fc2_bias,
    norm2_gain,
    norm2_bias,
    doc_lengths,
    adapter_ids,
    attn_down,
    attn_up,
    fc1_down,
    fc1_up,
    fc2_down,
    fc2_up,
):
    tok_rows, model_width = tokens.shape
    adapter_count = attn_down.shape[1]
    rank_size = attn_down.shape[3]
    lane_count = adapter_count * rank_size
    seq_count = lax.axis_size("seq")
    if seq_count <= HEADS:
        per_group = HEADS // seq_count
        part_count = 1
    else:
        per_group = 1
        part_count = seq_count // HEADS
    group_count = seq_count // part_count
    group_width = per_group * HEAD_DIM
    row_count = tok_rows // part_count
    query_count = seq_count * row_count
    key_count = seq_count * tok_rows
    seq_index = lax.axis_index("seq")
    part_index = seq_index // group_count
    score_scale = HEAD_DIM ** (-0.5)
    lengths = doc_lengths[0]
    starts = jnp.cumsum(lengths) - lengths
    local_pos = seq_index * tok_rows + jnp.arange(tok_rows, dtype=jnp.int32)
    local_seg = segment_of(local_pos, starts)
    doc_range = jnp.arange(lengths.shape[0], dtype=jnp.int32)
    chosen = jnp.sum(
        jnp.where(local_seg[:, None] == doc_range[None, :], adapter_ids[0][None, :], 0), axis=1
    )
    lane_owner = jnp.arange(lane_count, dtype=jnp.int32) // rank_size
    select = (chosen[:, None] == lane_owner[None, :]).astype(jnp.float32)
    select_three = jnp.tile(select, (1, 3))
    key_seg = segment_of(jnp.arange(key_count, dtype=jnp.int32), starts)
    slot_index = jnp.arange(query_count, dtype=jnp.int32)
    query_seg = segment_of(
        slot_index // row_count * tok_rows + slot_index % row_count * part_count + part_index,
        starts,
    )
    qkv_down = jnp.concatenate([stack_down(attn_down[i]) for i in range(3)], axis=1)
    qkv_up = [stack_up(attn_up[i]) for i in range(3)]
    out_down = stack_down(attn_down[3])
    out_up = stack_up(attn_up[3])
    fc1_down_all = stack_down(fc1_down)
    fc1_up_all = stack_up(fc1_up)
    fc2_down_all = stack_down(fc2_down)
    fc2_up_all = stack_up(fc2_up)
    full_qkv, full_out, full_fc1, full_fc2 = (
        lax.all_gather(w_qkv, "wt", axis=0, tiled=True),
        lax.all_gather(w_out, "wt", axis=0, tiled=True),
        lax.all_gather(w_fc1, "wt", axis=0, tiled=True),
        lax.all_gather(w_fc2, "wt", axis=0, tiled=True),
    )
    qkv_main = jnp.dot(tokens, full_qkv, preferred_element_type=jnp.float32)
    small_qkv = (
        jnp.dot(tokens, qkv_down, preferred_element_type=jnp.float32) * select_three
    ).astype(jnp.bfloat16)
    adapter_qkv = jnp.concatenate(
        [
            jnp.dot(
                small_qkv[:, i * lane_count : (i + 1) * lane_count],
                qkv_up[i],
                preferred_element_type=jnp.float32,
            )
            for i in range(3)
        ],
        axis=1,
    )
    bias_qkv = jnp.concatenate([qv_bias[0], jnp.zeros((model_width,), jnp.float32), qv_bias[1]])
    qkv = (qkv_main + bias_qkv + adapter_qkv).astype(jnp.bfloat16)

    def query_layout(local):
        return local.reshape(row_count, seq_count, group_width)

    def key_layout(local):
        spread = jnp.broadcast_to(
            local.reshape(tok_rows, 1, group_count, group_width),
            (tok_rows, part_count, group_count, group_width),
        )
        return spread.reshape(tok_rows, seq_count, group_width)

    q_heads, k_heads, v_heads = (
        lax.all_to_all(
            query_layout(qkv[:, :model_width]), "seq", split_axis=1, concat_axis=0, tiled=True
        ),
        lax.all_to_all(
            key_layout(qkv[:, model_width : 2 * model_width]),
            "seq",
            split_axis=1,
            concat_axis=0,
            tiled=True,
        ),
        lax.all_to_all(
            key_layout(qkv[:, 2 * model_width :]), "seq", split_axis=1, concat_axis=0, tiled=True
        ),
    )
    q_heads = q_heads.reshape(query_count, per_group, HEAD_DIM)
    k_heads = k_heads.reshape(key_count, per_group, HEAD_DIM)
    v_heads = v_heads.reshape(key_count, per_group, HEAD_DIM)
    block_rows = min(512, query_count)
    block_count = query_count // block_rows

    def scores_of(query_block, seg_block):
        raw_scores = (
            jnp.einsum("qhd,khd->hqk", query_block, k_heads, preferred_element_type=jnp.float32)
            * score_scale
        )
        same_doc = (seg_block[:, None] == key_seg[None, :])[None]
        return jnp.where(same_doc, raw_scores, -1e30)

    def forward_block(carry, inputs):
        query_block, seg_block = inputs
        scores = scores_of(query_block, seg_block)
        row_top = jnp.max(scores, axis=2, keepdims=True)
        log_total = row_top + jnp.log(jnp.sum(jnp.exp(scores - row_top), axis=2, keepdims=True))
        probs = jnp.exp(scores - log_total).astype(jnp.bfloat16)
        block_out = jnp.einsum("hqk,khd->qhd", probs, v_heads, preferred_element_type=jnp.float32)
        return (carry, (block_out.astype(jnp.bfloat16), log_total))

    blocks_q = q_heads.reshape(block_count, block_rows, per_group, HEAD_DIM)
    blocks_seg = query_seg.reshape(block_count, block_rows)
    _, (attended, log_totals) = lax.scan(forward_block, 0, (blocks_q, blocks_seg))
    attended_tok = lax.all_to_all(
        attended.reshape(query_count, 1, group_width),
        "seq",
        split_axis=0,
        concat_axis=1,
        tiled=True,
    ).reshape(tok_rows, model_width)
    out_main = jnp.dot(attended_tok, full_out, preferred_element_type=jnp.float32)
    small_out = (
        jnp.dot(attended_tok, out_down, preferred_element_type=jnp.float32) * select
    ).astype(jnp.bfloat16)
    z_value = out_main + out_bias + jnp.dot(small_out, out_up, preferred_element_type=jnp.float32)
    first_sum = tokens.astype(jnp.float32) + z_value
    first_norm, norm1_back = jax.vjp(
        lambda value: layer_norm(value, norm1_gain, norm1_bias), first_sum
    )
    first_low = first_norm.astype(jnp.bfloat16)
    fc1_main = jnp.dot(first_low, full_fc1, preferred_element_type=jnp.float32)
    small_fc1 = (
        jnp.dot(first_low, fc1_down_all, preferred_element_type=jnp.float32) * select
    ).astype(jnp.bfloat16)
    pre_act = (
        fc1_main + fc1_bias + jnp.dot(small_fc1, fc1_up_all, preferred_element_type=jnp.float32)
    )
    act_value, gelu_back = jax.vjp(gelu_exact, pre_act)
    act_low = act_value.astype(jnp.bfloat16)
    fc2_main = jnp.dot(act_low, full_fc2, preferred_element_type=jnp.float32)
    small_fc2 = (
        jnp.dot(act_low, fc2_down_all, preferred_element_type=jnp.float32) * select
    ).astype(jnp.bfloat16)
    y_value = (
        fc2_main + fc2_bias + jnp.dot(small_fc2, fc2_up_all, preferred_element_type=jnp.float32)
    )
    output, norm2_back = jax.vjp(
        lambda value: layer_norm(value, norm2_gain, norm2_bias), first_norm + y_value
    )
    d_second = norm2_back(cotangent.astype(jnp.float32))[0]
    d_y = d_second.astype(jnp.bfloat16)
    d_act = times_transposed(d_y, full_fc2)
    low_fc2 = (times_transposed(d_y, fc2_up_all) * select).astype(jnp.bfloat16)
    d_act = d_act + times_transposed(low_fc2, fc2_down_all)
    grad_fc2_up = left_inner(small_fc2, d_y)
    grad_fc2_down = left_inner(act_low, low_fc2)
    d_pre = gelu_back(d_act)[0].astype(jnp.bfloat16)
    d_first_low = times_transposed(d_pre, full_fc1)
    low_fc1 = (times_transposed(d_pre, fc1_up_all) * select).astype(jnp.bfloat16)
    d_first_low = d_first_low + times_transposed(low_fc1, fc1_down_all)
    grad_fc1_up = left_inner(small_fc1, d_pre)
    grad_fc1_down = left_inner(first_low, low_fc1)
    d_first = norm1_back(d_second + d_first_low)[0]
    d_z = d_first.astype(jnp.bfloat16)
    d_attended = times_transposed(d_z, full_out)
    low_out = (times_transposed(d_z, out_up) * select).astype(jnp.bfloat16)
    d_attended = (d_attended + times_transposed(low_out, out_down)).astype(jnp.bfloat16)
    grad_out_up = left_inner(small_out, d_z)
    grad_out_down = left_inner(attended_tok, low_out)
    d_heads = lax.all_to_all(
        query_layout(d_attended), "seq", split_axis=1, concat_axis=0, tiled=True
    ).reshape(block_count, block_rows, per_group, HEAD_DIM)

    def backward_block(carry, inputs):
        d_keys, d_values = carry
        query_block, seg_block, log_total, d_block = inputs
        prob_full = jnp.exp(scores_of(query_block, seg_block) - log_total)
        d_probs = jnp.einsum("qhd,khd->hqk", d_block, v_heads, preferred_element_type=jnp.float32)
        row_dot = jnp.sum(prob_full * d_probs, axis=2, keepdims=True)
        d_raw = (prob_full * (d_probs - row_dot) * score_scale).astype(jnp.bfloat16)
        d_query = jnp.einsum("hqk,khd->qhd", d_raw, k_heads, preferred_element_type=jnp.float32)
        d_keys = d_keys + jnp.einsum(
            "hqk,qhd->khd", d_raw, query_block, preferred_element_type=jnp.float32
        )
        d_values = d_values + jnp.einsum(
            "hqk,qhd->khd",
            prob_full.astype(jnp.bfloat16),
            d_block,
            preferred_element_type=jnp.float32,
        )
        return ((d_keys, d_values), d_query)

    zero_keys = jnp.zeros((key_count, per_group, HEAD_DIM), jnp.float32)
    (d_keys, d_values), d_queries = lax.scan(
        backward_block, (zero_keys, zero_keys), (blocks_q, blocks_seg, log_totals, d_heads)
    )
    back_q, back_k, back_v = (
        lax.all_to_all(
            d_queries.reshape(query_count, 1, group_width).astype(jnp.bfloat16),
            "seq",
            split_axis=0,
            concat_axis=1,
            tiled=True,
        ).astype(jnp.float32),
        lax.all_to_all(
            d_keys.reshape(key_count, 1, group_width).astype(jnp.bfloat16),
            "seq",
            split_axis=0,
            concat_axis=1,
            tiled=True,
        ).astype(jnp.float32),
        lax.all_to_all(
            d_values.reshape(key_count, 1, group_width).astype(jnp.bfloat16),
            "seq",
            split_axis=0,
            concat_axis=1,
            tiled=True,
        ).astype(jnp.float32),
    )
    d_q = back_q.reshape(tok_rows, model_width)
    d_k = jnp.sum(back_k.reshape(tok_rows, part_count, group_count, group_width), axis=1).reshape(
        tok_rows, model_width
    )
    d_v = jnp.sum(back_v.reshape(tok_rows, part_count, group_count, group_width), axis=1).reshape(
        tok_rows, model_width
    )
    d_qkv = jnp.concatenate([d_q, d_k, d_v], axis=1).astype(jnp.bfloat16)
    d_tokens = times_transposed(d_qkv, full_qkv)
    low_qkv = (
        jnp.concatenate(
            [
                times_transposed(d_qkv[:, i * model_width : (i + 1) * model_width], qkv_up[i])
                for i in range(3)
            ],
            axis=1,
        )
        * select_three
    ).astype(jnp.bfloat16)
    input_grad = d_first + d_tokens + times_transposed(low_qkv, qkv_down)
    grad_qkv_down = left_inner(tokens, low_qkv)
    grad_qkv_up = [
        left_inner(
            small_qkv[:, i * lane_count : (i + 1) * lane_count],
            d_qkv[:, i * model_width : (i + 1) * model_width],
        )
        for i in range(3)
    ]
    grad_attn_down = jnp.stack(
        [
            unstack_down(
                grad_qkv_down[:, i * lane_count : (i + 1) * lane_count], adapter_count, rank_size
            )
            for i in range(3)
        ]
        + [unstack_down(grad_out_down, adapter_count, rank_size)]
    )
    grad_attn_up = jnp.stack(
        [
            unstack_up(piece_grad, adapter_count, rank_size)
            for piece_grad in grad_qkv_up + [grad_out_up]
        ]
    )
    summed = lax.psum(
        (
            grad_attn_down,
            grad_attn_up,
            unstack_down(grad_fc1_down, adapter_count, rank_size),
            unstack_up(grad_fc1_up, adapter_count, rank_size),
            unstack_down(grad_fc2_down, adapter_count, rank_size),
            unstack_up(grad_fc2_up, adapter_count, rank_size),
        ),
        ("seq", "wt"),
    )
    return (output, input_grad, summed[0], summed[1], summed[2], summed[3], summed[4], summed[5])


def solution(mesh):
    placed = (
        P(("wt", "seq"), None),
        P(("wt", "seq"), None),
        P("wt", None),
        P(),
        P("wt", None),
        P(),
        P(),
        P(),
        P("wt", None),
        P(),
        P("wt", None),
        P(),
        P(),
        P(),
        P("wt", None),
        P("wt", None),
        P(),
        P(),
        P(),
        P(),
        P(),
        P(),
    )
    return jax.shard_map(
        shards,
        mesh=mesh,
        in_specs=placed,
        out_specs=(P(("wt", "seq"), None), P(("wt", "seq"), None), P(), P(), P(), P(), P(), P()),
        check_vma=False,
    )
```

profile of v0, /device:TPU:0, one launch (start us, length us, event | category | flops | bytes accessed | tf_op | source)
XLA Modules:
  0.0 983.3 jit_solution(12695571320169822331)
XLA Ops:
  14.9 112.9 %all-gather.5.cloned.1.call-done = bf16[1024,3072]{1,0:T(8,128)(2,1)} async-done(((bf16[256,3072]{1,0:T(8,128)(2,1)}), bf16[1024,3072]{1,0:T(8,128)(2,1)}) %all-gather.5.cloned.1.call-update) | async-done | bytes 6291472 | tf_op jit(solution)/shard_map/all_gather | solution.py:122
  127.7 5.1 fusion.93
  138.6 8.9 all-to-all-done
  152.4 8.2 all-to-all-done.1
  167.5 6.3 all-to-all-done.2
  176.3 34.8 %while.27 = (s32[]{:T(128)}, bf16[4,512,2,64]{1,3,2,0:T(8,128)(2,1)}, f32[4,2,512,1]{2,1,3,0:T(2,128)}, s32[4,512]{1,0:T(4,128)S(1)}, s32[2048]{0:T(1024)S(1)}, ...) while((s32[]{:T(128)}, ...), condition=%wide.region_8.9_spmd, body=%wide.region_5.8_spmd.sunk | while | flops 561052672 | bytes 30719076 | solution.py:195
  220.3 12.8 %reduce = bf16[2048,128]{1,0:T(8,128)(2,1)} reduce(bf16[2048,1,128]{2,1,0:T(2,128)(2,1)S(1)} %reshape.406, bf16[]{:T(256)} %broadcast.396), dimensions={1}, to_apply=%reshape.406.reduce_sub_computation | reduce | bytes 1048578 | tf_op jit(solution)/shard_map/reshape | solution.py:197
  239.2 9.7 all-to-all-done.3
  258.5 65.0 %all-gather.9.cloned.1.call-done = bf16[1024,4096]{1,0:T(8,128)(2,1)} async-done(((bf16[256,4096]{1,0:T(8,128)(2,1)}), bf16[1024,4096]{1,0:T(8,128)(2,1)}) %all-gather.9.cloned.1.call-update) | async-done | bytes 8388624 | tf_op jit(solution)/shard_map/all_gather | solution.py:124
  323.5 5.9 convolution_add_fusion.2
  329.4 11.1 %multiply_convert_fusion.1 = (bf16[256,4096]{1,0:T(8,128)(2,1)S(1)}, f32[256,4096]{1,0:T(8,128)}, f32[256,4096]{1,0:T(8,128)}) fusion(f32[256,4096]{1,0:T(8,128)S(1)} %convolution_add_fusion.2, bf16[256,128]{1,0:T(8,128)(2,1)S(1)} %fusion.113, bf16[128,4096]{1,0:T(8,128)(2,1)S(1)} %bitcast.300), kind=kOutput, calls=%fused_computation.74 | convolution fusion | flops 337641472 | bytes 15794176 | tf_op jit(solution)/shard_map/dot_general | solution.py:218
  342.6 130.2 %all-gather.11.cloned.1.call-done = bf16[4096,1024]{1,0:T(8,128)(2,1)} async-done(((bf16[1024,1024]{1,0:T(8,128)(2,1)}), bf16[4096,1024]{1,0:T(8,128)(2,1)}) %all-gather.11.cloned.1.call-update) | async-done | bytes 8388624 | tf_op jit(solution)/shard_map/all_gather | solution.py:125
  472.8 6.4 convolution_add_fusion.10
  487.5 5.8 add_convert_fusion
  512.8 5.2 all-to-all-done.4
  518.7 191.4 %while.28 = (s32[]{:T(128)}, f32[2048,2,64]{0,2,1:T(8,128)}, f32[2048,2,64]{0,2,1:T(8,128)}, bf16[4,512,2,64]{1,3,2,0:T(8,128)(2,1)}, bf16[4,512,2,64]{1,3,2,0:T...) while((s32[]{:T(128)}, f32[2048,2,64]{0,2,1:T(8,128)}, ...), condition=%wide.region_19.20_spmd.clone, body=%wide.region_17.19_spmd.clone.sunk | while | flops 1398806528 | bytes 105163928 | solution.py:276
  530.2 15.0 %fusion.279 = f32[2048,2,64]{0,2,1:T(8,128)} fusion(f32[2,512,2048]{2,1,0:T(8,128)} %fusion.277, f32[2,512,2048]{2,1,0:T(8,128)} %fusion.278, f32[2,512]{1,0:T(2,128)S(1)} %dynamic-slice_bitcast_fusion.2, pred[512,2048]{1,0:T(8,128)(4,1)S(1)} %broadcast_compare_fusion.5, f32[2048,2,64]{0,2,1:T(8,128)} %get-tuple-element.516, pred[]{:T(512)S(6)} %compare.14, ...), kind=kOutput, calls=%fused_computation.40.clone.1 | convolution fusion | flops 292031488 | bytes 37888512 | tf_op jit(solution)/shard_map/while/body/eval_jaxpr/hqk,qhd->khd/dot_general | solution.py:264
  545.2 14.2 %fusion.281 = bf16[4,512,2,64]{1,3,2,0:T(8,128)(2,1)} fusion(bf16[4,512,2,64]{1,3,2,0:T(8,128)(2,1)} %get-tuple-element.518, s32[]{:T(128)} %get-tuple-element.515, bf16[2048,2,64]{0,2,1:T(8,128)(2,1)S(1)} %get-tuple-element.535, f32[2,512,2048]{2,1,0:T(8,128)} %fusion.277, f32[2,512,2048]{2,1,0:T(8,128)} %fusion.278, ...), kind=kOutput, calls=%fused_computation.43.clone.1 | convolution fusion | flops 291507200 | bytes 36446720 | tf_op jit(solution)/shard_map/while/body/eval_jaxpr/hqk,khd->qhd/dot_general | solution.py:263
  559.4 6.9 fusion.280
  577.5 15.3 %fusion.279 = f32[2048,2,64]{0,2,1:T(8,128)} fusion(f32[2,512,2048]{2,1,0:T(8,128)} %fusion.277, f32[2,512,2048]{2,1,0:T(8,128)} %fusion.278, f32[2,512]{1,0:T(2,128)S(1)} %dynamic-slice_bitcast_fusion.2, pred[512,2048]{1,0:T(8,128)(4,1)S(1)} %broadcast_compare_fusion.5, f32[2048,2,64]{0,2,1:T(8,128)} %get-tuple-element.516, pred[]{:T(512)S(6)} %compare.14, ...), kind=kOutput, calls=%fused_computation.40.clone.1 | convolution fusion | flops 292031488 | bytes 37888512 | tf_op jit(solution)/shard_map/while/body/eval_jaxpr/hqk,qhd->khd/dot_general | solution.py:264
  592.9 14.2 %fusion.281 = bf16[4,512,2,64]{1,3,2,0:T(8,128)(2,1)} fusion(bf16[4,512,2,64]{1,3,2,0:T(8,128)(2,1)} %get-tuple-element.518, s32[]{:T(128)} %get-tuple-element.515, bf16[2048,2,64]{0,2,1:T(8,128)(2,1)S(1)} %get-tuple-element.535, f32[2,512,2048]{2,1,0:T(8,128)} %fusion.277, f32[2,512,2048]{2,1,0:T(8,128)} %fusion.278, ...), kind=kOutput, calls=%fused_computation.43.clone.1 | convolution fusion | flops 291507200 | bytes 36446720 | tf_op jit(solution)/shard_map/while/body/eval_jaxpr/hqk,khd->qhd/dot_general | solution.py:263
  607.0 7.2 fusion.280
  625.5 15.3 %fusion.279 = f32[2048,2,64]{0,2,1:T(8,128)} fusion(f32[2,512,2048]{2,1,0:T(8,128)} %fusion.277, f32[2,512,2048]{2,1,0:T(8,128)} %fusion.278, f32[2,512]{1,0:T(2,128)S(1)} %dynamic-slice_bitcast_fusion.2, pred[512,2048]{1,0:T(8,128)(4,1)S(1)} %broadcast_compare_fusion.5, f32[2048,2,64]{0,2,1:T(8,128)} %get-tuple-element.516, pred[]{:T(512)S(6)} %compare.14, ...), kind=kOutput, calls=%fused_computation.40.clone.1 | convolution fusion | flops 292031488 | bytes 37888512 | tf_op jit(solution)/shard_map/while/body/eval_jaxpr/hqk,qhd->khd/dot_general | solution.py:264
  640.8 14.2 %fusion.281 = bf16[4,512,2,64]{1,3,2,0:T(8,128)(2,1)} fusion(bf16[4,512,2,64]{1,3,2,0:T(8,128)(2,1)} %get-tuple-element.518, s32[]{:T(128)} %get-tuple-element.515, bf16[2048,2,64]{0,2,1:T(8,128)(2,1)S(1)} %get-tuple-element.535, f32[2,512,2048]{2,1,0:T(8,128)} %fusion.277, f32[2,512,2048]{2,1,0:T(8,128)} %fusion.278, ...), kind=kOutput, calls=%fused_computation.43.clone.1 | convolution fusion | flops 291507200 | bytes 36446720 | tf_op jit(solution)/shard_map/while/body/eval_jaxpr/hqk,khd->qhd/dot_general | solution.py:263
  655.0 7.2 fusion.280
  673.4 15.3 %fusion.279 = f32[2048,2,64]{0,2,1:T(8,128)} fusion(f32[2,512,2048]{2,1,0:T(8,128)} %fusion.277, f32[2,512,2048]{2,1,0:T(8,128)} %fusion.278, f32[2,512]{1,0:T(2,128)S(1)} %dynamic-slice_bitcast_fusion.2, pred[512,2048]{1,0:T(8,128)(4,1)S(1)} %broadcast_compare_fusion.5, f32[2048,2,64]{0,2,1:T(8,128)} %get-tuple-element.516, pred[]{:T(512)S(6)} %compare.14, ...), kind=kOutput, calls=%fused_computation.40.clone.1 | convolution fusion | flops 292031488 | bytes 37888512 | tf_op jit(solution)/shard_map/while/body/eval_jaxpr/hqk,qhd->khd/dot_general | solution.py:264
  688.8 14.2 %fusion.281 = bf16[4,512,2,64]{1,3,2,0:T(8,128)(2,1)} fusion(bf16[4,512,2,64]{1,3,2,0:T(8,128)(2,1)} %get-tuple-element.518, s32[]{:T(128)} %get-tuple-element.515, bf16[2048,2,64]{0,2,1:T(8,128)(2,1)S(1)} %get-tuple-element.535, f32[2,512,2048]{2,1,0:T(8,128)} %fusion.277, f32[2,512,2048]{2,1,0:T(8,128)} %fusion.278, ...), kind=kOutput, calls=%fused_computation.43.clone.1 | convolution fusion | flops 291507200 | bytes 36446720 | tf_op jit(solution)/shard_map/while/body/eval_jaxpr/hqk,khd->qhd/dot_general | solution.py:263
  702.9 7.2 fusion.280
  714.5 13.0 %reduce.3 = bf16[2048,128]{1,0:T(8,128)(2,1)S(1)} reduce(bf16[2048,1,128]{2,1,0:T(2,128)(2,1)} %reshape.407, bf16[]{:T(256)} %broadcast.396), dimensions={1}, to_apply=%reshape.407.reduce_sub_computation | reduce | bytes 1048578 | tf_op jit(solution)/shard_map/convert_element_type | solution.py:281
  763.7 5.8 all-to-all-done.7
  779.4 6.0 fusion.104
  786.8 180.9 %all-reduce.3.cloned.1.call-done = (f32[4,8,1024,16]{2,3,1,0:T(8,128)}, f32[4,8,16,1024]{3,2,1,0:T(8,128)}, f32[8,1024,16]{1,2,0:T(8,128)}, f32[8,16,4096]{2,1,0...) async-done(((f32[4,8,1024,16]{2,3,1,0:T(8,128)}, f32[4,8,16,1024]{3,2,1,0:T(8,128)}, f32[8,1024,16]{1,2,0:T(8,128)}, f32[8,16,4096]{2,1,0:T(8,128)}, ...) | async-done | bytes 9437200 | tf_op jit(solution)/shard_map/psum | solution.py:345
  (361 shorter events, 222.3 us)
Async XLA Ops:
  7.2 322.2 %copy-start = (bf16[8,16,4096]{2,1,0:T(8,128)(2,1)S(1)}, bf16[8,16,4096]{2,1,0:T(8,128)(2,1)}, u32[]{:S(2)}) copy-start(bf16[8,16,4096]{2,1,0:T(8,128)(2,1)} %param.45) | copy-start | bytes 3145732
  7.2 120.5 %all-gather.5.cloned.1.call-start = ((), (), s32[]{:S(2)}) async-start(), calls=%async_computation.8 | async-start | bytes 7864320 | tf_op jit(solution)/shard_map/all_gather | solution.py:122
  8.0 246.0 %all-gather.7.cloned.1.call-start = ((), (), s32[]{:S(2)}) async-start(), calls=%async_computation.9 | async-start | bytes 2621440 | tf_op jit(solution)/shard_map/all_gather | solution.py:123
  8.7 314.7 %all-gather.9.cloned.1.call-start = ((), (), s32[]{:S(2)}) async-start(), calls=%async_computation.10 | async-start | bytes 10485760 | tf_op jit(solution)/shard_map/all_gather | solution.py:124
  11.4 121.4 %copy-start.48 = (bf16[256,384]{0,1:T(8,128)(2,1)}, bf16[256,384]{0,1:T(8,128)(2,1)S(1)}, u32[]{:S(2)}) copy-start(bf16[256,384]{0,1:T(8,128)(2,1)S(1)} %fusion.109) | copy-start | bytes 589828
  134.0 13.4 %all-to-all-start = ((bf16[256,8,128]{0,2,1:T(8,128)(2,1)}), bf16[256,8,128]{0,2,1:T(8,128)(2,1)S(1)}, u32[]{:S(2)}, u32[]{:S(2)}) async-start(bf16[256,8,128]{0,2,1:T(8,128)(2,1)} %bitcast.23), calls=%async_computation | async-start | bytes 1048576 | tf_op jit(solution)/shard_map/all_to_all | solution.py:156
  147.4 13.2 %all-to-all-start.1 = ((bf16[256,8,128]{2,0,1:T(8,128)(2,1)}), bf16[256,8,128]{2,0,1:T(8,128)(2,1)S(1)}, u32[]{:S(2)}, u32[]{:S(2)}) async-start(bf16[256,8,128]{2,0,1:T(8,128)(2,1)} %bitcast.263), calls=%async_computation.1 | async-start | bytes 1048576 | tf_op jit(solution)/shard_map/all_to_all | solution.py:159
  150.9 321.8 %all-gather.11.cloned.1.call-start = ((), (), s32[]{:S(2)}) async-start(), calls=%async_computation.11 | async-start | bytes 10485760 | tf_op jit(solution)/shard_map/all_gather | solution.py:125
  160.6 13.2 %all-to-all-start.2 = ((bf16[256,8,128]{2,0,1:T(8,128)(2,1)}), bf16[256,8,128]{2,0,1:T(8,128)(2,1)S(1)}, u32[]{:S(2)}, u32[]{:S(2)}) async-start(bf16[256,8,128]{2,0,1:T(8,128)(2,1)} %bitcast.262), calls=%async_computation.2 | async-start | bytes 1048576 | tf_op jit(solution)/shard_map/all_to_all | solution.py:166
  211.1 40.1 %copy-start.58 = (s32[4,512]{1,0:T(4,128)}, s32[4,512]{1,0:T(4,128)S(1)}, u32[]{:S(2)}) copy-start(s32[4,512]{1,0:T(4,128)S(1)} %get-tuple-element.598) | copy-start | bytes 24580
  233.1 20.9 %copy-start.81 = (f32[1024]{0:T(1024)S(1)}, f32[1024]{0:T(1024)}, u32[]{:S(2)}) copy-start(f32[1024]{0:T(1024)} %param.31) | copy-start | bytes 12292
  235.1 13.9 %all-to-all-start.3 = ((bf16[8,2,16384]{2,1,0:T(2,128)(2,1)}), bf16[8,2,16384]{2,1,0:T(2,128)(2,1)}, u32[]{:S(2)}, u32[]{:S(2)}) async-start(bf16[8,2,16384]{2,1,0:T(2,128)(2,1)} %reshape.409), calls=%async_computation.3 | async-start | bytes 1048576 | tf_op jit(solution)/shard_map/all_to_all | solution.py:196
  256.4 67.1 %copy-start.80 = (f32[4096]{0:T(1024)S(1)}, f32[4096]{0:T(1024)}, u32[]{:S(2)}) copy-start(f32[4096]{0:T(1024)} %param.35) | copy-start | bytes 49156
  256.8 72.6 %copy-start.63 = (f32[256]{0:T(256)}, f32[256]{0:T(256)S(1)}, u32[]{:S(2)}) copy-start(f32[256]{0:T(256)S(1)} %broadcast_multiply_fusion.1) | copy-start | bytes 3076
  257.1 72.3 %copy-start.72 = (f32[256]{0:T(256)}, f32[256]{0:T(256)S(1)}, u32[]{:S(2)}) copy-start(f32[256]{0:T(256)S(1)} %multiply_reduce_fusion.4) | copy-start | bytes 3076
  257.1 72.3 %copy-start.68 = (f32[256]{0:T(256)}, f32[256]{0:T(256)S(1)}, u32[]{:S(2)}) copy-start(f32[256]{0:T(256)S(1)} %fusion.149) | copy-start | bytes 3076
  258.5 70.9 %copy-start.52 = (bf16[256,128]{1,0:T(8,128)(2,1)}, bf16[256,128]{1,0:T(8,128)(2,1)S(1)}, u32[]{:S(2)}) copy-start(bf16[256,128]{1,0:T(8,128)(2,1)S(1)} %fusion.113) | copy-start | bytes 196612
  342.5 136.6 %copy-start.61 = (f32[1024]{0:T(1024)S(1)}, f32[1024]{0:T(1024)}, u32[]{:S(2)}) copy-start(f32[1024]{0:T(1024)} %param.32) | copy-start | bytes 12292
  342.5 136.6 %copy-start.64 = (f32[256]{0:T(256)S(1)}, f32[256]{0:T(256)}, u32[]{:S(2)}) copy-start(f32[256]{0:T(256)} %copy-done.63) | copy-start | bytes 3076
  342.6 136.6 %copy-start.67 = (f32[1024]{0:T(1024)S(1)}, f32[1024]{0:T(1024)}, u32[]{:S(2)}) copy-start(f32[1024]{0:T(1024)} %param.33) | copy-start | bytes 12292
  342.6 136.6 %copy-start.69 = (f32[256]{0:T(256)S(1)}, f32[256]{0:T(256)}, u32[]{:S(2)}) copy-start(f32[256]{0:T(256)} %copy-done.68) | copy-start | bytes 3076
  342.6 137.2 %copy-start.71 = (f32[1024]{0:T(1024)S(1)}, f32[1024]{0:T(1024)}, u32[]{:S(2)}) copy-start(f32[1024]{0:T(1024)} %param.38) | copy-start | bytes 12292
  504.6 13.4 %all-to-all-start.4 = ((bf16[256,8,128]{0,2,1:T(8,128)(2,1)}), bf16[256,8,128]{0,2,1:T(8,128)(2,1)S(1)}, u32[]{:S(2)}, u32[]{:S(2)}) async-start(bf16[256,8,128]{0,2,1:T(8,128)(2,1)} %bitcast.45), calls=%async_computation.4 | async-start | bytes 1048576 | tf_op jit(solution)/shard_map/all_to_all | solution.py:252
  710.2 21.7 %copy-start.59 = (bf16[128,256]{1,0:T(8,128)(2,1)S(1)}, bf16[128,256]{1,0:T(8,128)(2,1)}, u32[]{:S(2)}) copy-start(bf16[128,256]{1,0:T(8,128)(2,1)} %get-tuple-element.349) | copy-start | bytes 196612
  712.6 21.5 %copy-start.4 = (bf16[256,4096]{1,0:T(8,128)(2,1)S(1)}, bf16[256,4096]{1,0:T(8,128)(2,1)}, u32[]{:S(2)}) copy-start(bf16[256,4096]{1,0:T(8,128)(2,1)} %copy-done.3) | copy-start | bytes 6291460
  712.6 21.5 %copy-start.53 = (bf16[256,128]{1,0:T(8,128)(2,1)S(1)}, bf16[256,128]{1,0:T(8,128)(2,1)}, u32[]{:S(2)}) copy-start(bf16[256,128]{1,0:T(8,128)(2,1)} %copy-done.52) | copy-start | bytes 196612
  728.4 13.2 %all-to-all-start.5 = ((bf16[8,2,16384]{2,1,0:T(2,128)(2,1)}), bf16[8,2,16384]{2,1,0:T(2,128)(2,1)S(1)}, u32[]{:S(2)}, u32[]{:S(2)}) async-start(bf16[8,2,16384]{2,1,0:T(2,128)(2,1)} %reshape.415), calls=%async_computation.5 | async-start | bytes 1048576 | tf_op jit(solution)/shard_map/all_to_all | solution.py:280
  742.4 13.2 %all-to-all-start.6 = ((bf16[8,2,16384]{2,1,0:T(2,128)(2,1)}), bf16[8,2,16384]{2,1,0:T(2,128)(2,1)S(1)}, u32[]{:S(2)}, u32[]{:S(2)}) async-start(bf16[8,2,16384]{2,1,0:T(2,128)(2,1)} %reshape.413), calls=%async_computation.6 | async-start | bytes 1048576 | tf_op jit(solution)/shard_map/all_to_all | solution.py:287
  755.6 13.9 %all-to-all-start.7 = ((bf16[8,2,16384]{2,1,0:T(2,128)(2,1)}), bf16[8,2,16384]{2,1,0:T(2,128)(2,1)}, u32[]{:S(2)}, u32[]{:S(2)}) async-start(bf16[8,2,16384]{2,1,0:T(2,128)(2,1)} %reshape.411), calls=%async_computation.7 | async-start | bytes 1048576 | tf_op jit(solution)/shard_map/all_to_all | solution.py:294
  759.7 208.0 %all-reduce.3.cloned.1.call-start = ((), (), s32[]{:S(2)}) async-start(), calls=%async_computation.12 | async-start | bytes 18874368 | tf_op jit(solution)/shard_map/psum | solution.py:345
  760.8 12.7 %copy-start.31 = (f32[256,128]{0,1:T(8,128)S(1)}, f32[256,128]{0,1:T(8,128)}, u32[]{:S(2)}) copy-start(f32[256,128]{0,1:T(8,128)} %copy-done.30) | copy-start | bytes 393220
  761.7 12.9 %copy-start.24 = (bf16[256,1024]{1,0:T(8,128)(2,1)S(1)}, bf16[256,1024]{1,0:T(8,128)(2,1)}, u32[]{:S(2)}) copy-start(bf16[256,1024]{1,0:T(8,128)(2,1)} %param.26) | copy-start | bytes 1572868
  (66 other events, 269.8 us)
Sparse Core Ops, SparseCore 0:
  9.6 118.0 all-gather.4
  129.3 44.1 all-gather.6
  175.1 148.3 all-gather.8
  324.9 147.8 all-gather.10
  778.3 189.3 all-reduce.2
where the time goes:
time: 994 us; the launch traced here: 983 us
  waiting for transfers between devices  541 us (54%)
  matrix products  283 us (28%)
  local copies, waits for them, and re-layouts  60.4 us (6%)
  other arithmetic  53.4 us (5%)
  starting transfers between devices  29.8 us (3%)
  between operations  15.4 us (2%)
    psum x1, waiting for transfers between devices, shards(): lax.psum((grad_attn_down, grad_attn_up, unstack_down(grad_fc1_down, adapt...  181 us
    all_gather x1, waiting for transfers between devices, shards(): lax.all_gather(w_fc2, 'wt', axis=0, tiled=True)  130 us
    all_gather x1, waiting for transfers between devices, shards(): lax.all_gather(w_qkv, 'wt', axis=0, tiled=True)  113 us
    all_gather x1, waiting for transfers between devices, shards(): lax.all_gather(w_fc1, 'wt', axis=0, tiled=True)  65 us
    dot_general x4, matrix products, backward_block(): jnp.einsum('hqk,qhd->khd', d_raw, query_block, preferred_element_type=jnp...  61 us
    dot_general x4, matrix products, backward_block(): jnp.einsum('hqk,khd->qhd', d_raw, k_heads, preferred_element_type=jnp.flo...  56.6 us
    unnamed x192, local copies, waits for them, and re-layouts  28.7 us
    dot_general x4, matrix products, backward_block(): jnp.einsum('hqk,qhd->khd', prob_full.astype(jnp.bfloat16), d_block, prefe...  28.7 us
  transfers between devices with their start and end apart: 13, of which 12 were waited for; matrix products, arithmetic and copies ran while one was open for 13% of the time, Pallas kernels for 0%

commit v1 on v0

v1 whole, which is shorter than its diff:
```python
import functools

import jax
import jax.numpy as jnp
from jax import lax
from jax.experimental import pallas as pl
from jax.experimental.pallas import tpu as pltpu
from jax.sharding import PartitionSpec as P

HEADS = 16
HEAD_DIM = 64
LANES = 128
PAIR = LANES // HEAD_DIM
MESH = pl.DeviceIdType.MESH
F32 = jnp.float32
BF16 = jnp.bfloat16
VMEM_LIMIT = 60 * 2**20


def dot_nn(a, b):
    return lax.dot_general(a, b, (((1,), (0,)), ((), ())), preferred_element_type=F32)


def dot_nt(a, b):
    return lax.dot_general(a, b, (((1,), (1,)), ((), ())), preferred_element_type=F32)


def dot_tn(a, b):
    return lax.dot_general(a, b, (((0,), (0,)), ((), ())), preferred_element_type=F32)


class Geometry:
    def __init__(self, rows, width):
        self.seq = lax.axis_size("seq")
        self.wt = lax.axis_size("wt")
        self.rows = rows
        self.width = width
        self.groups = width // LANES
        self.parts = self.seq // self.groups
        chips = self.seq // 2
        nx = 1
        while nx * nx < chips:
            nx *= 2
        self.nx = nx
        self.ny = chips // nx
        self.keys = self.seq * rows
        self.queries = self.groups * rows


def doc_bounds(len_ref):
    count = len_ref.shape[1]
    starts, ends = [], []
    at = jnp.int32(0)
    for i in range(count):
        starts.append(at)
        at = at + len_ref[0, i]
        ends.append(at)
    return starts, ends


def segment_from(positions, starts):
    seg = jnp.zeros_like(positions)
    for start in starts[1:]:
        seg = seg + (positions >= start).astype(jnp.int32)
    return seg


def select_from(positions, starts, ends, id_ref, rank):
    owner = lax.broadcasted_iota(jnp.int32, positions.shape, 1) // rank
    picked = jnp.zeros(positions.shape, F32)
    for i in range(len(starts)):
        inside = (positions >= starts[i]) & (positions < ends[i]) & (owner == id_ref[0, i])
        picked = jnp.where(inside, 1.0, picked)
    return picked


class Spread:
    KINDS = 9

    def __init__(self, geo, here, region, send, recv, unit):
        self.geo, self.here, self.region = geo, here, region
        self.send, self.recv, self.unit = send, recv, unit

    def copy(self, kind, src, dst, x, y, core):
        return pltpu.make_async_remote_copy(
            src_ref=src,
            dst_ref=dst,
            send_sem=self.send.at[kind, self.unit],
            recv_sem=self.recv.at[kind, self.unit],
            device_id=(((y * self.geo.nx) + x) * 2 + core, self.here[3]),
            device_id_type=MESH,
        )

    def others(self):
        nx, ny = self.geo.nx, self.geo.ny
        x, y, core, _ = self.here
        row = [((x + d) % nx, y) for d in range(1, nx)]
        col = [(x, (y + d) % ny) for d in range(1, ny)]
        return row, col

    def plan(self):
        x, y, core, _ = self.here
        row, col = self.others()
        plan = {kind: [] for kind in range(self.KINDS)}
        for tx, ty in row:
            plan[0].append(((x, y), None, (tx, ty, core)))
        for tx, ty in col:
            plan[1].append(((x, y), None, (tx, ty, core)))
        for ux, uy in row:
            for tx, ty in col:
                plan[2].append(((ux, uy), 0, (tx, ty, core)))
        for ux, uy in col:
            for tx, ty in row:
                plan[3].append(((ux, uy), 1, (tx, ty, core)))
        plan[4].append(((x, y), None, (x, y, 1 - core)))
        for ux, uy in row:
            plan[5].append(((ux, uy), None, (x, y, 1 - core)))
        for ux, uy in col:
            plan[6].append(((ux, uy), None, (x, y, 1 - core)))
        for ux, _ in row:
            for _, uy in col:
                plan[7].append(((ux, uy), 0, (x, y, 1 - core)))
                plan[8].append(((ux, uy), 1, (x, y, 1 - core)))
        return plan

    def go(self, kind, own=None):
        core = self.here[2]
        for (ux, uy), half, (tx, ty, tcore) in self.plan()[kind]:
            dst = self.region(ux, uy, core, half)
            src = dst if own is None else own
            self.copy(kind, src, dst, tx, ty, tcore).start()

    def arrivals(self, kind):
        x, y, core, _ = self.here
        row, col = self.others()
        if kind == 0:
            return [(u, None, core) for u in row]
        if kind == 1:
            return [(u, None, core) for u in col]
        if kind in (2, 3):
            return [((ux, uy), kind - 2, core) for ux, _ in row for _, uy in col]
        if kind == 4:
            return [((x, y), None, 1 - core)]
        if kind == 5:
            return [(u, None, 1 - core) for u in row]
        if kind == 6:
            return [(u, None, 1 - core) for u in col]
        return [((ux, uy), kind - 7, 1 - core) for ux, _ in row for _, uy in col]

    def wait(self, kind):
        x, y, core, _ = self.here
        for (ux, uy), half, whose in self.arrivals(kind):
            ref = self.region(ux, uy, whose, half)
            self.copy(kind, ref, ref, x, y, 1 - core).wait_recv()

    def wait_sends(self):
        x, y, core, _ = self.here
        for kind in range(self.KINDS):
            for (ux, uy), half, _ in self.plan()[kind]:
                ref = self.region(ux, uy, core, half)
                self.copy(kind, ref, ref, x, y, 1 - core).wait_send()


def device_here(geo):
    s = lax.axis_index("seq")
    core = s % 2
    chip = s // 2
    return chip % geo.nx, chip // geo.nx, core, lax.axis_index("wt")


def greet(geo):
    s, w = lax.axis_index("seq"), lax.axis_index("wt")
    barrier = pltpu.get_barrier_semaphore()
    for d in range(1, geo.seq):
        pl.semaphore_signal(barrier, inc=1, device_id=((s + d) % geo.seq, w), device_id_type=MESH)
    for d in range(1, geo.wt):
        pl.semaphore_signal(barrier, inc=1, device_id=(s, (w + d) % geo.wt), device_id_type=MESH)
    pl.semaphore_wait(barrier, geo.seq + geo.wt - 2)


def forward_kernel(
    geo,
    weight_count,
    rank,
    len_ref,
    id_ref,
    tokens_ref,
    wqkv_ref,
    down_ref,
    up_ref,
    bias_ref,
    *refs,
):
    weights_in = refs[:weight_count]
    att_ref, q_ref, k_ref, v_ref, o_ref, lse_ref, slice_ref, small_ref = refs[weight_count : weight_count + 8]
    weights_out = refs[weight_count + 8 : 2 * weight_count + 8]
    (
        tok_buf,
        seg_buf,
        att_buf,
        local_sem,
        send_sem,
        recv_sem,
        slice_send,
        slice_recv,
        line_send,
        line_recv,
        att_send,
        att_recv,
    ) = refs[2 * weight_count + 8 :]
    here = device_here(geo)
    x, y, core, w = here
    s = lax.axis_index("seq")
    part, g = s // geo.groups, s % geo.groups
    rows, width, wt = geo.rows, geo.width, geo.wt
    lanes = pl.ds(pl.multiple_of(g * LANES, LANES), LANES)

    own_tok = pltpu.make_async_copy(tokens_ref, tok_buf.at[s], local_sem.at[0])
    own_tok.start()
    shard = wqkv_ref.shape[0]
    own_slices = []
    for j in range(3):
        src = wqkv_ref.at[:, pl.ds(pl.multiple_of(j * width + g * LANES, LANES), LANES)]
        dst = slice_ref.at[pl.ds(pl.multiple_of(w * shard, shard), shard), pl.ds(j * LANES, LANES)]
        own_slices.append(pltpu.make_async_copy(src, dst, local_sem.at[1 + j]))
        own_slices[-1].start()
    own_weights = []
    for m in range(weight_count):
        height = weights_in[m].shape[0]
        dst = weights_out[m].at[pl.ds(pl.multiple_of(w * height, height), height)]
        own_weights.append(pltpu.make_async_copy(weights_in[m], dst, local_sem.at[4 + m]))

    greet(geo)

    def token_region(ux, uy, whose, half):
        block = tok_buf.at[(uy * geo.nx + ux) * 2 + whose]
        if half is None:
            return block
        return block.at[pl.ds(half * (rows // 2), rows // 2)]

    tok = Spread(geo, here, token_region, send_sem, recv_sem, 0)
    tok.go(0, own=tokens_ref)
    tok.go(1, own=tokens_ref)
    tok.go(4, own=tokens_ref)

    def slice_copy(j, d):
        src = wqkv_ref.at[:, pl.ds(pl.multiple_of(j * width + g * LANES, LANES), LANES)]
        dst = slice_ref.at[pl.ds(pl.multiple_of(w * shard, shard), shard), pl.ds(j * LANES, LANES)]
        return pltpu.make_async_remote_copy(
            src_ref=src,
            dst_ref=dst,
            send_sem=slice_send.at[j, d],
            recv_sem=slice_recv.at[j, d],
            device_id=(s, (w + d) % wt),
            device_id_type=MESH,
        )

    def slice_arrival(j, d):
        origin = (w + wt - d) % wt
        dst = slice_ref.at[pl.ds(pl.multiple_of(origin * shard, shard), shard), pl.ds(j * LANES, LANES)]
        return pltpu.make_async_remote_copy(
            src_ref=dst,
            dst_ref=dst,
            send_sem=slice_send.at[j, d],
            recv_sem=slice_recv.at[j, d],
            device_id=(s, origin),
            device_id_type=MESH,
        )

    for d in range(1, wt):
        for j in range(3):
            slice_copy(j, d).start()
    for copy in own_weights:
        copy.start()

    starts, ends = doc_bounds(len_ref)
    seg_buf[...] = segment_from(lax.broadcasted_iota(jnp.int32, seg_buf.shape, 1), starts)

    seq = geo.seq
    mine = s

    def unit_rows(m, p, unit, half=None):
        height = weights_in[m].shape[0]
        piece = height // seq
        if half is None:
            return weights_out[m].at[pl.ds(pl.multiple_of(p * height + unit * piece, piece), piece)]
        piece = piece // 2
        return weights_out[m].at[
            pl.ds(pl.multiple_of(p * height + unit * 2 * piece + half * piece, piece), piece)
        ]

    def line_copy(m, p, up, own):
        height = weights_in[m].shape[0]
        piece = height // seq
        dst = unit_rows(m, p, mine)
        src = weights_in[m].at[pl.ds(pl.multiple_of(mine * piece, piece), piece)] if own else dst
        target = w + 1 if up else w - 1
        return pltpu.make_async_remote_copy(
            src_ref=src,
            dst_ref=dst,
            send_sem=line_send.at[0 if up else 1, m * wt + p],
            recv_sem=line_recv.at[m * wt + p],
            device_id=(s, target),
            device_id_type=MESH,
        )

    def nth_plane(j):
        below, above = w, wt - 1 - w
        both = jnp.minimum(below, above)
        in_turn = j < 2 * both
        dist = jnp.where(in_turn, j // 2 + 1, j - both + 1)
        from_below = jnp.where(in_turn, j % 2 == 0, below > above)
        return jnp.where(from_below, w - dist, w + dist)

    def weight_spread(m, p):
        def region(ux, uy, whose, half):
            return unit_rows(m, p, (uy * geo.nx + ux) * 2 + whose, half)

        return Spread(geo, here, region, send_sem, recv_sem, 1 + m * wt + p)

    units = [(m, j) for m in range(weight_count) for j in range(wt - 1)]

    def start_lines():
        for m in range(weight_count):
            @pl.when(w < wt - 1)
            def _():
                line_copy(m, w, True, True).start()

            @pl.when(w > 0)
            def _():
                line_copy(m, w, False, True).start()

    def tick(i):
        if 0 <= i < len(units):
            m, j = units[i]
            p = nth_plane(j)
            line_copy(m, p, True, False).wait_recv()

            @pl.when((p < w) & (w < wt - 1))
            def _():
                line_copy(m, p, True, False).start()

            @pl.when((p > w) & (w > 0))
            def _():
                line_copy(m, p, False, False).start()

            spread = weight_spread(m, p)
            spread.go(0)
            spread.go(1)
            spread.go(4)
        if 0 <= i - 1 < len(units):
            m, j = units[i - 1]
            spread = weight_spread(m, nth_plane(j))
            spread.wait(0)
            spread.go(2)
            spread.go(5)
            spread.wait(1)
            spread.go(3)
            spread.go(6)
        if 0 <= i - 2 < len(units):
            m, j = units[i - 2]
            spread = weight_spread(m, nth_plane(j))
            spread.wait(2)
            spread.go(7)
            spread.wait(3)
            spread.go(8)

    tick_count = len(units) + 2 if units else 0

    nx, ny = geo.nx, geo.ny
    row_n, col_n, diag_n = 2 * (nx - 1), 2 * (ny - 1), 2 * (nx - 1) * (ny - 1)

    def block_owner(i):
        r = i - 2
        c = r - row_n
        d = c - col_n
        dx_row, k_row = r % max(nx - 1, 1) + 1, r // max(nx - 1, 1)
        dy_col, k_col = c % max(ny - 1, 1) + 1, c // max(ny - 1, 1)
        half = max(diag_n // 2, 1)
        k_diag, in_diag = d // half, d % half
        dx_diag, dy_diag = in_diag % max(nx - 1, 1) + 1, in_diag // max(nx - 1, 1) + 1
        dx = jnp.where(i < 2, 0, jnp.where(i < 2 + row_n, dx_row, jnp.where(i < 2 + row_n + col_n, 0, dx_diag)))
        dy = jnp.where(i < 2 + row_n, 0, jnp.where(i < 2 + row_n + col_n, dy_col, dy_diag))
        kk = jnp.where(i < 2, i, jnp.where(i < 2 + row_n, k_row, jnp.where(i < 2 + row_n + col_n, k_col, k_diag)))
        return (((y + dy) % ny) * nx + (x + dx) % nx) * 2 + (core + kk) % 2

    def project(i, carry):
        @pl.when(i == 0)
        def _():
            own_tok.wait()
            for copy in own_slices:
                copy.wait()
            for d in range(1, wt):
                for j in range(3):
                    slice_arrival(j, d).wait_recv()
            start_lines()

        @pl.when(i == 1)
        def _():
            tok.wait(4)

        @pl.when(i == 2)
        def _():
            tok.wait(0)
            tok.go(2)
            tok.go(5)
            tok.wait(1)
            tok.go(3)
            tok.go(6)

        @pl.when(i == 2 + row_n // 2)
        def _():
            tok.wait(5)

        @pl.when(i == 2 + row_n + col_n // 2)
        def _():
            tok.wait(6)

        @pl.when(i == 2 + row_n + col_n)
        def _():
            tok.wait(2)
            tok.go(7)
            tok.wait(3)
            tok.go(8)

        @pl.when(i == 2 + row_n + col_n + diag_n // 2)
        def _():
            tok.wait(7)
            tok.wait(8)

        t = block_owner(i)
        block = tok_buf[t]
        at = pl.ds(pl.multiple_of(t * rows, rows), rows)
        pos = t * rows + lax.broadcasted_iota(jnp.int32, (rows, LANES), 0)
        chosen = select_from(pos, starts, ends, id_ref, rank)
        main = dot_nn(block, slice_ref[...])
        small = dot_nt(block, down_ref[...])
        for j in range(3):
            cut = slice(j * LANES, (j + 1) * LANES)
            low = (small[:, cut] * chosen).astype(BF16)
            small_ref[at, cut] = low
            value = main[:, cut] + dot_nn(low, up_ref[cut, lanes])
            if j == 0:
                value = value + bias_ref[0:1, lanes]

                @pl.when(t // geo.groups == part)
                def _():
                    inner = pl.ds(pl.multiple_of((t % geo.groups) * rows, rows), rows)
                    q_ref[inner, :] = value.astype(BF16)
            elif j == 1:
                k_ref[at, :] = value.astype(BF16)
            else:
                v_ref[at, :] = (value + bias_ref[1:2, lanes]).astype(BF16)
        return carry

    lax.fori_loop(0, geo.seq, project, 0)

    scale = HEAD_DIM ** (-0.5)
    chunk = min(2048, geo.keys)
    chunks = geo.keys // chunk
    first_head = lax.broadcasted_iota(jnp.int32, (rows, LANES), 1) < HEAD_DIM

    def att_copy(b):
        return pltpu.make_async_remote_copy(
            src_ref=att_buf.at[b],
            dst_ref=att_ref.at[:, lanes],
            send_sem=att_send.at[b],
            recv_sem=att_recv.at[g],
            device_id=(part * geo.groups + b, w),
            device_id_type=MESH,
        )

    def attend(i, carry):
        for n in range(min(tick_count, geo.groups)):
            @pl.when(i == n)
            def _():
                tick(n)

        b = (g + 1 + i) % geo.groups
        inner = pl.ds(pl.multiple_of(b * rows, rows), rows)
        query = q_ref[inner, :] * jnp.asarray(scale, BF16)
        q_pos = (part * geo.groups + b) * rows + lax.broadcasted_iota(jnp.int32, (rows, 1), 0)
        q_seg = segment_from(q_pos, starts)
        results = []
        for h in range(PAIR):
            mask = first_head if h == 0 else jnp.logical_not(first_head)
            q_head = jnp.where(mask, query, jnp.zeros_like(query))

            def one(c, state):
                top, total, acc = state
                keys_at = pl.ds(pl.multiple_of(c * chunk, chunk), chunk)
                score = dot_nt(q_head, k_ref[keys_at, :])
                score = jnp.where(q_seg == seg_buf[:, keys_at], score, -1e30)
                peak = jnp.max(score, axis=1, keepdims=True)
                if top is not None:
                    peak = jnp.maximum(top, peak)
                weight = jnp.exp(score - peak)
                add = jnp.sum(weight, axis=1, keepdims=True)
                out = dot_nn(weight.astype(BF16), v_ref[keys_at, :])
                if top is not None:
                    fade = jnp.exp(top - peak)
                    add = add + total * fade
                    out = out + acc * fade
                return peak, add, out

            state = one(0, (None, None, None))
            if chunks > 1:
                state = lax.fori_loop(1, chunks, one, state)
            top, total, acc = state
            results.append((acc / total, top + jnp.log(total)))
        out = jnp.where(first_head, results[0][0], results[1][0])
        o_ref[inner, :] = out
        lse_ref[inner, :] = jnp.where(first_head, results[0][1], results[1][1])
        att_buf[b] = out.astype(BF16)

        @pl.when(b != g)
        def _():
            att_copy(b).start()

        return carry

    lax.fori_loop(0, geo.groups, attend, 0)
    own_att = pltpu.make_async_copy(att_buf.at[g], att_ref.at[:, lanes], local_sem.at[0])
    own_att.start()

    for n in range(geo.groups, tick_count):
        tick(n)

    for d in range(1, geo.groups):
        other = (g + d) % geo.groups
        cut = pl.ds(pl.multiple_of(other * LANES, LANES), LANES)
        pltpu.make_async_remote_copy(
            src_ref=att_ref.at[:, cut],
            dst_ref=att_ref.at[:, cut],
            send_sem=att_send.at[other],
            recv_sem=att_recv.at[other],
            device_id=(part * geo.groups + other, w),
            device_id_type=MESH,
        ).wait_recv()
        att_copy(other).wait_send()
    own_att.wait()
    tok.wait_sends()
    for d in range(1, wt):
        for j in range(3):
            slice_copy(j, d).wait_send()
    for m in range(weight_count):
        own_weights[m].wait()

        @pl.when(w < wt - 1)
        def _():
            line_copy(m, w, True, True).wait_send()

        @pl.when(w > 0)
        def _():
            line_copy(m, w, False, True).wait_send()

    for m, j in units:
        p = nth_plane(j)

        @pl.when((p < w) & (w < wt - 1))
        def _():
            line_copy(m, p, True, False).wait_send()

        @pl.when((p > w) & (w > 0))
        def _():
            line_copy(m, p, False, False).wait_send()

        spread = weight_spread(m, p)
        for kind in range(4, 9):
            spread.wait(kind)
        spread.wait_sends()


def forward_attention(geo, rank, lengths, ids, tokens, w_qkv, down, up, bias, weights):
    rows, width = geo.rows, geo.width
    count = len(weights)
    any_spec = pl.BlockSpec(memory_space=pl.ANY)
    vmem = pl.BlockSpec(memory_space=pltpu.VMEM)
    smem = pl.BlockSpec(memory_space=pltpu.SMEM)
    shapes = [
        jax.ShapeDtypeStruct((rows, width), BF16),
        jax.ShapeDtypeStruct((geo.queries, LANES), BF16),
        jax.ShapeDtypeStruct((geo.keys, LANES), BF16),
        jax.ShapeDtypeStruct((geo.keys, LANES), BF16),
        jax.ShapeDtypeStruct((geo.queries, LANES), F32),
        jax.ShapeDtypeStruct((geo.queries, LANES), F32),
        jax.ShapeDtypeStruct((width, 3 * LANES), BF16),
        jax.ShapeDtypeStruct((geo.keys, 3 * LANES), BF16),
    ] + [jax.ShapeDtypeStruct((v.shape[0] * geo.wt, v.shape[1]), BF16) for v in weights]
    units = 1 + count * geo.wt
    dma = pltpu.SemaphoreType.DMA
    results = pl.pallas_call(
        functools.partial(forward_kernel, geo, count, rank),
        out_shape=shapes,
        in_specs=[smem, smem, any_spec, any_spec, vmem, vmem, vmem] + [any_spec] * count,
        out_specs=[any_spec] + [vmem] * 7 + [any_spec] * count,
        scratch_shapes=[
            pltpu.VMEM((geo.seq, rows, width), BF16),
            pltpu.VMEM((1, geo.keys), jnp.int32),
            pltpu.VMEM((geo.groups, rows, LANES), BF16),
            dma((4 + count,)),
            dma((Spread.KINDS, units)),
            dma((Spread.KINDS, units)),
            dma((3, geo.wt)),
            dma((3, geo.wt)),
            dma((2, max(count, 1) * geo.wt)),
            dma((max(count, 1) * geo.wt,)),
            dma((geo.groups,)),
            dma((geo.groups,)),
        ],
        compiler_params=pltpu.CompilerParams(
            collective_id=0, has_side_effects=True, vmem_limit_bytes=VMEM_LIMIT
        ),
        name="gather_attend",
    )(lengths, ids, tokens, w_qkv, down, up, bias, *weights)
    return results[:8], results[8:]


def backward_kernel(geo, len_ref, part_ref, q_ref, k_ref, v_ref, o_ref, lse_ref, g_ref, dq_ref, dk_ref, dv_ref, dk_acc, dv_acc):
    rows = geo.rows
    part = part_ref[0, 0]
    scale = HEAD_DIM ** (-0.5)
    starts, ends = doc_bounds(len_ref)
    first_head = lax.broadcasted_iota(jnp.int32, (rows, LANES), 1) < HEAD_DIM
    dk_acc[...] = jnp.zeros_like(dk_acc)
    dv_acc[...] = jnp.zeros_like(dv_acc)

    def seg_of(position):
        seg = jnp.int32(0)
        for start in starts[1:]:
            seg = seg + (position >= start).astype(jnp.int32)
        return seg

    def pick(values, index):
        found = values[0]
        for i in range(1, len(values)):
            found = jnp.where(index == i, values[i], found)
        return found

    def query_block(b, carry):
        at = pl.ds(pl.multiple_of(b * rows, rows), rows)
        origin = (part * geo.groups + b) * rows
        query = q_ref[at, :] * jnp.asarray(scale, BF16)
        cot = g_ref[at, :]
        lse = lse_ref[at, :]
        both = cot.astype(F32) * o_ref[at, :]
        q_pos = origin + lax.broadcasted_iota(jnp.int32, (rows, 1), 0)
        q_seg = segment_from(q_pos, starts)
        heads = []
        for h in range(PAIR):
            mask = first_head if h == 0 else jnp.logical_not(first_head)
            zero = jnp.zeros_like(query)
            heads.append(
                (
                    jnp.where(mask, query, zero),
                    jnp.where(mask, cot, zero),
                    lse[:, h * HEAD_DIM : h * HEAD_DIM + 1],
                    jnp.sum(jnp.where(mask, both, 0.0), axis=1, keepdims=True),
                )
            )
        low = pick(starts, seg_of(origin)) // rows
        high = (pick(ends, seg_of(origin + rows - 1)) + rows - 1) // rows

        def key_block(c, accs):
            keys_at = pl.ds(pl.multiple_of(c * rows, rows), rows)
            key, value = k_ref[keys_at, :], v_ref[keys_at, :]
            k_pos = c * rows + lax.broadcasted_iota(jnp.int32, (1, rows), 1)
            same = q_seg == segment_from(k_pos, starts)
            new = []
            dk_parts, dv_parts = [], []
            for h in range(PAIR):
                q_head, g_head, lse_head, dot_head = heads[h]
                score = jnp.where(same, dot_nt(q_head, key), -1e30)
                prob = jnp.exp(score - lse_head)
                d_prob = dot_nt(g_head, value)
                raw = (prob * (d_prob - dot_head) * scale).astype(BF16)
                new.append(accs[h] + dot_nn(raw, key))
                dk_parts.append(dot_tn(raw, q_head))
                dv_parts.append(dot_tn(prob.astype(BF16), g_head))
            dk_acc[keys_at, :] += dk_parts[0] + dk_parts[1]
            dv_acc[keys_at, :] += dv_parts[0] + dv_parts[1]
            return tuple(new)

        zero = jnp.zeros((rows, LANES), F32)
        accs = lax.fori_loop(low, high, key_block, (zero, zero))
        dq_ref[at, :] = jnp.where(first_head, accs[0], accs[1]).astype(BF16)
        return carry

    lax.fori_loop(0, geo.groups, query_block, 0)
    dk_ref[...] = (dk_acc[...] * HEAD_DIM**0.5).astype(BF16)
    dv_ref[...] = dv_acc[...].astype(BF16)


def backward_attention(geo, lengths, part, q, k, v, o, lse, d_heads):
    smem = pl.BlockSpec(memory_space=pltpu.SMEM)
    vmem = pl.BlockSpec(memory_space=pltpu.VMEM)
    return pl.pallas_call(
        functools.partial(backward_kernel, geo),
        out_shape=[
            jax.ShapeDtypeStruct((geo.queries, LANES), BF16),
            jax.ShapeDtypeStruct((geo.keys, LANES), BF16),
            jax.ShapeDtypeStruct((geo.keys, LANES), BF16),
        ],
        in_specs=[smem, smem] + [vmem] * 6,
        out_specs=[vmem] * 3,
        scratch_shapes=[pltpu.VMEM((geo.keys, LANES), F32)] * 2,
        compiler_params=pltpu.CompilerParams(vmem_limit_bytes=VMEM_LIMIT),
        name="attend_back",
    )(lengths, part, q, k, v, o, lse, d_heads)


def layer_norm(value, gain, shift):
    mean = jnp.mean(value, axis=-1, keepdims=True)
    centred = value - mean
    spread = jnp.mean(centred * centred, axis=-1, keepdims=True)
    return centred * lax.rsqrt(spread + 1e-05) * gain + shift


def gelu_exact(value):
    return jax.nn.gelu(value, approximate=False)


def times_transposed(grad, weight):
    return lax.dot_general(
        grad, weight, (((1,), (1,)), ((), ())), preferred_element_type=jnp.float32
    )


def left_inner(left, right):
    return lax.dot_general(
        left, right, (((0,), (0,)), ((), ())), preferred_element_type=jnp.float32
    )


def stack_down(down):
    return jnp.transpose(down, (1, 0, 2)).reshape(down.shape[1], down.shape[0] * down.shape[2])


def stack_up(up):
    return up.reshape(up.shape[0] * up.shape[1], up.shape[2])


def unstack_down(stacked, adapter_count, rank_size):
    return jnp.transpose(stacked.reshape(stacked.shape[0], adapter_count, rank_size), (1, 0, 2))


def unstack_up(stacked, adapter_count, rank_size):
    return stacked.reshape(adapter_count, rank_size, stacked.shape[1])


def segment_of(positions, starts):
    return jnp.sum((positions[:, None] >= starts[None, :]).astype(jnp.int32), axis=1) - 1


def shards(
    tokens,
    cotangent,
    w_qkv,
    qv_bias,
    w_out,
    out_bias,
    norm1_gain,
    norm1_bias,
    w_fc1,
    fc1_bias,
    w_fc2,
    fc2_bias,
    norm2_gain,
    norm2_bias,
    doc_lengths,
    adapter_ids,
    attn_down,
    attn_up,
    fc1_down,
    fc1_up,
    fc2_down,
    fc2_up,
):
    tok_rows, model_width = tokens.shape
    adapter_count = attn_down.shape[1]
    rank_size = attn_down.shape[3]
    lane_count = adapter_count * rank_size
    seq_count = lax.axis_size("seq")
    geo = Geometry(tok_rows, model_width)
    seq_index = lax.axis_index("seq")
    part_index = seq_index // geo.groups
    head_index = seq_index % geo.groups
    lengths = doc_lengths[0]
    starts = jnp.cumsum(lengths) - lengths
    local_pos = seq_index * tok_rows + jnp.arange(tok_rows, dtype=jnp.int32)
    local_seg = segment_of(local_pos, starts)
    doc_range = jnp.arange(lengths.shape[0], dtype=jnp.int32)
    chosen = jnp.sum(
        jnp.where(local_seg[:, None] == doc_range[None, :], adapter_ids[0][None, :], 0), axis=1
    )
    lane_owner = jnp.arange(lane_count, dtype=jnp.int32) // rank_size
    select = (chosen[:, None] == lane_owner[None, :]).astype(jnp.float32)
    out_down = stack_down(attn_down[3])
    out_up = stack_up(attn_up[3])
    fc1_down_all = stack_down(fc1_down)
    fc1_up_all = stack_up(fc1_up)
    fc2_down_all = stack_down(fc2_down)
    fc2_up_all = stack_up(fc2_up)
    down_rows = jnp.transpose(attn_down, (0, 1, 3, 2)).reshape(4 * lane_count, model_width)
    up_rows = attn_up.reshape(4 * lane_count, model_width)
    weights = (w_out, w_fc1, w_fc2)
    inside = [v.shape[0] % (32 * seq_count) == 0 for v in weights]
    (attended_tok, q_heads, k_heads, v_heads, o_heads, lse_heads, w_slice, small_all), gathered = forward_attention(
        geo,
        rank_size,
        doc_lengths,
        adapter_ids,
        tokens,
        w_qkv,
        down_rows[: 3 * lane_count],
        up_rows[: 3 * lane_count],
        qv_bias,
        [v for v, here in zip(weights, inside) if here],
    )
    gathered = list(gathered)
    full_out, full_fc1, full_fc2 = [
        gathered.pop(0) if here else lax.all_gather(v, "wt", axis=0, tiled=True)
        for v, here in zip(weights, inside)
    ]
    out_main = jnp.dot(attended_tok, full_out, preferred_element_type=jnp.float32)
    small_out = (
        jnp.dot(attended_tok, out_down, preferred_element_type=jnp.float32) * select
    ).astype(jnp.bfloat16)
    z_value = out_main + out_bias + jnp.dot(small_out, out_up, preferred_element_type=jnp.float32)
    first_sum = tokens.astype(jnp.float32) + z_value
    first_norm, norm1_back = jax.vjp(
        lambda value: layer_norm(value, norm1_gain, norm1_bias), first_sum
    )
    first_low = first_norm.astype(jnp.bfloat16)
    fc1_main = jnp.dot(first_low, full_fc1, preferred_element_type=jnp.float32)
    small_fc1 = (
        jnp.dot(first_low, fc1_down_all, preferred_element_type=jnp.float32) * select
    ).astype(jnp.bfloat16)
    pre_act = (
        fc1_main + fc1_bias + jnp.dot(small_fc1, fc1_up_all, preferred_element_type=jnp.float32)
    )
    act_value, gelu_back = jax.vjp(gelu_exact, pre_act)
    act_low = act_value.astype(jnp.bfloat16)
    fc2_main = jnp.dot(act_low, full_fc2, preferred_element_type=jnp.float32)
    small_fc2 = (
        jnp.dot(act_low, fc2_down_all, preferred_element_type=jnp.float32) * select
    ).astype(jnp.bfloat16)
    y_value = (
        fc2_main + fc2_bias + jnp.dot(small_fc2, fc2_up_all, preferred_element_type=jnp.float32)
    )
    output, norm2_back = jax.vjp(
        lambda value: layer_norm(value, norm2_gain, norm2_bias), first_norm + y_value
    )
    d_second = norm2_back(cotangent.astype(jnp.float32))[0]
    d_y = d_second.astype(jnp.bfloat16)
    d_act = times_transposed(d_y, full_fc2)
    low_fc2 = (times_transposed(d_y, fc2_up_all) * select).astype(jnp.bfloat16)
    d_act = d_act + times_transposed(low_fc2, fc2_down_all)
    grad_fc2_up = left_inner(small_fc2, d_y)
    grad_fc2_down = left_inner(act_low, low_fc2)
    d_pre = gelu_back(d_act)[0].astype(jnp.bfloat16)
    d_first_low = times_transposed(d_pre, full_fc1)
    low_fc1 = (times_transposed(d_pre, fc1_up_all) * select).astype(jnp.bfloat16)
    d_first_low = d_first_low + times_transposed(low_fc1, fc1_down_all)
    grad_fc1_up = left_inner(small_fc1, d_pre)
    grad_fc1_down = left_inner(first_low, low_fc1)
    d_first = norm1_back(d_second + d_first_low)[0]
    d_z = d_first.astype(jnp.bfloat16)
    d_attended = times_transposed(d_z, full_out)
    low_out = (times_transposed(d_z, out_up) * select).astype(jnp.bfloat16)
    d_attended = (d_attended + times_transposed(low_out, out_down)).astype(jnp.bfloat16)
    grad_out_up = left_inner(small_out, d_z)
    grad_out_down = left_inner(attended_tok, low_out)
    blocks = [
        [p * geo.groups + i for i in range(geo.groups)] for p in range(geo.parts)
    ]
    d_heads = lax.all_to_all(
        d_attended.reshape(tok_rows, geo.groups, LANES),
        "seq",
        split_axis=1,
        concat_axis=0,
        axis_index_groups=blocks,
        tiled=True,
    ).reshape(geo.queries, LANES)
    d_q, d_k, d_v = backward_attention(
        geo, doc_lengths, part_index.reshape(1, 1), q_heads, k_heads, v_heads, o_heads, lse_heads, d_heads
    )
    if geo.parts > 1:
        d_q = lax.dynamic_update_slice_in_dim(
            jnp.zeros((geo.keys, LANES), BF16), d_q, part_index * geo.queries, 0
        )
    d_three = jnp.concatenate([d_q, d_k, d_v], axis=1)
    partial = times_transposed(d_three, w_slice).astype(BF16).reshape(seq_count, tok_rows, model_width)
    d_tokens = jnp.sum(
        lax.all_to_all(partial, "seq", split_axis=0, concat_axis=0, tiled=True).astype(F32), axis=0
    )
    up_slice = lax.dynamic_slice_in_dim(up_rows[: 3 * lane_count], head_index * LANES, LANES, 1)
    low_part = jnp.concatenate(
        [
            times_transposed(
                d_three[:, i * LANES : (i + 1) * LANES], up_slice[i * lane_count : (i + 1) * lane_count]
            )
            for i in range(3)
        ],
        axis=1,
    )
    low_sum = lax.psum_scatter(low_part, "seq", scatter_dimension=0, tiled=True)
    low_qkv = (low_sum * jnp.tile(select, (1, 3))).astype(BF16)
    input_grad = d_first + d_tokens + jnp.dot(
        low_qkv, down_rows[: 3 * lane_count], preferred_element_type=F32
    )
    grad_qkv_down = left_inner(low_qkv, tokens)
    grad_qkv_up = []
    for i in range(3):
        cut = slice(i * LANES, (i + 1) * LANES)
        own = left_inner(small_all[:, cut], d_three[:, cut])
        grad_qkv_up.append(
            lax.dynamic_update_slice_in_dim(
                jnp.zeros((lane_count, model_width), F32), own, head_index * LANES, 1
            )
        )
    grad_attn_down = jnp.stack(
        [
            jnp.transpose(
                grad_qkv_down[i * lane_count : (i + 1) * lane_count].reshape(
                    adapter_count, rank_size, model_width
                ),
                (0, 2, 1),
            )
            for i in range(3)
        ]
        + [unstack_down(grad_out_down, adapter_count, rank_size)]
    )
    grad_attn_up = jnp.stack(
        [
            unstack_up(piece_grad, adapter_count, rank_size)
            for piece_grad in grad_qkv_up + [grad_out_up]
        ]
    )
    summed = lax.psum(
        (
            grad_attn_down,
            grad_attn_up,
            unstack_down(grad_fc1_down, adapter_count, rank_size),
            unstack_up(grad_fc1_up, adapter_count, rank_size),
            unstack_down(grad_fc2_down, adapter_count, rank_size),
            unstack_up(grad_fc2_up, adapter_count, rank_size),
        ),
        ("seq", "wt"),
    )
    return (output, input_grad, summed[0], summed[1], summed[2], summed[3], summed[4], summed[5])


def solution(mesh):
    placed = (
        P(("wt", "seq"), None),
        P(("wt", "seq"), None),
        P("wt", None),
        P(),
        P("wt", None),
        P(),
        P(),
        P(),
        P("wt", None),
        P(),
        P("wt", None),
        P(),
        P(),
        P(),
        P("wt", None),
        P("wt", None),
        P(),
        P(),
        P(),
        P(),
        P(),
        P(),
    )
    return jax.shard_map(
        shards,
        mesh=mesh,
        in_specs=placed,
        out_specs=(P(("wt", "seq"), None), P(("wt", "seq"), None), P(), P(), P(), P(), P(), P()),
        check_vma=False,
    )
```

time: 994 us -> 551 us (0.55)
  waiting for transfers between devices: 541 us -> 181 us
  matrix products: 283 us -> 59.7 us
  Pallas kernels: 0 us -> 188 us
  blocking collectives: 0 us -> 70.8 us
  other arithmetic: 53.4 us -> 10.3 us
  local copies, waits for them, and re-layouts: 60.4 us -> 20.5 us
  starting transfers between devices: 29.8 us -> 4.49 us
    all_gather x4 -> x0, waiting for transfers between devices: 308 us -> none  [the longest x1 130 us: shards(): lax.all_gather(w_fc2, 'wt', axis=0, tiled=True)]
    dot_general x33 -> x1, matrix products: 211 us -> 1.43 us  [shards(): jnp.dot(low_qkv, down_rows[:3 * lane_count], preferred_element_type=F32)]
    pallas_call x0 -> x2, Pallas kernels: none -> 188 us  [the longest x1 156 us: forward_attention(): pl.pallas_call(functools.partial(forward_kernel, geo, count, rank), out_s...]
    all_to_all x0 -> x1, blocking collectives: none -> 70.8 us  [shards(): lax.all_to_all(partial, 'seq', split_axis=0, concat_axis=0, tiled=True)]
    all_to_all x8 -> x1, waiting for transfers between devices: 49.2 us -> 9.68 us  [shards(): lax.all_to_all(d_attended.reshape(tok_rows, geo.groups, LANES), 'seq', sp...]
    psum x1, waiting for transfers between devices: 181 us -> 143 us  [shards(): lax.psum((grad_attn_down, grad_attn_up, unstack_down(grad_fc1_down, adapt...]
    reduce_scatter x0 -> x1, waiting for transfers between devices: none -> 29 us  [shards(): low_sum = lax.psum_scatter(low_part, 'seq', scatter_dimension=0, tiled=True)]
    all_to_all x8 -> x1, starting transfers between devices: 29.6 us -> 4.15 us  [shards(): lax.all_to_all(d_attended.reshape(tok_rows, geo.groups, LANES), 'seq', sp...]
  transfers between devices with their start and end apart: 13 -> 3, of which waited for: 12 -> 3; matrix products, arithmetic and copies ran while one was open for 13% -> 4% of each run, Pallas kernels for 0% -> 0%
where the time goes in v1:
time: 551 us; the launch traced here: 550 us
  Pallas kernels  188 us (34%)
  waiting for transfers between devices  181 us (33%)
  blocking collectives  70.8 us (13%)
  matrix products  59.7 us (11%)
  local copies, waits for them, and re-layouts  20.5 us (4%)
  between operations  14.9 us (3%)
  other arithmetic  10.3 us (2%)
    pallas_call x1, Pallas kernels, forward_attention(): pl.pallas_call(functools.partial(forward_kernel, geo, count, rank), out_s...  156 us
    psum x1, waiting for transfers between devices, shards(): lax.psum((grad_attn_down, grad_attn_up, unstack_down(grad_fc1_down, adapt...  143 us
    all_to_all x1, blocking collectives, shards(): lax.all_to_all(partial, 'seq', split_axis=0, concat_axis=0, tiled=True)  70.8 us
    pallas_call x1, Pallas kernels, backward_attention(): pl.pallas_call(functools.partial(backward_kernel, geo), out_shape=[jax.Sh...  31.9 us
    reduce_scatter x1, waiting for transfers between devices, shards(): low_sum = lax.psum_scatter(low_part, 'seq', scatter_dimension=0, tiled=True)  29 us
    dot_general x13, matrix products, times_transposed(): lax.dot_general(grad, weight, (((1,), (1,)), ((), ())), preferred_element...  23.1 us
    dot_general x10, matrix products, left_inner(): lax.dot_general(left, right, (((0,), (0,)), ((), ())), preferred_element_...  12.9 us
    unnamed x110, local copies, waits for them, and re-layouts  12.2 us
  transfers between devices with their start and end apart: 3, of which 3 were waited for; matrix products, arithmetic and copies ran while one was open for 4% of the time, Pallas kernels for 0%

profile of v1, /device:TPU:0, one launch (start us, length us, event | category | flops | bytes accessed | tf_op | source)
XLA Modules:
  0.0 550.2 jit_solution(17320875441499799341)
XLA Ops:
  7.2 2.2 slice.49
  11.4 2.1 slice.62
  13.9 156.2 %gather_attend.1 = (bf16[256,1024]{1,0:T(8,128)(2,1)}, bf16[2048,128]{1,0:T(8,128)(2,1)}, bf16[2048,128]{1,0:T(8,128)(2,1)}, bf16[2048,128]{1,0:T(8,128)(2,1)}, ...) custom-call(s32[1,4]{1,0:T(1,128)} %len_ref.3, ...), custom_call_target="tpu_custom_call" | custom-call | tf_op jit(solution)/shard_map/gather_attend/pallas_call | solution.py:592
  170.2 2.6 convolution_add_fusion.8
  172.9 2.1 fusion.19
  176.3 2.4 convolution_add_fusion.2
  178.8 10.9 %multiply_convert_fusion = (bf16[256,4096]{1,0:T(8,128)(2,1)S(1)}, f32[256,4096]{1,0:T(8,128)}, f32[256,4096]{1,0:T(8,128)}) fusion(f32[256,4096]{1,0:T(8,128)S(1)} %convolution_add_fusion.2, bf16[256,128]{1,0:T(8,128)(2,1)S(1)} %fusion.20, bf16[128,4096]{1,0:T(8,128)(2,1)S(1)} %bitcast.127), kind=kOutput, calls=%fused_computation.7 | convolution fusion | flops 337641472 | bytes 15794176 | tf_op jit(solution)/shard_map/dot_general | solution.py:840
  190.5 2.4 convolution_add_fusion.9
  193.8 1.4 fusion.39
  195.4 4.3 fusion.44
  200.1 6.0 %add_convert_fusion = bf16[256,4096]{1,0:T(8,128)(2,1)S(1)} fusion(f32[256,4096]{1,0:T(8,128)} %get-tuple-element.49, f32[256,4096]{1,0:T(8,128)} %fusion.44, bf16[256,128]{1,0:T(8,128)(2,1)S(1)} %fusion.21, bf16[4096,128]{0,1:T(8,128)(2,1)S(1)} %bitcast.154, f32[256,4096]{1,0:T(8,128)} %get-tuple-element.58), kind=kOutput, calls=%fused_computation.6 | convolution fusion | flops 284164096 | bytes 15794176 | tf_op jit(solution)/shard_map/dot_general | solution.py:724
  206.1 2.4 fusion.45
  213.6 4.2 all-to-all-start
  217.8 9.7 %all-to-all-done = bf16[256,8,128]{2,0,1:T(8,128)(2,1)} async-done(((bf16[256,8,128]{2,0,1:T(8,128)(2,1)}), bf16[256,8,128]{2,0,1:T(8,128)(2,1)}, u32[]{:S(2)}, u32[]{:S(2)}) %all-to-all-start) | async-done | bytes 524320 | tf_op jit(solution)/shard_map/all_to_all | solution.py:877
  227.5 31.9 %attend_back.1 = (bf16[2048,128]{1,0:T(8,128)(2,1)}, bf16[2048,128]{1,0:T(8,128)(2,1)}, bf16[2048,128]{1,0:T(8,128)(2,1)}) custom-call(s32[1,4]{1,0:T(1,128)} %len_ref.3, s32[1,1]{1,0:T(1,128)} %bitcast.17.part_ref, bf16[2048,128]{1,0:T(8,128)(2,1)} %get-tuple-element.26.q_ref, bf16[2048,128]{1,0:T(8,128)(2,1)} %get-tuple-element.27.k_ref, ...), custom_call_target="tpu_custom_call" | custom-call | tf_op jit(solution)/shard_map/attend_back/pallas_call | solution.py:697
  259.4 1.3 fusion.32
  260.7 1.3 fusion.28
  262.1 1.4 fusion.30
  263.5 2.0 pad_maximum_fusion
  266.7 2.3 fusion.48
  270.2 2.2 fusion.50
  272.4 2.2 fusion.53
  274.6 1.8 fusion.51
  276.4 1.8 fusion.52
  279.6 1.5 pad_maximum_fusion.2
  281.1 29.0 %reduce-scatter.2.cloned.1.call-done = f32[256,384]{0,1:T(8,128)} async-done(((f32[2048,384]{0,1:T(8,128)}), f32[256,384]{0,1:T(8,128)}) %reduce-scatter.2.cloned.1.call-update) | async-done | bytes 393232 | tf_op jit(solution)/shard_map/reduce_scatter | solution.py:907
  311.7 1.5 pad_maximum_fusion.1
  314.5 3.5 convolution_convert_fusion
  318.0 70.8 %all_to_all.20 = bf16[8,256,1024]{2,1,0:T(8,128)(2,1)S(1)} all-to-all(bf16[8,256,1024]{2,1,0:T(8,128)(2,1)S(1)} %bitcast.133), channel_id=1, replica_groups=mesh['seq'=8,'wt'=4] {'seq'}, dimensions={0} | all-to-all | bytes 8388608 | tf_op jit(solution)/shard_map/all_to_all | solution.py:895
  390.3 1.4 convolution_add_fusion.3
  391.8 142.7 %all-reduce.3.cloned.1.call-done = (f32[4,8,1024,16]{2,3,1,0:T(8,128)}, f32[4,8,16,1024]{3,2,1,0:T(8,128)}, f32[8,1024,16]{1,2,0:T(8,128)}, f32[8,16,4096]{2,1,0...) async-done(((f32[4,8,1024,16]{2,3,1,0:T(8,128)}, f32[4,8,16,1024]{3,2,1,0:T(8,128)}, f32[8,1024,16]{1,2,0:T(8,128)}, f32[8,16,4096]{2,1,0:T(8,128)}, ...) | async-done | bytes 9437200 | tf_op jit(solution)/shard_map/psum | solution.py:940
  534.5 3.3 copy.46
  (160 shorter events, 24.6 us)
Async XLA Ops:
  7.2 171.6 %copy-start = (bf16[8,16,4096]{2,1,0:T(8,128)(2,1)S(1)}, bf16[8,16,4096]{2,1,0:T(8,128)(2,1)}, u32[]{:S(2)}) copy-start(bf16[8,16,4096]{2,1,0:T(8,128)(2,1)} %param.41) | copy-start | bytes 3145732
  7.2 6.4 %copy-start.43 = (s32[1,4]{1,0:T(1,128)S(1)}, s32[1,4]{1,0:T(1,128)}, u32[]{:S(2)}) copy-start(s32[1,4]{1,0:T(1,128)} %len_ref.3) | copy-start | bytes 52
  7.2 6.6 %copy-start.44 = (s32[1,4]{1,0:T(1,128)S(1)}, s32[1,4]{1,0:T(1,128)}, u32[]{:S(2)}) copy-start(s32[1,4]{1,0:T(1,128)} %id_ref.1) | copy-start | bytes 52
  10.4 164.6 %copy-start.11 = (bf16[1,8,16,1024]{3,2,1,0:T(8,128)(2,1)}, bf16[1,8,16,1024]{3,2,1,0:T(8,128)(2,1)S(1)}, u32[]{:S(2)}) copy-start(bf16[1,8,16,1024]{3,2,1,0:T(8,128)(2,1)S(1)} %slice.52) | copy-start | bytes 786436
  13.9 156.3 %copy-start.48 = (f32[1024]{0:T(1024)S(1)}, f32[1024]{0:T(1024)}, u32[]{:S(2)}) copy-start(f32[1024]{0:T(1024)} %param.27) | copy-start | bytes 12292
  170.2 4.8 copy-start.8
  170.2 5.4 copy-start.39
  170.2 5.4 copy-start.40
  170.2 6.0 %copy-start.45 = (bf16[1024,4096]{1,0:T(8,128)(2,1)S(1)}, bf16[1024,4096]{1,0:T(8,128)(2,1)}, u32[]{:S(2)}) copy-start(bf16[1024,4096]{1,0:T(8,128)(2,1)} %get-tuple-element.24) | copy-start | bytes 25165828
  172.8 3.1 copy-start.21
  172.9 3.4 copy-start.47
  176.3 14.2 %slice-start = ((s8[8388608]{0:T(1024)(128)(4,1)}), s8[4194304]{0:T(1024)(128)(4,1)S(1)}, s32[]{:S(2)}) async-start(s8[8388608]{0:T(1024)(128)(4,1)} %bitcast.161), calls=%async_computation.5 | async-start | bytes 8388608
  178.7 11.0 %copy-start.19 = (bf16[8,4096,16]{1,2,0:T(8,128)(2,1)S(1)}, bf16[8,4096,16]{1,2,0:T(8,128)(2,1)}, u32[]{:S(2)}) copy-start(bf16[8,4096,16]{1,2,0:T(8,128)(2,1)} %param.42) | copy-start | bytes 3145732
  178.7 11.7 %slice-start.1 = ((s8[8388608]{0:T(1024)(128)(4,1)}), s8[4194304]{0:T(1024)(128)(4,1)S(1)}, s32[]{:S(2)}) async-start(s8[8388608]{0:T(1024)(128)(4,1)} %bitcast.161), calls=%async_computation.6 | async-start | bytes 8388608
  178.8 11.7 %copy-start.49 = (f32[1024]{0:T(1024)S(1)}, f32[1024]{0:T(1024)}, u32[]{:S(2)}) copy-start(f32[1024]{0:T(1024)} %param.33) | copy-start | bytes 12292
  195.4 4.3 copy-start.10
  200.1 6.0 %copy-start.37 = (bf16[256,128]{1,0:T(8,128)(2,1)}, bf16[256,128]{1,0:T(8,128)(2,1)S(1)}, u32[]{:S(2)}) copy-start(bf16[256,128]{1,0:T(8,128)(2,1)S(1)} %fusion.21) | copy-start | bytes 196612
  213.6 13.9 %all-to-all-start = ((bf16[256,8,128]{2,0,1:T(8,128)(2,1)}), bf16[256,8,128]{2,0,1:T(8,128)(2,1)}, u32[]{:S(2)}, u32[]{:S(2)}) async-start(bf16[256,8,128]{2,0,1:T(8,128)(2,1)} %bitcast.144), calls=%async_computation | async-start | bytes 1048576 | tf_op jit(solution)/shard_map/all_to_all | solution.py:877
  217.7 92.4 %reduce-scatter.2.cloned.1.call-start = ((), (), s32[]{:S(2)}) async-start(), calls=%async_computation.3 | async-start | bytes 3538944 | tf_op jit(solution)/shard_map/reduce_scatter | solution.py:907
  263.4 3.2 copy-start.25
  265.4 7.0 %copy-start.23 = (bf16[256,128]{1,0:T(8,128)(2,1)S(1)}, bf16[256,128]{1,0:T(8,128)(2,1)}, u32[]{:S(2)}) copy-start(bf16[256,128]{1,0:T(8,128)(2,1)} %copy-done.22) | copy-start | bytes 196612
  265.5 269.0 %all-reduce.3.cloned.1.call-start = ((), (), s32[]{:S(2)}) async-start(), calls=%async_computation.4 | async-start | bytes 18874368 | tf_op jit(solution)/shard_map/psum | solution.py:940
  266.6 7.9 %copy-start.4 = (bf16[256,4096]{1,0:T(8,128)(2,1)S(1)}, bf16[256,4096]{1,0:T(8,128)(2,1)}, u32[]{:S(2)}) copy-start(bf16[256,4096]{1,0:T(8,128)(2,1)} %copy-done.3) | copy-start | bytes 6291460
  266.6 7.9 %copy-start.36 = (bf16[256,128]{1,0:T(8,128)(2,1)S(1)}, bf16[256,128]{1,0:T(8,128)(2,1)}, u32[]{:S(2)}) copy-start(bf16[256,128]{1,0:T(8,128)(2,1)} %copy-done.35) | copy-start | bytes 196612
  266.6 9.7 %copy-start.38 = (bf16[256,128]{1,0:T(8,128)(2,1)S(1)}, bf16[256,128]{1,0:T(8,128)(2,1)}, u32[]{:S(2)}) copy-start(bf16[256,128]{1,0:T(8,128)(2,1)} %copy-done.37) | copy-start | bytes 196612
  278.3 31.7 %copy-start.30 = (f32[256,128]{0,1:T(8,128)S(1)}, f32[256,128]{0,1:T(8,128)}, u32[]{:S(2)}) copy-start(f32[256,128]{0,1:T(8,128)} %copy.33) | copy-start | bytes 393220
  278.7 32.4 %copy-start.9 = (bf16[256,1024]{1,0:T(8,128)(2,1)S(1)}, bf16[256,1024]{1,0:T(8,128)(2,1)}, u32[]{:S(2)}) copy-start(bf16[256,1024]{1,0:T(8,128)(2,1)} %tokens_ref.1) | copy-start | bytes 1572868
  279.6 32.1 %copy-start.18 = (f32[1024,128]{0,1:T(8,128)S(1)}, f32[1024,128]{0,1:T(8,128)}, u32[]{:S(2)}) copy-start(f32[1024,128]{0,1:T(8,128)} %fusion.48) | copy-start | bytes 1572868
  534.5 3.3 copy-start.16
  534.5 4.6 copy-start.29
  534.5 5.4 copy-start.15
  537.8 3.4 copy-start.14
  (23 other events, 45.1 us)
Sparse Core Ops, SparseCore 0:
  265.6 44.4 reduce-scatter.1
  318.2 216.2 all-reduce.2

commit v2 on v1

--- a/solution.py
+++ b/solution.py
@@ -77,9 +77,9 @@
 class Spread:
     KINDS = 9
 
-    def __init__(self, geo, here, region, send, recv, unit):
+    def __init__(self, geo, here, region, send, recv, unit, first=0):
         self.geo, self.here, self.region = geo, here, region
-        self.send, self.recv, self.unit = send, recv, unit
+        self.send, self.recv, self.unit, self.first = send, recv, unit, first
 
     def copy(self, kind, src, dst, x, y, core):
         return pltpu.make_async_remote_copy(
@@ -87,7 +87,7 @@
             dst_ref=dst,
             send_sem=self.send.at[kind, self.unit],
             recv_sem=self.recv.at[kind, self.unit],
-            device_id=(((y * self.geo.nx) + x) * 2 + core, self.here[3]),
+            device_id=(self.first + ((y * self.geo.nx) + x) * 2 + core, self.here[3]),
             device_id_type=MESH,
         )
 
@@ -707,6 +707,547 @@
         compiler_params=pltpu.CompilerParams(vmem_limit_bytes=VMEM_LIMIT),
         name="attend_back",
     )(lengths, part, q, k, v, o, lse, d_heads)
+
+
+class Block:
+    def __init__(self, geo):
+        chips = geo.groups // 2
+        self.nx = min(geo.nx, chips)
+        self.ny = chips // self.nx
+
+
+class PairSum:
+    def __init__(self, count, me, core, first, w, bufs, sems, make, stage=None):
+        self.count, self.me, self.core, self.first, self.w = count, me, core, first, w
+        self.near_out, self.near_in, self.far_in = bufs
+        self.near_send, self.near_recv, self.far_send, self.far_recv = sems
+        self.make = make
+        self.slots = self.near_out.shape[0]
+        self.stage = stage
+
+    def slot(self, chip):
+        return ((chip + self.count - self.me + self.count - 1) % self.count) % self.slots
+
+    def near(self, chip):
+        return pltpu.make_async_remote_copy(
+            src_ref=self.near_out.at[self.slot(chip)],
+            dst_ref=self.near_in.at[chip],
+            send_sem=self.near_send.at[chip],
+            recv_sem=self.near_recv.at[chip],
+            device_id=(self.first + self.me * 2 + 1 - self.core, self.w),
+            device_id_type=MESH,
+        )
+
+    def far(self, chip):
+        return pltpu.make_async_remote_copy(
+            src_ref=self.near_in.at[chip],
+            dst_ref=self.far_in.at[self.me],
+            send_sem=self.far_send.at[chip],
+            recv_sem=self.far_recv.at[self.me],
+            device_id=(self.first + chip * 2 + self.core, self.w),
+            device_id_type=MESH,
+        )
+
+    def far_arrival(self, chip):
+        return pltpu.make_async_remote_copy(
+            src_ref=self.far_in.at[chip],
+            dst_ref=self.far_in.at[chip],
+            send_sem=self.far_send.at[chip],
+            recv_sem=self.far_recv.at[chip],
+            device_id=(self.first + chip * 2 + self.core, self.w),
+            device_id_type=MESH,
+        )
+
+    def start(self):
+        def step(d, carry):
+            chip = (self.me + 1 + d) % self.count
+            if self.slots < self.count:
+
+                @pl.when(d >= self.slots)
+                def _():
+                    self.near((self.me + 1 + d - self.slots) % self.count).wait_send()
+
+            self.near_out[d % self.slots] = self.make(chip, 1 - self.core).astype(BF16)
+            self.near(chip).start()
+            return carry
+
+        lax.fori_loop(0, self.count, step, 0)
+
+    def send(self):
+        def step(d, carry):
+            chip = (self.me + 1 + d) % self.count
+            own = self.make(chip, self.core)
+            self.near(chip).wait_recv()
+            self.near_in[chip] = (own + self.near_in[chip].astype(F32)).astype(BF16)
+            self.far(chip).start()
+            return carry
+
+        lax.fori_loop(0, self.count - 1, step, 0)
+
+    def finish(self):
+        total = self.make(self.me, self.core)
+        self.near(self.me).wait_recv()
+        total = total + self.near_in[self.me].astype(F32)
+        if self.stage is None:
+            for d in range(1, self.count):
+                chip = (self.me + d) % self.count
+                self.far_arrival(chip).wait_recv()
+                total = total + self.far_in[chip].astype(F32)
+            return total
+        stage, sem = self.stage
+
+        def fetch(d):
+            chip = (self.me + d) % self.count
+            return pltpu.make_async_copy(self.far_in.at[chip], stage.at[d % 2], sem.at[d % 2])
+
+        self.far_arrival((self.me + 1) % self.count).wait_recv()
+        fetch(1).start()
+        for d in range(1, self.count):
+            if d + 1 < self.count:
+                self.far_arrival((self.me + d + 1) % self.count).wait_recv()
+                fetch(d + 1).start()
+            fetch(d).wait()
+            total = total + stage[d % 2].astype(F32)
+        return total
+
+    def drain(self):
+        for d in range(self.count):
+            chip = (self.me + 1 + d) % self.count
+            if d >= self.count - self.slots:
+                self.near(chip).wait_send()
+            if d < self.count - 1:
+                self.far(chip).wait_send()
+
+
+def closing_kernel(
+    geo,
+    rank,
+    len_ref,
+    id_ref,
+    tokens_ref,
+    first_ref,
+    dq_ref,
+    dk_ref,
+    dv_ref,
+    slice_ref,
+    down_ref,
+    up_ref,
+    small_ref,
+    out_down_ref,
+    out_up_ref,
+    fc1_down_ref,
+    fc2_up_ref,
+    fc1_up_ref,
+    fc2_down_ref,
+    grad_ref,
+    sum1_ref,
+    sum2_ref,
+    tok_far,
+    tok_out,
+    tok_in,
+    tok_stage,
+    small_buf,
+    set1_out,
+    set1_in,
+    set1_far,
+    set2_out,
+    set2_in,
+    set2_far,
+    down_acc,
+    up_acc,
+    mine1,
+    mine2,
+    place_buf,
+    fold_buf,
+    all1,
+    all2,
+    places,
+    done1,
+    done2,
+    tok_sems,
+    set1_sems,
+    set2_sems,
+    line_send,
+    line_recv,
+    spread_send,
+    spread_recv,
+    local_sem,
+    stage_sem,
+    small_sem,
+):
+    x, y, core, w = device_here(geo)
+    s = lax.axis_index("seq")
+    rows, width, wt, groups, parts = geo.rows, geo.width, geo.wt, geo.groups, geo.parts
+    part, g = s // groups, s % groups
+    docs = len_ref.shape[1]
+    doc_rows = docs * rank
+    lane_count = down_ref.shape[0] // 3
+    lanes = pl.ds(pl.multiple_of(g * LANES, LANES), LANES)
+    starts, ends = doc_bounds(len_ref)
+    ids = [id_ref[0, d] for d in range(docs)]
+    fresh = []
+    for d in range(docs):
+        seen = jnp.bool_(False)
+        for e in range(d):
+            seen = seen | (ids[e] == ids[d])
+        fresh.append(jnp.where(seen, 0.0, 1.0))
+
+    greet_all(geo)
+
+    def iota(shape, dim):
+        return lax.broadcasted_iota(jnp.int32, shape, dim)
+
+    def zero_one(condition):
+        return jnp.where(condition, 1.0, 0.0).astype(BF16)
+
+    def chosen_of(t):
+        pos = t * rows + iota((rows, LANES), 0)
+        return select_from(pos, starts, ends, id_ref, rank)
+
+    def fold(j):
+        a, b = iota((lane_count, LANES), 0), iota((lane_count, LANES), 1)
+        return zero_one((b >= j * rank) & (b < (j + 1) * rank) & (a % rank == b - j * rank))
+
+    def make_tokens(chip, whose):
+        t = chip * 2 + whose
+        at = pl.ds(pl.multiple_of(t * rows, rows), rows)
+        if parts == 1:
+            d_q = dq_ref[at, :]
+        else:
+            inner = pl.ds(pl.multiple_of((t % groups) * rows, rows), rows)
+            d_q = jnp.where(t // groups == part, dq_ref[inner, :], jnp.zeros((rows, LANES), BF16))
+        pieces = [d_q, dk_ref[at, :], dv_ref[at, :]]
+        chosen = chosen_of(t)
+        total = jnp.zeros((rows, width), F32)
+        low = jnp.zeros((rows, LANES), F32)
+        for j in range(3):
+            total = total + dot_nt(pieces[j], slice_ref[:, j * LANES : (j + 1) * LANES])
+            part_low = dot_nt(pieces[j], up_ref[pl.ds(j * lane_count, lane_count), lanes])
+            low = low + dot_nn((part_low * chosen).astype(BF16), fold(j))
+        return jnp.concatenate([total, low], axis=1)
+
+    tok = PairSum(
+        geo.seq // 2, s // 2, core, 0, w, (tok_out, tok_in, tok_far), [tok_sems.at[i] for i in range(4)], make_tokens,
+        (tok_stage, stage_sem),
+    )
+
+    singles = [out_down_ref, out_up_ref, fc1_down_ref, fc2_up_ref, fc1_up_ref, fc2_down_ref]
+
+    def by_document(value):
+        return dot_tn(fold_buf[...], value)[:doc_rows]
+
+    def make_set1(chip, whose):
+        owner = chip * 2 + whose
+        cols = []
+        for ref in singles:
+            wide = ref.shape[1] // groups
+            cols.append(by_document(ref[:, pl.ds(pl.multiple_of(owner * wide, LANES), wide)]))
+        return jnp.concatenate(cols, axis=1)
+
+    def make_set2(chip, whose):
+        owner = chip * 2 + whose
+        cut = pl.ds(pl.multiple_of(owner * LANES, LANES), LANES)
+        return jnp.concatenate([down_acc[j * doc_rows : (j + 1) * doc_rows, cut] for j in range(3)], axis=1)
+
+    chips = groups // 2
+    set1 = PairSum(
+        chips, g // 2, core, part * groups, w, (set1_out, set1_in, set1_far), [set1_sems.at[i] for i in range(4)], make_set1
+    )
+    set2 = PairSum(
+        chips, g // 2, core, part * groups, w, (set2_out, set2_in, set2_far), [set2_sems.at[i] for i in range(4)], make_set2
+    )
+
+    def peer(n):
+        plane = (w + n) % wt
+        other = (part + n // wt) % parts
+        return other * groups + g, plane, other * wt + plane
+
+    mine_at = part * wt + w
+
+    def line_copy(kind, n, src, dst_all):
+        device, plane, _ = peer(n)
+        return pltpu.make_async_remote_copy(
+            src_ref=src,
+            dst_ref=dst_all.at[mine_at],
+            send_sem=line_send.at[kind, n],
+            recv_sem=line_recv.at[kind, mine_at],
+            device_id=(device, plane),
+            device_id_type=MESH,
+        )
+
+    def line_arrival(kind, n, dst_all):
+        device, plane, at = peer(n)
+        return pltpu.make_async_remote_copy(
+            src_ref=dst_all.at[at],
+            dst_ref=dst_all.at[at],
+            send_sem=line_send.at[kind, n],
+            recv_sem=line_recv.at[kind, at],
+            device_id=(device, plane),
+            device_id_type=MESH,
+        )
+
+    peers = range(1, wt * parts)
+
+    block = Block(geo)
+    chip_here = g // 2
+    here = (chip_here % block.nx, chip_here // block.nx, core, w)
+
+    def region_of(ref):
+        def region(ux, uy, whose, half):
+            one = ref.at[(uy * block.nx + ux) * 2 + whose]
+            if half is None:
+                return one
+            return one.at[pl.ds(half * (lane_count // 2), lane_count // 2)]
+
+        return region
+
+    spreads = [
+        Spread(block, here, region_of(ref), spread_send, spread_recv, i, part * groups)
+        for i, ref in enumerate((sum1_ref, sum2_ref))
+    ]
+    finals = [done1, done2]
+    outs = [sum1_ref, sum2_ref]
+
+    def place(kind, mine, dst_all):
+        total = dot_nn(place_buf[:, :doc_rows], mine[...])
+        for n in peers:
+            line_arrival(kind, n, dst_all).wait_recv()
+            if kind == 0:
+                line_arrival(2, n, places).wait_recv()
+            at = peer(n)[2]
+            total = total + dot_nn(places[at][:, :doc_rows], dst_all[at])
+        finals[kind][...] = total.astype(BF16)
+        for way in (0, 1, 4):
+            spreads[kind].go(way, own=finals[kind])
+        pltpu.make_async_copy(finals[kind], outs[kind].at[g], local_sem.at[kind]).start()
+
+    def pass_on(kind):
+        spread = spreads[kind]
+        spread.wait(0)
+        spread.go(2)
+        spread.go(5)
+        spread.wait(1)
+        spread.go(3)
+        spread.go(6)
+
+    def pass_last(kind):
+        spread = spreads[kind]
+        spread.wait(2)
+        spread.go(7)
+        spread.wait(3)
+        spread.go(8)
+
+    a, b = iota((lane_count, LANES), 0), iota((lane_count, LANES), 1)
+    places_all = jnp.zeros((lane_count, LANES), F32)
+    places_first = jnp.zeros((lane_count, LANES), F32)
+    for d in range(docs):
+        hit = (a // rank == ids[d]) & (b // rank == d) & (a % rank == b % rank)
+        places_all = jnp.where(hit, 1.0, places_all)
+        places_first = jnp.where(hit, fresh[d], places_first)
+    place_buf[...] = places_all.astype(BF16)
+    fold_buf[...] = places_first.astype(BF16)
+    for n in peers:
+        line_copy(2, n, place_buf, places).start()
+
+    set1.start()
+    tok.start()
+    set1.send()
+    tok.send()
+
+    def small_copy(t):
+        return pltpu.make_async_copy(
+            small_ref.at[pl.ds(pl.multiple_of(t * rows, rows), rows)], small_buf.at[t % 2], small_sem.at[t % 2]
+        )
+
+    def add_up(t, carry):
+        at = pl.ds(pl.multiple_of(t * rows, rows), rows)
+
+        @pl.when(t + 1 < geo.seq)
+        def _():
+            small_copy(t + 1).start()
+
+        small_copy(t).wait()
+        for j in range(3):
+            cut = slice(j * LANES, (j + 1) * LANES)
+            if j == 0:
+                if parts == 1:
+                    value = dq_ref[at, :]
+                else:
+                    inner = pl.ds(pl.multiple_of((t % groups) * rows, rows), rows)
+                    value = jnp.where(t // groups == part, dq_ref[inner, :], jnp.zeros((rows, LANES), BF16))
+            else:
+                value = (dk_ref if j == 1 else dv_ref)[at, :]
+            up_acc[cut, :] += dot_tn(small_buf[t % 2][:, cut], value)
+        return carry
+
+    up_acc[...] = jnp.zeros_like(up_acc)
+    small_copy(0).start()
+    lax.fori_loop(0, geo.seq, add_up, 0)
+
+    mine1[...] = set1.finish().astype(BF16)
+    for n in peers:
+        line_copy(0, n, mine1, all1).start()
+
+    total = tok.finish()
+    low = total[:, width:].astype(BF16)
+    total = total[:, :width] + first_ref[...]
+    chosen = chosen_of(s)
+    pos = s * rows + iota((rows, doc_rows), 0)
+    doc_of = iota((rows, doc_rows), 1) // rank
+    in_doc = doc_of == segment_from(pos, starts)
+    tokens = tokens_ref[...]
+    for j in range(3):
+        a, b = iota((LANES, lane_count), 0), iota((LANES, lane_count), 1)
+        widen = zero_one((a >= j * rank) & (a < (j + 1) * rank) & (b % rank == a - j * rank))
+        wide = (dot_nn(low, widen) * chosen).astype(BF16)
+        total = total + dot_nn(wide, down_ref[j * lane_count : (j + 1) * lane_count, :])
+        by_doc = dot_nn(low, widen[:, :doc_rows])
+        by_doc = jnp.where(in_doc, by_doc, 0.0).astype(BF16)
+        down_acc[j * doc_rows : (j + 1) * doc_rows, :] = dot_tn(by_doc, tokens)
+    set2.start()
+    grad_ref[...] = total
+    set2.send()
+    place(0, mine1, all1)
+    for j in range(3):
+        mine2[:, (3 + j) * LANES : (4 + j) * LANES] = by_document(
+            up_acc[j * lane_count : (j + 1) * lane_count, :].astype(BF16)
+        ).astype(BF16)
+    mine2[:, : 3 * LANES] = set2.finish().astype(BF16)
+    for n in peers:
+        line_copy(1, n, mine2, all2).start()
+    pass_on(0)
+    pass_last(0)
+    place(1, mine2, all2)
+    pass_on(1)
+    pass_last(1)
+    for kind in range(2):
+        for way in range(4, 9):
+            spreads[kind].wait(way)
+        spreads[kind].wait_sends()
+        pltpu.make_async_copy(finals[kind], outs[kind].at[g], local_sem.at[kind]).wait()
+    for n in peers:
+        line_copy(0, n, mine1, all1).wait_send()
+        line_copy(1, n, mine2, all2).wait_send()
+        line_copy(2, n, place_buf, places).wait_send()
+    tok.drain()
+    set1.drain()
+    set2.drain()
+
+
+def greet_all(geo):
+    s, w = lax.axis_index("seq"), lax.axis_index("wt")
+    barrier = pltpu.get_barrier_semaphore()
+    part, g = s // geo.groups, s % geo.groups
+    for d in range(1, geo.seq):
+        pl.semaphore_signal(barrier, inc=1, device_id=((s + d) % geo.seq, w), device_id_type=MESH)
+    count = geo.seq - 1
+    for d in range(1, geo.wt):
+        for q in range(geo.parts):
+            other = ((part + q) % geo.parts) * geo.groups + g
+            pl.semaphore_signal(barrier, inc=1, device_id=(other, (w + d) % geo.wt), device_id_type=MESH)
+            count += 1
+    pl.semaphore_wait(barrier, count)
+
+
+def closing(geo, rank, lengths, ids, tokens, d_first, dq, dk, dv, w_slice, down, up, small, grads):
+    rows, width = geo.rows, geo.width
+    docs = lengths.shape[1]
+    doc_rows = docs * rank
+    lane_count = down.shape[0] // 3
+    set1 = sum(v.shape[1] for v in grads) // geo.groups
+    set2 = 6 * LANES
+    chips, near = geo.seq // 2, geo.groups // 2
+    peers = geo.wt * geo.parts
+    smem = pl.BlockSpec(memory_space=pltpu.SMEM)
+    vmem = pl.BlockSpec(memory_space=pltpu.VMEM)
+    any_spec = pl.BlockSpec(memory_space=pl.ANY)
+    dma = pltpu.SemaphoreType.DMA
+    wide = width + LANES
+    return pl.pallas_call(
+        functools.partial(closing_kernel, geo, rank),
+        out_shape=[
+            jax.ShapeDtypeStruct((rows, width), F32),
+            jax.ShapeDtypeStruct((geo.groups, lane_count, set1), BF16),
+            jax.ShapeDtypeStruct((geo.groups, lane_count, set2), BF16),
+            jax.ShapeDtypeStruct((chips, rows, wide), BF16),
+        ],
+        in_specs=[smem, smem] + [vmem] * 8 + [any_spec] + [vmem] * len(grads),
+        out_specs=[vmem, any_spec, any_spec, any_spec],
+        scratch_shapes=[
+            pltpu.VMEM((min(chips, 4), rows, wide), BF16),
+            pltpu.VMEM((chips, rows, wide), BF16),
+            pltpu.VMEM((2, rows, wide), BF16),
+            pltpu.VMEM((2, rows, 3 * lane_count), BF16),
+            pltpu.VMEM((near, doc_rows, set1), BF16),
+            pltpu.VMEM((near, doc_rows, set1), BF16),
+            pltpu.VMEM((near, doc_rows, set1), BF16),
+            pltpu.VMEM((near, doc_rows, 3 * LANES), BF16),
+            pltpu.VMEM((near, doc_rows, 3 * LANES), BF16),
+            pltpu.VMEM((near, doc_rows, 3 * LANES), BF16),
+            pltpu.VMEM((3 * doc_rows, width), F32),
+            pltpu.VMEM((3 * lane_count, LANES), F32),
+            pltpu.VMEM((doc_rows, set1), BF16),
+            pltpu.VMEM((doc_rows, set2), BF16),
+            pltpu.VMEM((lane_count, LANES), BF16),
+            pltpu.VMEM((lane_count, LANES), BF16),
+            pltpu.VMEM((peers, doc_rows, set1), BF16),
+            pltpu.VMEM((peers, doc_rows, set2), BF16),
+            pltpu.VMEM((peers, lane_count, LANES), BF16),
+            pltpu.VMEM((lane_count, set1), BF16),
+            pltpu.VMEM((lane_count, set2), BF16),
+            dma((4, chips)),
+            dma((4, near)),
+            dma((4, near)),
+            dma((3, peers)),
+            dma((3, peers)),
+            dma((Spread.KINDS, 2)),
+            dma((Spread.KINDS, 2)),
+            dma((2,)),
+            dma((2,)),
+            dma((2,)),
+        ],
+        compiler_params=pltpu.CompilerParams(
+            collective_id=1, has_side_effects=True, vmem_limit_bytes=VMEM_LIMIT
+        ),
+        name="close",
+    )(lengths, ids, tokens, d_first, dq, dk, dv, w_slice, down, up, small, *grads)
+
+
+def unpack_kernel(one_ref, two_ref, down_ref, up_ref, fc1_down_ref, fc2_up_ref, fc1_up_ref, fc2_down_ref):
+    for j in range(3):
+        down_ref[j] = two_ref[0, :, j * LANES : (j + 1) * LANES].astype(F32)
+        up_ref[j] = two_ref[0, :, (3 + j) * LANES : (4 + j) * LANES].astype(F32)
+    at = 0
+    for ref in (down_ref.at[3], up_ref.at[3], fc1_down_ref, fc2_up_ref, fc1_up_ref, fc2_down_ref):
+        wide = ref.shape[1]
+        ref[...] = one_ref[0, :, at : at + wide].astype(F32)
+        at += wide
+
+
+def unpack(geo, one, two, lane_count):
+    groups = geo.groups
+    thick = (one.shape[2] - 4 * LANES) // 2
+
+    def whole(wide):
+        return jax.ShapeDtypeStruct((lane_count, wide * groups), F32)
+
+    def flat(wide):
+        return pl.BlockSpec((lane_count, wide), lambda i: (0, i))
+
+    four = jax.ShapeDtypeStruct((4, lane_count, LANES * groups), F32)
+    four_spec = pl.BlockSpec((4, lane_count, LANES), lambda i: (0, 0, i))
+    return pl.pallas_call(
+        unpack_kernel,
+        grid=(groups,),
+        out_shape=[four, four, whole(LANES), whole(LANES), whole(thick), whole(thick)],
+        in_specs=[
+            pl.BlockSpec((1,) + one.shape[1:], lambda i: (i, 0, 0)),
+            pl.BlockSpec((1,) + two.shape[1:], lambda i: (i, 0, 0)),
+        ],
+        out_specs=[four_spec, four_spec, flat(LANES), flat(LANES), flat(thick), flat(thick)],
+        compiler_params=pltpu.CompilerParams(vmem_limit_bytes=VMEM_LIMIT // 2),
+        name="unpack",
+    )(one, two)
 
 
 def layer_norm(value, gain, shift):
@@ -857,20 +1398,20 @@
     low_fc2 = (times_transposed(d_y, fc2_up_all) * select).astype(jnp.bfloat16)
     d_act = d_act + times_transposed(low_fc2, fc2_down_all)
     grad_fc2_up = left_inner(small_fc2, d_y)
-    grad_fc2_down = left_inner(act_low, low_fc2)
+    grad_fc2_down = left_inner(low_fc2, act_low)
     d_pre = gelu_back(d_act)[0].astype(jnp.bfloat16)
     d_first_low = times_transposed(d_pre, full_fc1)
     low_fc1 = (times_transposed(d_pre, fc1_up_all) * select).astype(jnp.bfloat16)
     d_first_low = d_first_low + times_transposed(low_fc1, fc1_down_all)
     grad_fc1_up = left_inner(small_fc1, d_pre)
-    grad_fc1_down = left_inner(first_low, low_fc1)
+    grad_fc1_down = left_inner(low_fc1, first_low)
     d_first = norm1_back(d_second + d_first_low)[0]
     d_z = d_first.astype(jnp.bfloat16)
     d_attended = times_transposed(d_z, full_out)
     low_out = (times_transposed(d_z, out_up) * select).astype(jnp.bfloat16)
     d_attended = (d_attended + times_transposed(low_out, out_down)).astype(jnp.bfloat16)
     grad_out_up = left_inner(small_out, d_z)
-    grad_out_down = left_inner(attended_tok, low_out)
+    grad_out_down = left_inner(low_out, attended_tok)
     blocks = [
         [p * geo.groups + i for i in range(geo.groups)] for p in range(geo.parts)
     ]
@@ -885,70 +1426,44 @@
     d_q, d_k, d_v = backward_attention(
         geo, doc_lengths, part_index.reshape(1, 1), q_heads, k_heads, v_heads, o_heads, lse_heads, d_heads
     )
-    if geo.parts > 1:
-        d_q = lax.dynamic_update_slice_in_dim(
-            jnp.zeros((geo.keys, LANES), BF16), d_q, part_index * geo.queries, 0
-        )
-    d_three = jnp.concatenate([d_q, d_k, d_v], axis=1)
-    partial = times_transposed(d_three, w_slice).astype(BF16).reshape(seq_count, tok_rows, model_width)
-    d_tokens = jnp.sum(
-        lax.all_to_all(partial, "seq", split_axis=0, concat_axis=0, tiled=True).astype(F32), axis=0
+    set1 = [
+        v.astype(BF16) for v in (grad_out_down, grad_out_up, grad_fc1_down, grad_fc2_up, grad_fc1_up, grad_fc2_down)
+    ]
+    input_grad, sum1, sum2, _ = closing(
+        geo,
+        rank_size,
+        doc_lengths,
+        adapter_ids,
+        tokens,
+        d_first,
+        d_q,
+        d_k,
+        d_v,
+        w_slice,
+        down_rows[: 3 * lane_count],
+        up_rows[: 3 * lane_count],
+        small_all,
+        set1,
     )
-    up_slice = lax.dynamic_slice_in_dim(up_rows[: 3 * lane_count], head_index * LANES, LANES, 1)
-    low_part = jnp.concatenate(
-        [
-            times_transposed(
-                d_three[:, i * LANES : (i + 1) * LANES], up_slice[i * lane_count : (i + 1) * lane_count]
-            )
-            for i in range(3)
-        ],
-        axis=1,
+
+    down4, up4, fc1_down_sum, fc2_up_sum, fc1_up_sum, fc2_down_sum = unpack(geo, sum1, sum2, lane_count)
+
+    def as_up(rows):
+        return rows.reshape(rows.shape[:-2] + (adapter_count, rank_size, rows.shape[-1]))
+
+    def as_down(rows):
+        return jnp.swapaxes(as_up(rows), -1, -2)
+
+    return (
+        output,
+        input_grad,
+        as_down(down4),
+        as_up(up4),
+        as_down(fc1_down_sum),
+        as_up(fc1_up_sum),
+        as_down(fc2_down_sum),
+        as_up(fc2_up_sum),
     )
-    low_sum = lax.psum_scatter(low_part, "seq", scatter_dimension=0, tiled=True)
-    low_qkv = (low_sum * jnp.tile(select, (1, 3))).astype(BF16)
-    input_grad = d_first + d_tokens + jnp.dot(
-        low_qkv, down_rows[: 3 * lane_count], preferred_element_type=F32
-    )
-    grad_qkv_down = left_inner(low_qkv, tokens)
-    grad_qkv_up = []
-    for i in range(3):
-        cut = slice(i * LANES, (i + 1) * LANES)
-        own = left_inner(small_all[:, cut], d_three[:, cut])
-        grad_qkv_up.append(
-            lax.dynamic_update_slice_in_dim(
-                jnp.zeros((lane_count, model_width), F32), own, head_index * LANES, 1
-            )
-        )
-    grad_attn_down = jnp.stack(
-        [
-            jnp.transpose(
-                grad_qkv_down[i * lane_count : (i + 1) * lane_count].reshape(
-                    adapter_count, rank_size, model_width
-                ),
-                (0, 2, 1),
-            )
-            for i in range(3)
-        ]
-        + [unstack_down(grad_out_down, adapter_count, rank_size)]
-    )
-    grad_attn_up = jnp.stack(
-        [
-            unstack_up(piece_grad, adapter_count, rank_size)
-            for piece_grad in grad_qkv_up + [grad_out_up]
-        ]
-    )
-    summed = lax.psum(
-        (
-            grad_attn_down,
-            grad_attn_up,
-            unstack_down(grad_fc1_down, adapter_count, rank_size),
-            unstack_up(grad_fc1_up, adapter_count, rank_size),
-            unstack_down(grad_fc2_down, adapter_count, rank_size),
-            unstack_up(grad_fc2_up, adapter_count, rank_size),
-        ),
-        ("seq", "wt"),
-    )
-    return (output, input_grad, summed[0], summed[1], summed[2], summed[3], summed[4], summed[5])
 
 
 def solution(mesh):

time: 551 us -> 348 us (0.63)
  waiting for transfers between devices: 181 us -> 0.01 us
  Pallas kernels: 188 us -> 277 us
  blocking collectives: 70.8 us -> 0 us
  between operations: 14.9 us -> 1.24 us
  matrix products: 59.7 us -> 48.5 us
  local copies, waits for them, and re-layouts: 20.5 us -> 12.4 us
  other arithmetic: 10.3 us -> 3.39 us
    psum x1 -> x0, waiting for transfers between devices: 143 us -> none  [shards(): lax.psum((grad_attn_down, grad_attn_up, unstack_down(grad_fc1_down, adapt...]
    pallas_call x0 -> x2, Pallas kernels: none -> 88.9 us  [the longest x1 84.4 us: closing(): pl.pallas_call(functools.partial(closing_kernel, geo, rank), out_shape=[j...]
    all_to_all x1 -> x0, blocking collectives: 70.8 us -> none  [shards(): lax.all_to_all(partial, 'seq', split_axis=0, concat_axis=0, tiled=True)]
    reduce_scatter x1 -> x0, waiting for transfers between devices: 29 us -> none  [shards(): low_sum = lax.psum_scatter(low_part, 'seq', scatter_dimension=0, tiled=True)]
    all_to_all x1, waiting for transfers between devices: 9.68 us -> 0.01 us  [shards(): lax.all_to_all(d_attended.reshape(tok_rows, geo.groups, LANES), 'seq', sp...]
    dot_general x13 -> x9, matrix products: 23.1 us -> 15.3 us  [times_transposed(): lax.dot_general(grad, weight, (((1,), (1,)), ((), ())), preferred_element...]
    unnamed x110 -> x69, local copies, waits for them, and re-layouts: 12.2 us -> 5.2 us
    dot_general x10 -> x6, matrix products: 12.9 us -> 11 us  [left_inner(): lax.dot_general(left, right, (((0,), (0,)), ((), ())), preferred_element_...]
  transfers between devices with their start and end apart: 3 -> 1, of which waited for: 3 -> 0; matrix products, arithmetic and copies ran while one was open for 4% -> 3% of each run, Pallas kernels for 0% -> 0%
where the time goes in v2:
time: 348 us; the launch traced here: 347 us
  Pallas kernels  277 us (80%)
  matrix products  48.5 us (14%)
  local copies, waits for them, and re-layouts  12.4 us (4%)
  starting transfers between devices  4.51 us (1%)
    pallas_call x1, Pallas kernels, forward_attention(): pl.pallas_call(functools.partial(forward_kernel, geo, count, rank), out_s...  156 us
    pallas_call x1, Pallas kernels, closing(): pl.pallas_call(functools.partial(closing_kernel, geo, rank), out_shape=[j...  84.4 us
    pallas_call x1, Pallas kernels, backward_attention(): pl.pallas_call(functools.partial(backward_kernel, geo), out_shape=[jax.Sh...  31.8 us
    dot_general x9, matrix products, times_transposed(): lax.dot_general(grad, weight, (((1,), (1,)), ((), ())), preferred_element...  15.3 us
    dot_general x6, matrix products, left_inner(): lax.dot_general(left, right, (((0,), (0,)), ((), ())), preferred_element_...  11 us
    dot_general x1, matrix products, shards(): jnp.dot(small_fc1, fc1_up_all, preferred_element_type=jnp.float32)  11 us
  transfers between devices with their start and end apart: 1, of which 0 were waited for; matrix products, arithmetic and copies ran while one was open for 3% of the time, Pallas kernels for 0%

profile of v2, /device:TPU:0, one launch (start us, length us, event | category | flops | bytes accessed | tf_op | source)
XLA Modules:
  0.0 347.2 jit_solution(10896890788831400788)
XLA Ops:
  0.7 2.2 slice.22
  2.9 1.0 slice.25
  3.9 1.1 slice.24
  4.9 2.1 slice.26
  7.4 156.3 %gather_attend.1 = (bf16[256,1024]{1,0:T(8,128)(2,1)}, bf16[2048,128]{1,0:T(8,128)(2,1)}, bf16[2048,128]{1,0:T(8,128)(2,1)}, bf16[2048,128]{1,0:T(8,128)(2,1)}, ...) custom-call(s32[1,4]{1,0:T(1,128)} %len_ref.5, ...), custom_call_target="tpu_custom_call" | custom-call | tf_op jit(solution)/shard_map/gather_attend/pallas_call | solution.py:592
  163.8 2.6 convolution_add_fusion.7
  166.4 2.1 fusion.14
  169.8 2.3 convolution_add_fusion.2
  172.3 11.0 %multiply_convert_fusion = (bf16[256,4096]{1,0:T(8,128)(2,1)S(1)}, f32[256,4096]{1,0:T(8,128)}, f32[256,4096]{1,0:T(8,128)}) fusion(f32[256,4096]{1,0:T(8,128)S(1)} %convolution_add_fusion.2, bf16[256,128]{1,0:T(8,128)(2,1)S(1)} %fusion.15, bf16[128,4096]{1,0:T(8,128)(2,1)S(1)} %bitcast.88), kind=kOutput, calls=%fused_computation.8 | convolution fusion | flops 337641472 | bytes 15794176 | tf_op jit(solution)/shard_map/dot_general | solution.py:1381
  183.2 0.7 fusion.12
  184.0 2.3 convolution_add_fusion.8
  187.3 1.4 fusion.26
  189.2 4.3 %fusion.30 = f32[256,4096]{1,0:T(8,128)} fusion(bf16[256,1024]{1,0:T(8,128)(2,1)S(1)} %add_convert_fusion.1, bf16[4096,1024]{1,0:T(8,128)(2,1)S(1)} %bitcast.108), kind=kOutput, calls=%fused_computation.91 | convolution fusion | flops 2147483648 | bytes 13107200 | tf_op jit(solution)/shard_map/dot_general | solution.py:1265
  193.5 5.7 %add_convert_fusion = bf16[256,4096]{1,0:T(8,128)(2,1)S(1)} fusion(f32[256,4096]{1,0:T(8,128)} %get-tuple-element.61, f32[256,4096]{1,0:T(8,128)} %fusion.30, bf16[256,128]{1,0:T(8,128)(2,1)S(1)} %fusion.16, bf16[4096,128]{0,1:T(8,128)(2,1)S(1)} %bitcast.100, f32[256,4096]{1,0:T(8,128)} %get-tuple-element.67), kind=kOutput, calls=%fused_computation.7 | convolution fusion | flops 284164096 | bytes 15794176 | tf_op jit(solution)/shard_map/dot_general | solution.py:1265
  199.3 0.7 fusion.13
  200.0 2.4 fusion.31
  203.8 0.8 copy-done.9
  204.6 0.8 fusion.23
  205.7 0.9 copy.34
  206.6 4.5 %all-to-all-start = ((bf16[256,8,128]{2,0,1:T(8,128)(2,1)}), bf16[256,8,128]{2,0,1:T(8,128)(2,1)}, u32[]{:S(2)}, u32[]{:S(2)}) async-start(bf16[256,8,128]{2,0,1:T(8,128)(2,1)} %bitcast.98), calls=%async_computation | async-start | bytes 1048576 | tf_op jit(solution)/shard_map/all_to_all | solution.py:1418
  211.1 3.1 convolution_convert_fusion.fc2_down_ref
  214.1 1.0 convolution_convert_fusion.2.fc2_up_ref
  215.1 1.0 convolution_convert_fusion.3.fc1_down_ref
  216.1 1.0 convolution_convert_fusion.4.out_up_ref
  217.1 2.0 convolution_convert_fusion.5.out_down_ref
  219.1 3.0 convolution_convert_fusion.1.fc1_up_ref
  222.1 31.8 %attend_back.1 = (bf16[2048,128]{1,0:T(8,128)(2,1)}, bf16[2048,128]{1,0:T(8,128)(2,1)}, bf16[2048,128]{1,0:T(8,128)(2,1)}) custom-call(s32[1,4]{1,0:T(1,128)} %len_ref.5, s32[1,1]{1,0:T(1,128)} %bitcast.17.part_ref, bf16[2048,128]{1,0:T(8,128)(2,1)} %get-tuple-element.35.q_ref, bf16[2048,128]{1,0:T(8,128)(2,1)} %get-tuple-element.36.k_ref, ...), custom_call_target="tpu_custom_call" | custom-call | tf_op jit(solution)/shard_map/attend_back/pallas_call | solution.py:697
  254.0 84.4 %close.1 = (f32[256,1024]{1,0:T(8,128)}, bf16[8,128,1536]{2,1,0:T(8,128)(2,1)}, bf16[8,128,768]{2,1,0:T(8,128)(2,1)}, bf16[4,256,1152]{2,1,0:T(8,128)(2,1)}) custom-call(s32[1,4]{1,0:T(1,128)} %len_ref.5, s32[1,4]{1,0:T(1,128)} %id_ref.3, bf16[256,1024]{1,0:T(8,128)(2,1)} %tokens_ref.3, f32[256,1024]{1,0:T(8,128)} %copy-done.3, ...), custom_call_target="tpu_custom_call" | custom-call | tf_op jit(solution)/shard_map/close/pallas_call | solution.py:1166
  338.4 1.9 copy-done.1
  340.2 1.4 copy-done.2
  341.7 4.5 %unpack.1 = (f32[4,128,1024]{2,1,0:T(8,128)}, f32[4,128,1024]{2,1,0:T(8,128)}, f32[128,1024]{1,0:T(8,128)}, f32[128,1024]{1,0:T(8,128)}, f32[128,4096]{1,0:T(8,128)}, /*index=5*/f32[128,4096]{1,0:T(8,128)}) custom-call(bf16[8,128,1536]{2,1,0:T(8,128)(2,1)S(1)} %copy-done.1, bf16[8,128,768]{2,1,0:T(8,128)(2,1)S(1)} %copy-done.2), custom_call_target="tpu_custom_call" | custom-call | tf_op jit(solution)/shard_map/unpack/pallas_call | solution.py:1239
  346.2 1.0 copy.36
  (94 shorter events, 4.7 us)
Async XLA Ops:
  0.6 171.6 %copy-start = (bf16[8,16,4096]{2,1,0:T(8,128)(2,1)S(1)}, bf16[8,16,4096]{2,1,0:T(8,128)(2,1)}, u32[]{:S(2)}) copy-start(bf16[8,16,4096]{2,1,0:T(8,128)(2,1)} %param.41) | copy-start | bytes 3145732
  0.6 6.4 %copy-start.25 = (s32[1,4]{1,0:T(1,128)S(1)}, s32[1,4]{1,0:T(1,128)}, u32[]{:S(2)}) copy-start(s32[1,4]{1,0:T(1,128)} %len_ref.5) | copy-start | bytes 52
  0.7 6.7 %copy-start.26 = (s32[1,4]{1,0:T(1,128)S(1)}, s32[1,4]{1,0:T(1,128)}, u32[]{:S(2)}) copy-start(s32[1,4]{1,0:T(1,128)} %id_ref.3) | copy-start | bytes 52
  3.9 164.7 %copy-start.7 = (bf16[1,8,16,1024]{3,2,1,0:T(8,128)(2,1)}, bf16[1,8,16,1024]{3,2,1,0:T(8,128)(2,1)S(1)}, u32[]{:S(2)}) copy-start(bf16[1,8,16,1024]{3,2,1,0:T(8,128)(2,1)S(1)} %slice.25) | copy-start | bytes 786436
  7.4 156.3 %copy-start.30 = (f32[1024]{0:T(1024)S(1)}, f32[1024]{0:T(1024)}, u32[]{:S(2)}) copy-start(f32[1024]{0:T(1024)} %param.27) | copy-start | bytes 12292
  163.7 4.8 %copy-start.6 = (bf16[256,1024]{1,0:T(8,128)(2,1)S(1)}, bf16[256,1024]{1,0:T(8,128)(2,1)}, u32[]{:S(2)}) copy-start(bf16[256,1024]{1,0:T(8,128)(2,1)} %tokens_ref.3) | copy-start | bytes 1572868
  163.7 5.5 %copy-start.22 = (f32[1024]{0:T(1024)S(1)}, f32[1024]{0:T(1024)}, u32[]{:S(2)}) copy-start(f32[1024]{0:T(1024)} %param.28) | copy-start | bytes 12292
  163.8 5.4 %copy-start.23 = (f32[1024]{0:T(1024)S(1)}, f32[1024]{0:T(1024)}, u32[]{:S(2)}) copy-start(f32[1024]{0:T(1024)} %param.29) | copy-start | bytes 12292
  163.8 6.0 %copy-start.28 = (bf16[1024,4096]{1,0:T(8,128)(2,1)S(1)}, bf16[1024,4096]{1,0:T(8,128)(2,1)}, u32[]{:S(2)}) copy-start(bf16[1024,4096]{1,0:T(8,128)(2,1)} %get-tuple-element.33) | copy-start | bytes 25165828
  166.4 3.1 copy-start.14
  166.4 3.4 copy-start.29
  168.5 3.7 %copy-start.15 = (bf16[256,128]{1,0:T(8,128)(2,1)}, bf16[256,128]{1,0:T(8,128)(2,1)S(1)}, u32[]{:S(2)}) copy-start(bf16[256,128]{1,0:T(8,128)(2,1)S(1)} %fusion.14) | copy-start | bytes 196612
  169.8 2.4 copy-start.19
  169.8 14.1 %slice-start = ((s8[8388608]{0:T(1024)(128)(4,1)}), s8[4194304]{0:T(1024)(128)(4,1)S(1)}, s32[]{:S(2)}) async-start(s8[8388608]{0:T(1024)(128)(4,1)} %bitcast.107), calls=%async_computation.1 | async-start | bytes 8388608
  172.2 11.0 %copy-start.11 = (bf16[8,4096,16]{1,2,0:T(8,128)(2,1)S(1)}, bf16[8,4096,16]{1,2,0:T(8,128)(2,1)}, u32[]{:S(2)}) copy-start(bf16[8,4096,16]{1,2,0:T(8,128)(2,1)} %param.42) | copy-start | bytes 3145732
  172.2 11.7 %slice-start.1 = ((s8[8388608]{0:T(1024)(128)(4,1)}), s8[4194304]{0:T(1024)(128)(4,1)S(1)}, s32[]{:S(2)}) async-start(s8[8388608]{0:T(1024)(128)(4,1)} %bitcast.107), calls=%async_computation.2 | async-start | bytes 8388608
  172.2 11.7 %copy-start.31 = (f32[1024]{0:T(1024)S(1)}, f32[1024]{0:T(1024)}, u32[]{:S(2)}) copy-start(f32[1024]{0:T(1024)} %param.33) | copy-start | bytes 12292
  183.2 3.1 copy-start.5
  184.0 2.4 copy-start.12
  184.0 2.9 copy-start.10
  184.0 2.9 copy-start.24
  189.2 4.3 %copy-start.21 = (bf16[256,128]{1,0:T(8,128)(2,1)}, bf16[256,128]{1,0:T(8,128)(2,1)S(1)}, u32[]{:S(2)}) copy-start(bf16[256,128]{1,0:T(8,128)(2,1)S(1)} %fusion.16) | copy-start | bytes 196612
  199.2 3.1 copy-start.4
  202.9 1.7 copy-start.9
  203.5 12.6 %copy-start.3 = (f32[256,1024]{1,0:T(8,128)}, f32[256,1024]{1,0:T(8,128)S(1)}, u32[]{:S(2)}) copy-start(f32[256,1024]{1,0:T(8,128)S(1)} %broadcast_add_fusion.first_ref) | copy-start | bytes 3145732
  204.6 2.0 copy-start.17
  205.6 10.4 %copy-start.16 = (bf16[256,128]{1,0:T(8,128)(2,1)S(1)}, bf16[256,128]{1,0:T(8,128)(2,1)}, u32[]{:S(2)}) copy-start(bf16[256,128]{1,0:T(8,128)(2,1)} %copy-done.15) | copy-start | bytes 196612
  206.5 12.5 %copy-start.20 = (bf16[256,128]{1,0:T(8,128)(2,1)S(1)}, bf16[256,128]{1,0:T(8,128)(2,1)}, u32[]{:S(2)}) copy-start(bf16[256,128]{1,0:T(8,128)(2,1)} %copy-done.19) | copy-start | bytes 196612
  206.5 10.5 %copy-start.18 = (bf16[256,128]{1,0:T(8,128)(2,1)S(1)}, bf16[256,128]{1,0:T(8,128)(2,1)}, u32[]{:S(2)}) copy-start(bf16[256,128]{1,0:T(8,128)(2,1)} %copy-done.17) | copy-start | bytes 196612
  206.6 15.6 %all-to-all-start = ((bf16[256,8,128]{2,0,1:T(8,128)(2,1)}), bf16[256,8,128]{2,0,1:T(8,128)(2,1)}, u32[]{:S(2)}, u32[]{:S(2)}) async-start(bf16[256,8,128]{2,0,1:T(8,128)(2,1)} %bitcast.98), calls=%async_computation | async-start | bytes 1048576 | tf_op jit(solution)/shard_map/all_to_all | solution.py:1418
  338.3 1.9 copy-start.1
  341.6 4.5 %copy-start.13 = (f32[256,1024]{1,0:T(8,128)S(1)}, f32[256,1024]{1,0:T(8,128)}, u32[]{:S(2)}) copy-start(f32[256,1024]{1,0:T(8,128)} %get-tuple-element.81) | copy-start | bytes 3145732
  (3 other events, 3.4 us)

commit v3 on v2

--- a/solution.py
+++ b/solution.py
@@ -207,6 +207,7 @@
         line_recv,
         att_send,
         att_recv,
+        *weights_buf,
     ) = refs[2 * weight_count + 8 :]
     here = device_here(geo)
     x, y, core, w = here
@@ -228,7 +229,14 @@
     for m in range(weight_count):
         height = weights_in[m].shape[0]
         dst = weights_out[m].at[pl.ds(pl.multiple_of(w * height, height), height)]
-        own_weights.append(pltpu.make_async_copy(weights_in[m], dst, local_sem.at[4 + m]))
+        stage = weights_buf[m]
+        pltpu.make_async_copy(weights_in[m], stage, local_sem.at[4 + m]).start()
+        own_weights.append(
+            (
+                pltpu.make_async_copy(weights_in[m], stage, local_sem.at[4 + m]),
+                pltpu.make_async_copy(stage, dst, local_sem.at[4 + m]),
+            )
+        )
 
     greet(geo)
 
@@ -270,9 +278,6 @@
     for d in range(1, wt):
         for j in range(3):
             slice_copy(j, d).start()
-    for copy in own_weights:
-        copy.start()
-
     starts, ends = doc_bounds(len_ref)
     seg_buf[...] = segment_from(lax.broadcasted_iota(jnp.int32, seg_buf.shape, 1), starts)
 
@@ -318,7 +323,7 @@
 
         return Spread(geo, here, region, send_sem, recv_sem, 1 + m * wt + p)
 
-    units = [(m, j) for m in range(weight_count) for j in range(wt - 1)]
+    units = [(m, j) for j in range(wt - 1) for m in range(weight_count)]
 
     def start_lines():
         for m in range(weight_count):
@@ -390,6 +395,9 @@
             own_tok.wait()
             for copy in own_slices:
                 copy.wait()
+            for fetch, store in own_weights:
+                fetch.wait()
+                store.start()
             for d in range(1, wt):
                 for j in range(3):
                     slice_arrival(j, d).wait_recv()
@@ -434,7 +442,7 @@
         pos = t * rows + lax.broadcasted_iota(jnp.int32, (rows, LANES), 0)
         chosen = select_from(pos, starts, ends, id_ref, rank)
         main = dot_nn(block, slice_ref[...])
-        small = dot_nt(block, down_ref[...])
+        small = dot_nt(block, down_ref[: 3 * LANES, :])
         for j in range(3):
             cut = slice(j * LANES, (j + 1) * LANES)
             low = (small[:, cut] * chosen).astype(BF16)
@@ -544,7 +552,7 @@
         for j in range(3):
             slice_copy(j, d).wait_send()
     for m in range(weight_count):
-        own_weights[m].wait()
+        own_weights[m][1].wait()
 
         @pl.when(w < wt - 1)
         def _():
@@ -607,7 +615,8 @@
             dma((max(count, 1) * geo.wt,)),
             dma((geo.groups,)),
             dma((geo.groups,)),
-        ],
+        ]
+        + [pltpu.VMEM(v.shape, BF16) for v in weights],
         compiler_params=pltpu.CompilerParams(
             collective_id=0, has_side_effects=True, vmem_limit_bytes=VMEM_LIMIT
         ),
@@ -881,7 +890,7 @@
     part, g = s // groups, s % groups
     docs = len_ref.shape[1]
     doc_rows = docs * rank
-    lane_count = down_ref.shape[0] // 3
+    lane_count = down_ref.shape[0] // 4
     lanes = pl.ds(pl.multiple_of(g * LANES, LANES), LANES)
     starts, ends = doc_bounds(len_ref)
     ids = [id_ref[0, d] for d in range(docs)]
@@ -1153,7 +1162,7 @@
     rows, width = geo.rows, geo.width
     docs = lengths.shape[1]
     doc_rows = docs * rank
-    lane_count = down.shape[0] // 3
+    lane_count = down.shape[0] // 4
     set1 = sum(v.shape[1] for v in grads) // geo.groups
     set2 = 6 * LANES
     chips, near = geo.seq // 2, geo.groups // 2
@@ -1353,8 +1362,8 @@
         adapter_ids,
         tokens,
         w_qkv,
-        down_rows[: 3 * lane_count],
-        up_rows[: 3 * lane_count],
+        down_rows,
+        up_rows,
         qv_bias,
         [v for v, here in zip(weights, inside) if here],
     )
@@ -1440,8 +1449,8 @@
         d_k,
         d_v,
         w_slice,
-        down_rows[: 3 * lane_count],
-        up_rows[: 3 * lane_count],
+        down_rows,
+        up_rows,
         small_all,
         set1,
     )

time: 348 us -> 305 us (0.88)
  Pallas kernels: 277 us -> 233 us
  local copies, waits for them, and re-layouts: 12.4 us -> 7.99 us
    pallas_call x1, Pallas kernels: 156 us -> 119 us  [forward_attention(): pl.pallas_call(functools.partial(forward_kernel, geo, count, rank), out_s...]
    pallas_call x1, Pallas kernels: 31.8 us -> 25.7 us  [backward_attention(): pl.pallas_call(functools.partial(backward_kernel, geo), out_shape=[jax.Sh...]
    slice x2 -> x0, local copies, waits for them, and re-layouts: 4.29 us -> none  [the longest x1 2.2 us: shards(): up_rows[:3 * lane_count]]
  transfers between devices with their start and end apart: 1 -> 1, of which waited for: 0 -> 0; matrix products, arithmetic and copies ran while one was open for 3% -> 4% of each run, Pallas kernels for 0% -> 0%
where the time goes in v3:
time: 305 us; the launch traced here: 301 us
  Pallas kernels  233 us (76%)
  matrix products  48.5 us (16%)
  local copies, waits for them, and re-layouts  7.99 us (3%)
  other arithmetic  5.43 us (2%)
  starting transfers between devices  4.38 us (1%)
    pallas_call x1, Pallas kernels, forward_attention(): pl.pallas_call(functools.partial(forward_kernel, geo, count, rank), out_s...  119 us
    pallas_call x1, Pallas kernels, closing(): pl.pallas_call(functools.partial(closing_kernel, geo, rank), out_shape=[j...  84.5 us
    pallas_call x1, Pallas kernels, backward_attention(): pl.pallas_call(functools.partial(backward_kernel, geo), out_shape=[jax.Sh...  25.7 us
    dot_general x9, matrix products, times_transposed(): lax.dot_general(grad, weight, (((1,), (1,)), ((), ())), preferred_element...  15.3 us
    dot_general x6, matrix products, left_inner(): lax.dot_general(left, right, (((0,), (0,)), ((), ())), preferred_element_...  11 us
    dot_general x1, matrix products, shards(): jnp.dot(small_fc1, fc1_up_all, preferred_element_type=jnp.float32)  11 us
  transfers between devices with their start and end apart: 1, of which 0 were waited for; matrix products, arithmetic and copies ran while one was open for 4% of the time, Pallas kernels for 0%

profile of v3, /device:TPU:0, one launch (start us, length us, event | category | flops | bytes accessed | tf_op | source)
XLA Modules:
  0.0 300.9 jit_solution(2555154024099269529)
XLA Ops:
  0.7 0.9 reduce-window_clone.1
  2.3 1.0 slice.6
  3.3 1.0 slice.7
  4.3 0.7 select_reduce_fusion
  5.0 118.8 %gather_attend.1 = (bf16[256,1024]{1,0:T(8,128)(2,1)}, bf16[2048,128]{1,0:T(8,128)(2,1)}, bf16[2048,128]{1,0:T(8,128)(2,1)}, bf16[2048,128]{1,0:T(8,128)(2,1)}, ...) custom-call(s32[1,4]{1,0:T(1,128)} %len_ref.5, ...), custom_call_target="tpu_custom_call" | custom-call | tf_op jit(solution)/shard_map/gather_attend/pallas_call | solution.py:600
  123.9 2.6 convolution_add_fusion.7
  126.5 2.1 fusion.14
  129.9 2.3 convolution_add_fusion.2
  132.3 11.0 %multiply_convert_fusion = (bf16[256,4096]{1,0:T(8,128)(2,1)S(1)}, f32[256,4096]{1,0:T(8,128)}, f32[256,4096]{1,0:T(8,128)}) fusion(f32[256,4096]{1,0:T(8,128)S(1)} %convolution_add_fusion.2, bf16[256,128]{1,0:T(8,128)(2,1)S(1)} %fusion.15, bf16[128,4096]{1,0:T(8,128)(2,1)S(1)} %bitcast.89), kind=kOutput, calls=%fused_computation.8 | convolution fusion | flops 337641472 | bytes 15794176 | tf_op jit(solution)/shard_map/dot_general | solution.py:1390
  143.3 0.7 fusion.12
  144.1 2.3 convolution_add_fusion.8
  147.3 1.4 fusion.26
  149.2 4.3 %fusion.30 = f32[256,4096]{1,0:T(8,128)} fusion(bf16[256,1024]{1,0:T(8,128)(2,1)S(1)} %add_convert_fusion.1, bf16[4096,1024]{1,0:T(8,128)(2,1)S(1)} %bitcast.108), kind=kOutput, calls=%fused_computation.91 | convolution fusion | flops 2147483648 | bytes 13107200 | tf_op jit(solution)/shard_map/dot_general | solution.py:1274
  153.5 5.7 %add_convert_fusion = bf16[256,4096]{1,0:T(8,128)(2,1)S(1)} fusion(f32[256,4096]{1,0:T(8,128)} %get-tuple-element.61, f32[256,4096]{1,0:T(8,128)} %fusion.30, bf16[256,128]{1,0:T(8,128)(2,1)S(1)} %fusion.16, bf16[4096,128]{0,1:T(8,128)(2,1)S(1)} %bitcast.101, f32[256,4096]{1,0:T(8,128)} %get-tuple-element.67), kind=kOutput, calls=%fused_computation.7 | convolution fusion | flops 284164096 | bytes 15794176 | tf_op jit(solution)/shard_map/dot_general | solution.py:1274
  159.3 0.7 fusion.13
  160.0 2.4 fusion.31
  163.8 0.8 copy-done.7
  164.6 0.8 fusion.23
  165.6 0.9 copy.34
  166.5 4.4 %all-to-all-start = ((bf16[256,8,128]{2,0,1:T(8,128)(2,1)}), bf16[256,8,128]{2,0,1:T(8,128)(2,1)}, u32[]{:S(2)}, u32[]{:S(2)}) async-start(bf16[256,8,128]{2,0,1:T(8,128)(2,1)} %bitcast.99), calls=%async_computation | async-start | bytes 1048576 | tf_op jit(solution)/shard_map/all_to_all | solution.py:1427
  170.9 3.0 %convolution_convert_fusion.fc2_down_ref = bf16[128,4096]{1,0:T(8,128)(2,1)} fusion(bf16[256,128]{1,0:T(8,128)(2,1)S(1)} %fusion.16, bf16[256,4096]{1,0:T(8,128)(2,1)} %copy-done.5), kind=kOutput, calls=%fused_computation.4 | convolution fusion | flops 268959744 | bytes 3211264 | tf_op jit(solution)/shard_map/dot_general | solution.py:1280
  173.9 1.0 convolution_convert_fusion.2.fc2_up_ref
  174.9 1.0 convolution_convert_fusion.3.fc1_down_ref
  175.9 1.0 convolution_convert_fusion.4.out_up_ref
  176.9 2.0 convolution_convert_fusion.5.out_down_ref
  178.9 3.0 %convolution_convert_fusion.1.fc1_up_ref = bf16[128,4096]{1,0:T(8,128)(2,1)} fusion(bf16[256,128]{1,0:T(8,128)(2,1)S(1)} %fusion.15, bf16[256,4096]{1,0:T(8,128)(2,1)} %copy-done.4), kind=kOutput, calls=%fused_computation.5 | convolution fusion | flops 268959744 | bytes 3211264 | tf_op jit(solution)/shard_map/dot_general | solution.py:1280
  181.9 25.7 %attend_back.1 = (bf16[2048,128]{1,0:T(8,128)(2,1)}, bf16[2048,128]{1,0:T(8,128)(2,1)}, bf16[2048,128]{1,0:T(8,128)(2,1)}) custom-call(s32[1,4]{1,0:T(1,128)} %len_ref.5, s32[1,1]{1,0:T(1,128)} %bitcast.17.part_ref, bf16[2048,128]{1,0:T(8,128)(2,1)} %get-tuple-element.35.q_ref, bf16[2048,128]{1,0:T(8,128)(2,1)} %get-tuple-element.36.k_ref, ...), custom_call_target="tpu_custom_call" | custom-call | tf_op jit(solution)/shard_map/attend_back/pallas_call | solution.py:706
  207.6 84.5 %close.1 = (f32[256,1024]{1,0:T(8,128)}, bf16[8,128,1536]{2,1,0:T(8,128)(2,1)}, bf16[8,128,768]{2,1,0:T(8,128)(2,1)}, bf16[4,256,1152]{2,1,0:T(8,128)(2,1)}) custom-call(s32[1,4]{1,0:T(1,128)} %len_ref.5, s32[1,4]{1,0:T(1,128)} %id_ref.3, bf16[256,1024]{1,0:T(8,128)(2,1)} %tokens_ref.3, f32[256,1024]{1,0:T(8,128)} %copy-done.3, ...), custom_call_target="tpu_custom_call" | custom-call | tf_op jit(solution)/shard_map/close/pallas_call | solution.py:1175
  292.1 1.9 copy-done.1
  294.0 1.4 copy-done.2
  295.4 4.5 %unpack.1 = (f32[4,128,1024]{2,1,0:T(8,128)}, f32[4,128,1024]{2,1,0:T(8,128)}, f32[128,1024]{1,0:T(8,128)}, f32[128,1024]{1,0:T(8,128)}, f32[128,4096]{1,0:T(8,128)}, /*index=5*/f32[128,4096]{1,0:T(8,128)}) custom-call(bf16[8,128,1536]{2,1,0:T(8,128)(2,1)S(1)} %copy-done.1, bf16[8,128,768]{2,1,0:T(8,128)(2,1)S(1)} %copy-done.2), custom_call_target="tpu_custom_call" | custom-call | tf_op jit(solution)/shard_map/unpack/pallas_call | solution.py:1248
  300.0 1.0 copy.36
  (70 shorter events, 5.0 us)
Async XLA Ops:
  0.6 131.6 %copy-start = (bf16[8,16,4096]{2,1,0:T(8,128)(2,1)S(1)}, bf16[8,16,4096]{2,1,0:T(8,128)(2,1)}, u32[]{:S(2)}) copy-start(bf16[8,16,4096]{2,1,0:T(8,128)(2,1)} %param.41) | copy-start | bytes 3145732
  5.0 118.8 %copy-start.19 = (f32[1024]{0:T(1024)S(1)}, f32[1024]{0:T(1024)}, u32[]{:S(2)}) copy-start(f32[1024]{0:T(1024)} %param.27) | copy-start | bytes 12292
  123.8 4.8 %copy-start.6 = (bf16[256,1024]{1,0:T(8,128)(2,1)S(1)}, bf16[256,1024]{1,0:T(8,128)(2,1)}, u32[]{:S(2)}) copy-start(bf16[256,1024]{1,0:T(8,128)(2,1)} %tokens_ref.3) | copy-start | bytes 1572868
  123.8 5.4 %copy-start.13 = (f32[1024]{0:T(1024)S(1)}, f32[1024]{0:T(1024)}, u32[]{:S(2)}) copy-start(f32[1024]{0:T(1024)} %param.28) | copy-start | bytes 12292
  123.9 5.4 %copy-start.14 = (f32[1024]{0:T(1024)S(1)}, f32[1024]{0:T(1024)}, u32[]{:S(2)}) copy-start(f32[1024]{0:T(1024)} %param.29) | copy-start | bytes 12292
  123.9 6.0 %copy-start.17 = (bf16[1024,4096]{1,0:T(8,128)(2,1)S(1)}, bf16[1024,4096]{1,0:T(8,128)(2,1)}, u32[]{:S(2)}) copy-start(bf16[1024,4096]{1,0:T(8,128)(2,1)} %get-tuple-element.33) | copy-start | bytes 25165828
  126.5 3.1 %copy-start.12 = (bf16[8,1024,16]{1,2,0:T(8,128)(2,1)S(1)}, bf16[8,1024,16]{1,2,0:T(8,128)(2,1)}, u32[]{:S(2)}) copy-start(bf16[8,1024,16]{1,2,0:T(8,128)(2,1)} %param.40) | copy-start | bytes 786436
  126.5 3.4 %copy-start.18 = (f32[4096]{0:T(1024)S(1)}, f32[4096]{0:T(1024)}, u32[]{:S(2)}) copy-start(f32[4096]{0:T(1024)} %param.31) | copy-start | bytes 49156
  129.9 14.1 %slice-start = ((s8[8388608]{0:T(1024)(128)(4,1)}), s8[4194304]{0:T(1024)(128)(4,1)S(1)}, s32[]{:S(2)}) async-start(s8[8388608]{0:T(1024)(128)(4,1)} %bitcast.107), calls=%async_computation.1 | async-start | bytes 8388608
  132.3 11.0 %copy-start.9 = (bf16[8,4096,16]{1,2,0:T(8,128)(2,1)S(1)}, bf16[8,4096,16]{1,2,0:T(8,128)(2,1)}, u32[]{:S(2)}) copy-start(bf16[8,4096,16]{1,2,0:T(8,128)(2,1)} %param.42) | copy-start | bytes 3145732
  132.3 11.7 %slice-start.1 = ((s8[8388608]{0:T(1024)(128)(4,1)}), s8[4194304]{0:T(1024)(128)(4,1)S(1)}, s32[]{:S(2)}) async-start(s8[8388608]{0:T(1024)(128)(4,1)} %bitcast.107), calls=%async_computation.2 | async-start | bytes 8388608
  132.3 11.7 %copy-start.20 = (f32[1024]{0:T(1024)S(1)}, f32[1024]{0:T(1024)}, u32[]{:S(2)}) copy-start(f32[1024]{0:T(1024)} %param.33) | copy-start | bytes 12292
  143.3 3.1 %copy-start.5 = (bf16[256,4096]{1,0:T(8,128)(2,1)}, bf16[256,4096]{1,0:T(8,128)(2,1)S(1)}, u32[]{:S(2)}) copy-start(bf16[256,4096]{1,0:T(8,128)(2,1)S(1)} %get-tuple-element.60) | copy-start | bytes 6291460
  144.0 2.4 copy-start.10
  144.0 2.9 copy-start.8
  144.0 2.9 copy-start.15
  146.4 0.9 copy-start.16
  159.3 3.1 %copy-start.4 = (bf16[256,4096]{1,0:T(8,128)(2,1)}, bf16[256,4096]{1,0:T(8,128)(2,1)S(1)}, u32[]{:S(2)}) copy-start(bf16[256,4096]{1,0:T(8,128)(2,1)S(1)} %add_convert_fusion) | copy-start | bytes 6291460
  162.9 1.7 copy-start.7
  163.4 12.4 %copy-start.3 = (f32[256,1024]{1,0:T(8,128)}, f32[256,1024]{1,0:T(8,128)S(1)}, u32[]{:S(2)}) copy-start(f32[256,1024]{1,0:T(8,128)S(1)} %broadcast_add_fusion.first_ref) | copy-start | bytes 3145732
  166.5 15.4 %all-to-all-start = ((bf16[256,8,128]{2,0,1:T(8,128)(2,1)}), bf16[256,8,128]{2,0,1:T(8,128)(2,1)}, u32[]{:S(2)}, u32[]{:S(2)}) async-start(bf16[256,8,128]{2,0,1:T(8,128)(2,1)} %bitcast.99), calls=%async_computation | async-start | bytes 1048576 | tf_op jit(solution)/shard_map/all_to_all | solution.py:1427
  292.1 1.9 copy-start.1
  294.0 1.4 copy-start.2
  295.4 4.5 %copy-start.11 = (f32[256,1024]{1,0:T(8,128)S(1)}, f32[256,1024]{1,0:T(8,128)}, u32[]{:S(2)}) copy-start(f32[256,1024]{1,0:T(8,128)} %get-tuple-element.81) | copy-start | bytes 3145732

commit v4 on v2

--- a/solution.py
+++ b/solution.py
@@ -178,36 +178,69 @@
     pl.semaphore_wait(barrier, geo.seq + geo.wt - 2)
 
 
-def forward_kernel(
-    geo,
-    weight_count,
-    rank,
-    len_ref,
-    id_ref,
-    tokens_ref,
-    wqkv_ref,
-    down_ref,
-    up_ref,
-    bias_ref,
-    *refs,
-):
-    weights_in = refs[:weight_count]
-    att_ref, q_ref, k_ref, v_ref, o_ref, lse_ref, slice_ref, small_ref = refs[weight_count : weight_count + 8]
-    weights_out = refs[weight_count + 8 : 2 * weight_count + 8]
-    (
-        tok_buf,
-        seg_buf,
-        att_buf,
-        local_sem,
-        send_sem,
-        recv_sem,
-        slice_send,
-        slice_recv,
-        line_send,
-        line_recv,
-        att_send,
-        att_recv,
-    ) = refs[2 * weight_count + 8 :]
+def erf(v):
+    v = jnp.clip(v, -3.832506856900711, 3.832506856900711)
+    sq = v * v
+    top = jnp.full_like(v, 0.00022905065861350646)
+    for c in (0.0034082910107109506, 0.050955695062380861, 0.18520832239976145, 1.128379143519084):
+        top = top * sq + c
+    low = jnp.full_like(v, -1.1791602954361697e-7)
+    for c in (0.000023547966471313185, 0.0010179625278914885, 0.014070470171167667, 0.11098505178285362, 0.49746925110067538, 1.0):
+        low = low * sq + c
+    return v * top / low
+
+
+def normed(value):
+    mean = jnp.mean(value, axis=1, keepdims=True)
+    centred = value - mean
+    spread = lax.rsqrt(jnp.mean(centred * centred, axis=1, keepdims=True) + 1e-05)
+    return centred * spread, spread
+
+
+def normed_back(grad, gain, unit, spread):
+    g = grad * gain
+    return spread * (
+        g - jnp.mean(g, axis=1, keepdims=True) - unit * jnp.mean(g * unit, axis=1, keepdims=True)
+    )
+
+
+class Names:
+    def __init__(self, names, refs):
+        self.__dict__.update(zip(names, refs))
+
+
+MLP_INPUTS = (
+    "w_out", "w_fc1", "w_fc2", "cotangent", "out_bias", "gain1", "shift1", "fc1_bias", "fc2_bias", "gain2", "shift2",
+    "fc1_down", "fc1_up", "fc2_down", "fc2_up",
+)
+BASE_OUTPUTS = ("q", "k", "v", "o", "lse", "w_slice", "small")
+MLP_OUTPUTS = (
+    "output", "d_first", "d_heads", "g_out_down", "g_out_up", "g_fc1_down", "g_fc2_up", "g_fc1_up", "g_fc2_down",
+)
+BASE_SCRATCH = (
+    "tok", "seg", "att_send_buf", "local_sem", "send_sem", "recv_sem", "slice_send", "slice_recv", "line_send",
+    "line_recv", "att_send", "att_recv",
+)
+MLP_SCRATCH = (
+    "att", "full_out", "full_fc1", "full_fc2", "unit1", "h1", "h1_low", "act", "slope", "d_pre", "y", "d_att_buf",
+    "back_send", "back_recv",
+)
+
+
+def forward_kernel(geo, inside, rank, len_ref, id_ref, tokens_ref, wqkv_ref, down_ref, up_ref, bias_ref, *refs):
+    in_names = MLP_INPUTS if inside else ()
+    out_names = BASE_OUTPUTS + (MLP_OUTPUTS if inside else ("att",))
+    scratch_names = BASE_SCRATCH + (MLP_SCRATCH if inside else ())
+    r = Names(in_names + out_names + scratch_names, refs)
+    weights_in = (r.w_out, r.w_fc1, r.w_fc2) if inside else ()
+    weights_out = (r.full_out, r.full_fc1, r.full_fc2) if inside else ()
+    weight_count = len(weights_in)
+    att_ref, q_ref, k_ref, v_ref, o_ref, lse_ref, slice_ref, small_ref = (
+        r.att, r.q, r.k, r.v, r.o, r.lse, r.w_slice, r.small
+    )
+    tok_buf, seg_buf, att_buf, local_sem = r.tok, r.seg, r.att_send_buf, r.local_sem
+    send_sem, recv_sem, slice_send, slice_recv = r.send_sem, r.recv_sem, r.slice_send, r.slice_recv
+    line_send, line_recv, att_send, att_recv = r.line_send, r.line_recv, r.att_send, r.att_recv
     here = device_here(geo)
     x, y, core, w = here
     s = lax.axis_index("seq")
@@ -229,6 +262,7 @@
         height = weights_in[m].shape[0]
         dst = weights_out[m].at[pl.ds(pl.multiple_of(w * height, height), height)]
         own_weights.append(pltpu.make_async_copy(weights_in[m], dst, local_sem.at[4 + m]))
+        own_weights[-1].start()
 
     greet(geo)
 
@@ -270,9 +304,6 @@
     for d in range(1, wt):
         for j in range(3):
             slice_copy(j, d).start()
-    for copy in own_weights:
-        copy.start()
-
     starts, ends = doc_bounds(len_ref)
     seg_buf[...] = segment_from(lax.broadcasted_iota(jnp.int32, seg_buf.shape, 1), starts)
 
@@ -330,21 +361,31 @@
             def _():
                 line_copy(m, w, False, True).start()
 
+    def along(i):
+        if i >= len(units):
+            return
+        m, j = units[i]
+        p = nth_plane(j)
+        line_copy(m, p, True, False).wait_recv()
+
+        @pl.when((p < w) & (w < wt - 1))
+        def _():
+            line_copy(m, p, True, False).start()
+
+        @pl.when((p > w) & (w > 0))
+        def _():
+            line_copy(m, p, False, False).start()
+
+    ahead = 2
+
     def tick(i):
-        if 0 <= i < len(units):
+        if i == 0:
+            for n in range(ahead):
+                along(n)
+        along(i + ahead)
+        if i < len(units):
             m, j = units[i]
-            p = nth_plane(j)
-            line_copy(m, p, True, False).wait_recv()
-
-            @pl.when((p < w) & (w < wt - 1))
-            def _():
-                line_copy(m, p, True, False).start()
-
-            @pl.when((p > w) & (w > 0))
-            def _():
-                line_copy(m, p, False, False).start()
-
-            spread = weight_spread(m, p)
+            spread = weight_spread(m, nth_plane(j))
             spread.go(0)
             spread.go(1)
             spread.go(4)
@@ -367,6 +408,13 @@
 
     tick_count = len(units) + 2 if units else 0
 
+    def complete(m):
+        own_weights[m].wait()
+        for j in range(wt - 1):
+            spread = weight_spread(m, nth_plane(j))
+            for kind in range(4, 9):
+                spread.wait(kind)
+
     nx, ny = geo.nx, geo.ny
     row_n, col_n, diag_n = 2 * (nx - 1), 2 * (ny - 1), 2 * (nx - 1) * (ny - 1)
 
@@ -434,7 +482,7 @@
         pos = t * rows + lax.broadcasted_iota(jnp.int32, (rows, LANES), 0)
         chosen = select_from(pos, starts, ends, id_ref, rank)
         main = dot_nn(block, slice_ref[...])
-        small = dot_nt(block, down_ref[...])
+        small = dot_nt(block, down_ref[: 3 * LANES, :])
         for j in range(3):
             cut = slice(j * LANES, (j + 1) * LANES)
             low = (small[:, cut] * chosen).astype(BF16)
@@ -471,8 +519,8 @@
         )
 
     def attend(i, carry):
-        for n in range(min(tick_count, geo.groups)):
-            @pl.when(i == n)
+        for n in range(min(tick_count, geo.groups // 2)):
+            @pl.when(i == 2 * n + 1)
             def _():
                 tick(n)
 
@@ -523,29 +571,33 @@
     own_att = pltpu.make_async_copy(att_buf.at[g], att_ref.at[:, lanes], local_sem.at[0])
     own_att.start()
 
-    for n in range(geo.groups, tick_count):
-        tick(n)
+    def att_arrivals():
+        for d in range(1, geo.groups):
+            other = (g + d) % geo.groups
+            cut = pl.ds(pl.multiple_of(other * LANES, LANES), LANES)
+            pltpu.make_async_remote_copy(
+                src_ref=att_ref.at[:, cut],
+                dst_ref=att_ref.at[:, cut],
+                send_sem=att_send.at[other],
+                recv_sem=att_recv.at[other],
+                device_id=(part * geo.groups + other, w),
+                device_id_type=MESH,
+            ).wait_recv()
+        own_att.wait()
+
+    ticked = min(tick_count, geo.groups // 2)
+    if inside:
+        layer_rest(geo, rank, r, starts, ends, id_ref, down_ref, up_ref, att_arrivals, complete, tick, ticked, tick_count)
+    else:
+        att_arrivals()
 
     for d in range(1, geo.groups):
-        other = (g + d) % geo.groups
-        cut = pl.ds(pl.multiple_of(other * LANES, LANES), LANES)
-        pltpu.make_async_remote_copy(
-            src_ref=att_ref.at[:, cut],
-            dst_ref=att_ref.at[:, cut],
-            send_sem=att_send.at[other],
-            recv_sem=att_recv.at[other],
-            device_id=(part * geo.groups + other, w),
-            device_id_type=MESH,
-        ).wait_recv()
-        att_copy(other).wait_send()
-    own_att.wait()
+        att_copy((g + d) % geo.groups).wait_send()
     tok.wait_sends()
     for d in range(1, wt):
         for j in range(3):
             slice_copy(j, d).wait_send()
     for m in range(weight_count):
-        own_weights[m].wait()
-
         @pl.when(w < wt - 1)
         def _():
             line_copy(m, w, True, True).wait_send()
@@ -565,55 +617,247 @@
         def _():
             line_copy(m, p, False, False).wait_send()
 
-        spread = weight_spread(m, p)
-        for kind in range(4, 9):
-            spread.wait(kind)
-        spread.wait_sends()
-
-
-def forward_attention(geo, rank, lengths, ids, tokens, w_qkv, down, up, bias, weights):
+        weight_spread(m, p).wait_sends()
+
+
+def layer_rest(geo, rank, r, starts, ends, id_ref, down_ref, up_ref, att_arrivals, complete, tick, ticked, tick_count):
+    s, w = lax.axis_index("seq"), lax.axis_index("wt")
+    rows, width, groups = geo.rows, geo.width, geo.groups
+    part, g = s // groups, s % groups
+    hidden = r.full_fc1.shape[1]
+    step = min(512, hidden)
+    steps = hidden // step
+    band = 2 * LANES
+    bands = width // band
+    lane_count = r.fc1_down.shape[0]
+    out_rows = slice(3 * lane_count, 4 * lane_count)
+    pos = s * rows + lax.broadcasted_iota(jnp.int32, (rows, LANES), 0)
+    chosen = select_from(pos, starts, ends, id_ref, rank)
+
+    def masked(value):
+        return (value * chosen).astype(BF16)
+
+    def at_step(i):
+        return pl.ds(pl.multiple_of(i * step, step), step)
+
+    def at_band(i):
+        return pl.ds(pl.multiple_of(i * band, band), band)
+
+    pending = list(range(ticked, tick_count))
+    first_ticks, pending = pending[:1], pending[1:]
+    for n in first_ticks:
+        tick(n)
+    att_arrivals()
+    complete(0)
+    att = r.att[...]
+    small_out = masked(dot_nt(att, down_ref[out_rows, :]))
+
+    def out_band(i, carry):
+        cut = at_band(i)
+        value = dot_nn(r.att[...], r.full_out[:, cut]) + r.out_bias[:, cut]
+        value = value + dot_nn(small_out, up_ref[out_rows, cut])
+        r.y[:, cut] = value + r.tok[s, :, cut].astype(F32)
+        return carry
+
+    lax.fori_loop(0, bands, out_band, 0)
+    unit1, spread1 = normed(r.y[...])
+    h1 = unit1 * r.gain1[...] + r.shift1[...]
+    r.unit1[...] = unit1
+    r.h1[...] = h1
+    h1_low = h1.astype(BF16)
+    r.h1_low[...] = h1_low
+    small_fc1 = masked(dot_nt(h1_low, r.fc1_down[...]))
+
+    middle = max(len(pending) - 3, 0)
+    for n in pending[:middle]:
+        tick(n)
+    pending = pending[middle:]
+    complete(1)
+
+    def fc1_step(i, acc):
+        for n, t in enumerate(pending):
+            @pl.when(i == min(2 * n + 1, steps - 1))
+            def _():
+                tick(t)
+
+        cut = at_step(i)
+        pre = dot_nn(r.h1_low[...], r.full_fc1[:, cut]) + r.fc1_bias[:, cut]
+        pre = pre + dot_nn(small_fc1, r.fc1_up[:, cut])
+        share = 0.5 + 0.5 * erf(pre * 0.7071067811865476)
+        act = (pre * share).astype(BF16)
+        r.act[:, cut] = act
+        r.slope[:, cut] = share + pre * (jnp.exp(-0.5 * pre * pre) * 0.3989422804014327)
+        return acc + dot_nt(act, r.fc2_down[:, cut])
+
+    small_fc2 = masked(lax.fori_loop(0, steps, fc1_step, jnp.zeros((rows, lane_count), F32)))
+    complete(2)
+
+    def fc2_band(i, carry):
+        cut = at_band(i)
+        value = dot_nn(r.act[...], r.full_fc2[:, cut]) + r.fc2_bias[:, cut]
+        r.y[:, cut] = value + dot_nn(small_fc2, r.fc2_up[:, cut]) + r.h1[:, cut]
+        return carry
+
+    lax.fori_loop(0, bands, fc2_band, 0)
+    unit2, spread2 = normed(r.y[...])
+    r.output[...] = unit2 * r.gain2[...] + r.shift2[...]
+    d_second = normed_back(r.cotangent[...].astype(F32), r.gain2[...], unit2, spread2)
+    r.y[...] = d_second
+    d_y = d_second.astype(BF16)
+    low_fc2 = masked(dot_nt(d_y, r.fc2_up[...]))
+    r.g_fc2_up[...] = dot_tn(small_fc2, d_y).astype(BF16)
+
+    def back_step(i, acc):
+        cut = at_step(i)
+        d_act = dot_nt(d_y, r.full_fc2[cut, :]) + dot_nn(low_fc2, r.fc2_down[:, cut])
+        d_pre = (d_act * r.slope[:, cut]).astype(BF16)
+        r.d_pre[:, cut] = d_pre
+        r.g_fc2_down[:, cut] = dot_tn(low_fc2, r.act[:, cut]).astype(BF16)
+        r.g_fc1_up[:, cut] = dot_tn(small_fc1, d_pre).astype(BF16)
+        return acc + dot_nt(d_pre, r.fc1_up[:, cut])
+
+    low_fc1 = masked(lax.fori_loop(0, steps, back_step, jnp.zeros((rows, lane_count), F32)))
+    r.g_fc1_down[...] = dot_tn(low_fc1, r.h1_low[...]).astype(BF16)
+
+    def back_band(i, carry):
+        cut = at_band(i)
+        value = dot_nt(r.d_pre[...], r.full_fc1[cut, :]) + dot_nn(low_fc1, r.fc1_down[:, cut])
+        r.y[:, cut] += value
+        return carry
+
+    lax.fori_loop(0, bands, back_band, 0)
+    d_first = normed_back(r.y[...], r.gain1[...], r.unit1[...], spread1)
+    r.d_first[...] = d_first
+    d_z = d_first.astype(BF16)
+    low_out = masked(dot_nt(d_z, up_ref[out_rows, :]))
+
+    def back_copy(b):
+        return pltpu.make_async_remote_copy(
+            src_ref=r.d_att_buf.at[b],
+            dst_ref=r.d_heads.at[pl.ds(pl.multiple_of(g * rows, rows), rows)],
+            send_sem=r.back_send.at[b],
+            recv_sem=r.back_recv.at[g],
+            device_id=(part * groups + b, w),
+            device_id_type=MESH,
+        )
+
+    def attended_band(i, carry):
+        n = (g // 2 + 1 + i) % bands
+        cut = at_band(n)
+        value = dot_nt(d_z, r.full_out[cut, :]) + dot_nn(low_out, down_ref[out_rows, cut])
+        value = value.astype(BF16)
+        for h in range(2):
+            b = 2 * n + h
+            r.d_att_buf[b] = value[:, h * LANES : (h + 1) * LANES]
+
+            @pl.when(b != g)
+            def _():
+                back_copy(b).start()
+
+        return carry
+
+    lax.fori_loop(0, bands, attended_band, 0)
+    own = pltpu.make_async_copy(
+        r.d_att_buf.at[g], r.d_heads.at[pl.ds(pl.multiple_of(g * rows, rows), rows)], r.local_sem.at[0]
+    )
+    own.start()
+    r.g_out_down[...] = dot_tn(low_out, r.att[...]).astype(BF16)
+    r.g_out_up[...] = dot_tn(small_out, d_z).astype(BF16)
+    for d in range(1, groups):
+        other = (g + d) % groups
+        here = r.d_heads.at[pl.ds(pl.multiple_of(other * rows, rows), rows)]
+        pltpu.make_async_remote_copy(
+            src_ref=here,
+            dst_ref=here,
+            send_sem=r.back_send.at[other],
+            recv_sem=r.back_recv.at[other],
+            device_id=(part * groups + other, w),
+            device_id_type=MESH,
+        ).wait_recv()
+        back_copy(other).wait_send()
+    own.wait()
+
+
+def forward_attention(geo, rank, lengths, ids, tokens, w_qkv, down, up, bias, mlp):
     rows, width = geo.rows, geo.width
-    count = len(weights)
+    inside = mlp is not None
+    mlp = mlp or ()
     any_spec = pl.BlockSpec(memory_space=pl.ANY)
     vmem = pl.BlockSpec(memory_space=pltpu.VMEM)
     smem = pl.BlockSpec(memory_space=pltpu.SMEM)
+    lane_count = down.shape[0] // 4
+    struct = jax.ShapeDtypeStruct
     shapes = [
-        jax.ShapeDtypeStruct((rows, width), BF16),
-        jax.ShapeDtypeStruct((geo.queries, LANES), BF16),
-        jax.ShapeDtypeStruct((geo.keys, LANES), BF16),
-        jax.ShapeDtypeStruct((geo.keys, LANES), BF16),
-        jax.ShapeDtypeStruct((geo.queries, LANES), F32),
-        jax.ShapeDtypeStruct((geo.queries, LANES), F32),
-        jax.ShapeDtypeStruct((width, 3 * LANES), BF16),
-        jax.ShapeDtypeStruct((geo.keys, 3 * LANES), BF16),
-    ] + [jax.ShapeDtypeStruct((v.shape[0] * geo.wt, v.shape[1]), BF16) for v in weights]
+        struct((geo.queries, LANES), BF16),
+        struct((geo.keys, LANES), BF16),
+        struct((geo.keys, LANES), BF16),
+        struct((geo.queries, LANES), F32),
+        struct((geo.queries, LANES), F32),
+        struct((width, 3 * LANES), BF16),
+        struct((geo.keys, 3 * LANES), BF16),
+    ]
+    specs = [vmem] * 7
+    dma = pltpu.SemaphoreType.DMA
+    count = 3 if inside else 0
     units = 1 + count * geo.wt
-    dma = pltpu.SemaphoreType.DMA
-    results = pl.pallas_call(
-        functools.partial(forward_kernel, geo, count, rank),
-        out_shape=shapes,
-        in_specs=[smem, smem, any_spec, any_spec, vmem, vmem, vmem] + [any_spec] * count,
-        out_specs=[any_spec] + [vmem] * 7 + [any_spec] * count,
-        scratch_shapes=[
-            pltpu.VMEM((geo.seq, rows, width), BF16),
-            pltpu.VMEM((1, geo.keys), jnp.int32),
+    scratch = [
+        pltpu.VMEM((geo.seq, rows, width), BF16),
+        pltpu.VMEM((1, geo.keys), jnp.int32),
+        pltpu.VMEM((geo.groups, rows, LANES), BF16),
+        dma((4 + count,)),
+        dma((Spread.KINDS, units)),
+        dma((Spread.KINDS, units)),
+        dma((3, geo.wt)),
+        dma((3, geo.wt)),
+        dma((2, max(count, 1) * geo.wt)),
+        dma((max(count, 1) * geo.wt,)),
+        dma((geo.groups,)),
+        dma((geo.groups,)),
+    ]
+    if inside:
+        hidden = mlp[1].shape[1]
+        shapes += [
+            struct((rows, width), F32),
+            struct((rows, width), F32),
+            struct((geo.queries, LANES), BF16),
+            struct((lane_count, width), BF16),
+            struct((lane_count, width), BF16),
+            struct((lane_count, width), BF16),
+            struct((lane_count, width), BF16),
+            struct((lane_count, hidden), BF16),
+            struct((lane_count, hidden), BF16),
+        ]
+        specs += [vmem, vmem, any_spec] + [vmem] * 6
+        scratch += [
+            pltpu.VMEM((rows, width), BF16),
+            pltpu.VMEM((width, width), BF16),
+            pltpu.VMEM((width, hidden), BF16),
+            pltpu.VMEM((hidden, width), BF16),
+            pltpu.VMEM((rows, width), F32),
+            pltpu.VMEM((rows, width), F32),
+            pltpu.VMEM((rows, width), BF16),
+            pltpu.VMEM((rows, hidden), BF16),
+            pltpu.VMEM((rows, hidden), F32),
+            pltpu.VMEM((rows, hidden), BF16),
+            pltpu.VMEM((rows, width), F32),
             pltpu.VMEM((geo.groups, rows, LANES), BF16),
-            dma((4 + count,)),
-            dma((Spread.KINDS, units)),
-            dma((Spread.KINDS, units)),
-            dma((3, geo.wt)),
-            dma((3, geo.wt)),
-            dma((2, max(count, 1) * geo.wt)),
-            dma((max(count, 1) * geo.wt,)),
             dma((geo.groups,)),
             dma((geo.groups,)),
-        ],
+        ]
+    else:
+        shapes += [struct((rows, width), BF16)]
+        specs += [any_spec]
+    return pl.pallas_call(
+        functools.partial(forward_kernel, geo, inside, rank),
+        out_shape=shapes,
+        in_specs=[smem, smem, any_spec, any_spec, vmem, vmem, vmem] + [any_spec] * count + [vmem] * (len(mlp) - count),
+        out_specs=specs,
+        scratch_shapes=scratch,
         compiler_params=pltpu.CompilerParams(
             collective_id=0, has_side_effects=True, vmem_limit_bytes=VMEM_LIMIT
         ),
-        name="gather_attend",
-    )(lengths, ids, tokens, w_qkv, down, up, bias, *weights)
-    return results[:8], results[8:]
+        name="layer",
+    )(lengths, ids, tokens, w_qkv, down, up, bias, *mlp)
 
 
 def backward_kernel(geo, len_ref, part_ref, q_ref, k_ref, v_ref, o_ref, lse_ref, g_ref, dq_ref, dk_ref, dv_ref, dk_acc, dv_acc):
@@ -881,7 +1125,7 @@
     part, g = s // groups, s % groups
     docs = len_ref.shape[1]
     doc_rows = docs * rank
-    lane_count = down_ref.shape[0] // 3
+    lane_count = down_ref.shape[0] // 4
     lanes = pl.ds(pl.multiple_of(g * LANES, LANES), LANES)
     starts, ends = doc_bounds(len_ref)
     ids = [id_ref[0, d] for d in range(docs)]
@@ -1153,7 +1397,7 @@
     rows, width = geo.rows, geo.width
     docs = lengths.shape[1]
     doc_rows = docs * rank
-    lane_count = down.shape[0] // 3
+    lane_count = down.shape[0] // 4
     set1 = sum(v.shape[1] for v in grads) // geo.groups
     set2 = 6 * LANES
     chips, near = geo.seq // 2, geo.groups // 2
@@ -1293,76 +1537,25 @@
     return jnp.sum((positions[:, None] >= starts[None, :]).astype(jnp.int32), axis=1) - 1
 
 
-def shards(
-    tokens,
-    cotangent,
-    w_qkv,
-    qv_bias,
-    w_out,
-    out_bias,
-    norm1_gain,
-    norm1_bias,
-    w_fc1,
-    fc1_bias,
-    w_fc2,
-    fc2_bias,
-    norm2_gain,
-    norm2_bias,
-    doc_lengths,
-    adapter_ids,
-    attn_down,
-    attn_up,
-    fc1_down,
-    fc1_up,
-    fc2_down,
-    fc2_up,
+def select_local(tok_rows, lane_count, rank_size, lengths, ids):
+    starts = jnp.cumsum(lengths) - lengths
+    local_pos = lax.axis_index("seq") * tok_rows + jnp.arange(tok_rows, dtype=jnp.int32)
+    local_seg = segment_of(local_pos, starts)
+    doc_range = jnp.arange(lengths.shape[0], dtype=jnp.int32)
+    chosen = jnp.sum(jnp.where(local_seg[:, None] == doc_range[None, :], ids[None, :], 0), axis=1)
+    lane_owner = jnp.arange(lane_count, dtype=jnp.int32) // rank_size
+    return (chosen[:, None] == lane_owner[None, :]).astype(jnp.float32)
+
+
+def feed_forward(
+    geo, tokens, cotangent, attended_tok, weights, vectors, attn_maps, fc1_maps, fc2_maps, select
 ):
     tok_rows, model_width = tokens.shape
-    adapter_count = attn_down.shape[1]
-    rank_size = attn_down.shape[3]
-    lane_count = adapter_count * rank_size
-    seq_count = lax.axis_size("seq")
-    geo = Geometry(tok_rows, model_width)
-    seq_index = lax.axis_index("seq")
-    part_index = seq_index // geo.groups
-    head_index = seq_index % geo.groups
-    lengths = doc_lengths[0]
-    starts = jnp.cumsum(lengths) - lengths
-    local_pos = seq_index * tok_rows + jnp.arange(tok_rows, dtype=jnp.int32)
-    local_seg = segment_of(local_pos, starts)
-    doc_range = jnp.arange(lengths.shape[0], dtype=jnp.int32)
-    chosen = jnp.sum(
-        jnp.where(local_seg[:, None] == doc_range[None, :], adapter_ids[0][None, :], 0), axis=1
-    )
-    lane_owner = jnp.arange(lane_count, dtype=jnp.int32) // rank_size
-    select = (chosen[:, None] == lane_owner[None, :]).astype(jnp.float32)
-    out_down = stack_down(attn_down[3])
-    out_up = stack_up(attn_up[3])
-    fc1_down_all = stack_down(fc1_down)
-    fc1_up_all = stack_up(fc1_up)
-    fc2_down_all = stack_down(fc2_down)
-    fc2_up_all = stack_up(fc2_up)
-    down_rows = jnp.transpose(attn_down, (0, 1, 3, 2)).reshape(4 * lane_count, model_width)
-    up_rows = attn_up.reshape(4 * lane_count, model_width)
-    weights = (w_out, w_fc1, w_fc2)
-    inside = [v.shape[0] % (32 * seq_count) == 0 for v in weights]
-    (attended_tok, q_heads, k_heads, v_heads, o_heads, lse_heads, w_slice, small_all), gathered = forward_attention(
-        geo,
-        rank_size,
-        doc_lengths,
-        adapter_ids,
-        tokens,
-        w_qkv,
-        down_rows[: 3 * lane_count],
-        up_rows[: 3 * lane_count],
-        qv_bias,
-        [v for v, here in zip(weights, inside) if here],
-    )
-    gathered = list(gathered)
-    full_out, full_fc1, full_fc2 = [
-        gathered.pop(0) if here else lax.all_gather(v, "wt", axis=0, tiled=True)
-        for v, here in zip(weights, inside)
-    ]
+    full_out, full_fc1, full_fc2 = [lax.all_gather(v, "wt", axis=0, tiled=True) for v in weights]
+    out_bias, norm1_gain, norm1_bias, fc1_bias, fc2_bias, norm2_gain, norm2_bias = vectors
+    out_down, out_up = attn_maps
+    fc1_down_all, fc1_up_all = fc1_maps
+    fc2_down_all, fc2_up_all = fc2_maps
     out_main = jnp.dot(attended_tok, full_out, preferred_element_type=jnp.float32)
     small_out = (
         jnp.dot(attended_tok, out_down, preferred_element_type=jnp.float32) * select
@@ -1423,12 +1616,79 @@
         axis_index_groups=blocks,
         tiled=True,
     ).reshape(geo.queries, LANES)
+    grads = [grad_out_down, grad_out_up, grad_fc1_down, grad_fc2_up, grad_fc1_up, grad_fc2_down]
+    return output, d_first, d_heads, [v.astype(BF16) for v in grads]
+
+
+def shards(
+    tokens,
+    cotangent,
+    w_qkv,
+    qv_bias,
+    w_out,
+    out_bias,
+    norm1_gain,
+    norm1_bias,
+    w_fc1,
+    fc1_bias,
+    w_fc2,
+    fc2_bias,
+    norm2_gain,
+    norm2_bias,
+    doc_lengths,
+    adapter_ids,
+    attn_down,
+    attn_up,
+    fc1_down,
+    fc1_up,
+    fc2_down,
+    fc2_up,
+):
+    tok_rows, model_width = tokens.shape
+    adapter_count = attn_down.shape[1]
+    rank_size = attn_down.shape[3]
+    lane_count = adapter_count * rank_size
+    seq_count = lax.axis_size("seq")
+    geo = Geometry(tok_rows, model_width)
+    part_index = lax.axis_index("seq") // geo.groups
+    down_rows = jnp.transpose(attn_down, (0, 1, 3, 2)).reshape(4 * lane_count, model_width)
+    up_rows = attn_up.reshape(4 * lane_count, model_width)
+    weights = (w_out, w_fc1, w_fc2)
+    vectors = (out_bias, norm1_gain, norm1_bias, fc1_bias, fc2_bias, norm2_gain, norm2_bias)
+
+    def rows_of(down):
+        return jnp.swapaxes(down, 1, 2).reshape(lane_count, down.shape[1])
+
+    inside = all(v.shape[0] % (32 * seq_count) == 0 for v in weights)
+    mlp = None
+    if inside:
+        mlp = (
+            weights
+            + (cotangent,)
+            + tuple(v.reshape(1, -1) for v in vectors)
+            + (rows_of(fc1_down), stack_up(fc1_up), rows_of(fc2_down), stack_up(fc2_up))
+        )
+    q_heads, k_heads, v_heads, o_heads, lse_heads, w_slice, small_all, *rest = forward_attention(
+        geo, rank_size, doc_lengths, adapter_ids, tokens, w_qkv, down_rows, up_rows, qv_bias, mlp
+    )
+    if inside:
+        output, d_first, d_heads, *set1 = rest
+    else:
+        output, d_first, d_heads, set1 = feed_forward(
+            geo,
+            tokens,
+            cotangent,
+            rest[0],
+            weights,
+            vectors,
+            (stack_down(attn_down[3]), stack_up(attn_up[3])),
+            (stack_down(fc1_down), stack_up(fc1_up)),
+            (stack_down(fc2_down), stack_up(fc2_up)),
+            select_local(tok_rows, lane_count, rank_size, doc_lengths[0], adapter_ids[0]),
+        )
     d_q, d_k, d_v = backward_attention(
         geo, doc_lengths, part_index.reshape(1, 1), q_heads, k_heads, v_heads, o_heads, lse_heads, d_heads
     )
-    set1 = [
-        v.astype(BF16) for v in (grad_out_down, grad_out_up, grad_fc1_down, grad_fc2_up, grad_fc1_up, grad_fc2_down)
-    ]
     input_grad, sum1, sum2, _ = closing(
         geo,
         rank_size,
@@ -1440,8 +1700,8 @@
         d_k,
         d_v,
         w_slice,
-        down_rows[: 3 * lane_count],
-        up_rows[: 3 * lane_count],
+        down_rows,
+        up_rows,
         small_all,
         set1,
     )

time: 348 us -> 279 us (0.80)
  matrix products: 48.5 us -> 0 us
  local copies, waits for them, and re-layouts: 12.4 us -> 5.86 us
  Pallas kernels: 277 us -> 272 us
  starting transfers between devices: 4.51 us -> 0 us
    dot_general x24 -> x0, matrix products: 48.5 us -> none  [the longest x9 15.3 us: times_transposed(): lax.dot_general(grad, weight, (((1,), (1,)), ((), ())), preferred_element...]
    slice x4 -> x0, local copies, waits for them, and re-layouts: 6.32 us -> none  [the longest x1 2.2 us: shards(): up_rows[:3 * lane_count]]
    pallas_call x1, Pallas kernels: 156 us -> 152 us  [forward_attention(): pl.pallas_call(functools.partial(forward_kernel, geo, inside, rank), out_...]
    all_to_all x1 -> x0, starting transfers between devices: 4.51 us -> none  [shards(): lax.all_to_all(d_attended.reshape(tok_rows, geo.groups, LANES), 'seq', sp...]
  transfers between devices with their start and end apart: 1 -> 0, of which waited for: 0 -> 0; matrix products, arithmetic and copies ran while one was open for 3% -> 0% of each run, Pallas kernels for 0% -> 0%
where the time goes in v4:
time: 279 us
  Pallas kernels  272 us (97%)
  local copies, waits for them, and re-layouts  5.86 us (2%)
    pallas_call x1, Pallas kernels, forward_attention(): pl.pallas_call(functools.partial(forward_kernel, geo, inside, rank), out_...  152 us
    pallas_call x1, Pallas kernels, closing(): pl.pallas_call(functools.partial(closing_kernel, geo, rank), out_shape=[j...  84.3 us
    pallas_call x1, Pallas kernels, backward_attention(): pl.pallas_call(functools.partial(backward_kernel, geo), out_shape=[jax.Sh...  32 us
    unnamed x10, local copies, waits for them, and re-layouts  5.86 us

profile of v4, /device:TPU:0, one launch (start us, length us, event | category | flops | bytes accessed | tf_op | source)
XLA Modules:
  0.0 279.0 jit_solution(16510076033469829141)
XLA Ops:
  0.7 151.6 %layer.1 = (bf16[2048,128]{1,0:T(8,128)(2,1)}, bf16[2048,128]{1,0:T(8,128)(2,1)}, bf16[2048,128]{1,0:T(8,128)(2,1)}, f32[2048,128]{1,0:T(8,128)}, f32[2048,128]{...) custom-call(s32[1,4]{1,0:T(1,128)} %len_ref.5, ...), custom_call_target="tpu_custom_call" | custom-call | tf_op jit(solution)/shard_map/layer/pallas_call | solution.py:850
  152.2 32.0 %attend_back.1 = (bf16[2048,128]{1,0:T(8,128)(2,1)}, bf16[2048,128]{1,0:T(8,128)(2,1)}, bf16[2048,128]{1,0:T(8,128)(2,1)}) custom-call(s32[1,4]{1,0:T(1,128)} %len_ref.5, s32[1,1]{1,0:T(1,128)} %bitcast.16.part_ref, bf16[2048,128]{1,0:T(8,128)(2,1)} %get-tuple-element.38.q_ref, bf16[2048,128]{1,0:T(8,128)(2,1)} %get-tuple-element.39.k_ref, ...), custom_call_target="tpu_custom_call" | custom-call | tf_op jit(solution)/shard_map/attend_back/pallas_call | solution.py:941
  184.2 84.3 %close.1 = (f32[256,1024]{1,0:T(8,128)}, bf16[8,128,1536]{2,1,0:T(8,128)(2,1)}, bf16[8,128,768]{2,1,0:T(8,128)(2,1)}, bf16[4,256,1152]{2,1,0:T(8,128)(2,1)}) custom-call(s32[1,4]{1,0:T(1,128)} %len_ref.5, s32[1,4]{1,0:T(1,128)} %id_ref.3, bf16[256,1024]{1,0:T(8,128)(2,1)} %tokens_ref.3, f32[256,1024]{1,0:T(8,128)} %get-tuple-element.37.first_ref, ...), custom_call_target="tpu_custom_call" | custom-call | tf_op jit(solution)/shard_map/close/pallas_call | solution.py:1410
  268.6 0.0 copy-start
  268.6 1.9 copy-done
  270.4 0.0 copy-start.1
  270.5 1.4 copy-done.1
  271.9 0.0 copy-start.2
  271.9 4.5 %unpack.1 = (f32[4,128,1024]{2,1,0:T(8,128)}, f32[4,128,1024]{2,1,0:T(8,128)}, f32[128,1024]{1,0:T(8,128)}, f32[128,1024]{1,0:T(8,128)}, f32[128,4096]{1,0:T(8,128)}, /*index=5*/f32[128,4096]{1,0:T(8,128)}) custom-call(bf16[8,128,1536]{2,1,0:T(8,128)(2,1)S(1)} %copy-done, bf16[8,128,768]{2,1,0:T(8,128)(2,1)S(1)} %copy-done.1), custom_call_target="tpu_custom_call" | custom-call | tf_op jit(solution)/shard_map/unpack/pallas_call | solution.py:1483
  276.4 0.0 copy-start.3
  276.4 0.0 copy-done.2
  276.4 1.0 copy.32
  277.4 0.6 copy-done.3
  278.0 1.0 copy.33
Async XLA Ops:
  268.6 1.9 copy-start
  270.4 1.4 copy-start.1
  271.9 4.5 %copy-start.2 = (f32[256,1024]{1,0:T(8,128)S(1)}, f32[256,1024]{1,0:T(8,128)}, u32[]{:S(2)}) copy-start(f32[256,1024]{1,0:T(8,128)} %get-tuple-element.72) | copy-start | bytes 3145732
  276.4 1.6 copy-start.3

commit v5 on v4

--- a/solution.py
+++ b/solution.py
@@ -277,33 +277,17 @@
     tok.go(1, own=tokens_ref)
     tok.go(4, own=tokens_ref)
 
-    def slice_copy(j, d):
-        src = wqkv_ref.at[:, pl.ds(pl.multiple_of(j * width + g * LANES, LANES), LANES)]
-        dst = slice_ref.at[pl.ds(pl.multiple_of(w * shard, shard), shard), pl.ds(j * LANES, LANES)]
-        return pltpu.make_async_remote_copy(
-            src_ref=src,
-            dst_ref=dst,
-            send_sem=slice_send.at[j, d],
-            recv_sem=slice_recv.at[j, d],
-            device_id=(s, (w + d) % wt),
-            device_id_type=MESH,
-        )
-
-    def slice_arrival(j, d):
-        origin = (w + wt - d) % wt
-        dst = slice_ref.at[pl.ds(pl.multiple_of(origin * shard, shard), shard), pl.ds(j * LANES, LANES)]
+    def slice_copy(j, p, up):
+        dst = slice_ref.at[pl.ds(pl.multiple_of(p * shard, shard), shard), pl.ds(j * LANES, LANES)]
         return pltpu.make_async_remote_copy(
             src_ref=dst,
             dst_ref=dst,
-            send_sem=slice_send.at[j, d],
-            recv_sem=slice_recv.at[j, d],
-            device_id=(s, origin),
+            send_sem=slice_send.at[0 if up else 1, j, p],
+            recv_sem=slice_recv.at[j, p],
+            device_id=(s, w + 1 if up else w - 1),
             device_id_type=MESH,
         )
 
-    for d in range(1, wt):
-        for j in range(3):
-            slice_copy(j, d).start()
     starts, ends = doc_bounds(len_ref)
     seg_buf[...] = segment_from(lax.broadcasted_iota(jnp.int32, seg_buf.shape, 1), starts)
 
@@ -349,10 +333,13 @@
 
         return Spread(geo, here, region, send_sem, recv_sem, 1 + m * wt + p)
 
-    units = [(m, j) for m in range(weight_count) for j in range(wt - 1)]
-
-    def start_lines():
-        for m in range(weight_count):
+    units = []
+    if inside:
+        units = [(m, j) for j in range(wt - 1) for m in (0, 1)] + [(2, j) for j in range(wt - 1)]
+
+    def start_lines(which):
+        for m in which if inside else ():
+
             @pl.when(w < wt - 1)
             def _():
                 line_copy(m, w, True, True).start()
@@ -376,19 +363,18 @@
         def _():
             line_copy(m, p, False, False).start()
 
-    ahead = 2
-
     def tick(i):
         if i == 0:
-            for n in range(ahead):
-                along(n)
-        along(i + ahead)
+            along(0)
+        if i == late_lines:
+            start_lines((2,))
         if i < len(units):
             m, j = units[i]
             spread = weight_spread(m, nth_plane(j))
             spread.go(0)
             spread.go(1)
             spread.go(4)
+        along(i + 1)
         if 0 <= i - 1 < len(units):
             m, j = units[i - 1]
             spread = weight_spread(m, nth_plane(j))
@@ -407,6 +393,9 @@
             spread.go(8)
 
     tick_count = len(units) + 2 if units else 0
+    late_lines = 0
+    early_ticks = min(3, tick_count)
+    loop_ticks = min(6, tick_count)
 
     def complete(m):
         own_weights[m].wait()
@@ -414,6 +403,18 @@
             spread = weight_spread(m, nth_plane(j))
             for kind in range(4, 9):
                 spread.wait(kind)
+
+    for copy in own_slices:
+        copy.wait()
+    for j in range(3):
+
+        @pl.when(w < wt - 1)
+        def _():
+            slice_copy(j, w, True).start()
+
+        @pl.when(w > 0)
+        def _():
+            slice_copy(j, w, False).start()
 
     nx, ny = geo.nx, geo.ny
     row_n, col_n, diag_n = 2 * (nx - 1), 2 * (ny - 1), 2 * (nx - 1) * (ny - 1)
@@ -435,13 +436,21 @@
     def project(i, carry):
         @pl.when(i == 0)
         def _():
+            start_lines((0, 1))
+            for n in range(wt - 1):
+                p = nth_plane(n)
+                for j in range(3):
+                    slice_copy(j, p, True).wait_recv()
+
+                    @pl.when((p < w) & (w < wt - 1))
+                    def _():
+                        slice_copy(j, p, True).start()
+
+                    @pl.when((p > w) & (w > 0))
+                    def _():
+                        slice_copy(j, p, False).start()
+
             own_tok.wait()
-            for copy in own_slices:
-                copy.wait()
-            for d in range(1, wt):
-                for j in range(3):
-                    slice_arrival(j, d).wait_recv()
-            start_lines()
 
         @pl.when(i == 1)
         def _():
@@ -475,6 +484,12 @@
         def _():
             tok.wait(7)
             tok.wait(8)
+
+        for n in range(early_ticks):
+
+            @pl.when(i == min(3 + 2 * n, geo.seq - 1))
+            def _():
+                tick(n)
 
         t = block_owner(i)
         block = tok_buf[t]
@@ -519,8 +534,9 @@
         )
 
     def attend(i, carry):
-        for n in range(min(tick_count, geo.groups // 2)):
-            @pl.when(i == 2 * n + 1)
+        for n in range(early_ticks, loop_ticks):
+
+            @pl.when(i == 2 * (n - early_ticks) + 1)
             def _():
                 tick(n)
 
@@ -585,18 +601,35 @@
             ).wait_recv()
         own_att.wait()
 
-    ticked = min(tick_count, geo.groups // 2)
     if inside:
-        layer_rest(geo, rank, r, starts, ends, id_ref, down_ref, up_ref, att_arrivals, complete, tick, ticked, tick_count)
+        layer_rest(geo, rank, r, starts, ends, id_ref, down_ref, up_ref, att_arrivals, complete, tick, loop_ticks, tick_count)
     else:
         att_arrivals()
 
     for d in range(1, geo.groups):
         att_copy((g + d) % geo.groups).wait_send()
     tok.wait_sends()
-    for d in range(1, wt):
-        for j in range(3):
-            slice_copy(j, d).wait_send()
+    for j in range(3):
+
+        @pl.when(w < wt - 1)
+        def _():
+            slice_copy(j, w, True).wait_send()
+
+        @pl.when(w > 0)
+        def _():
+            slice_copy(j, w, False).wait_send()
+
+        for n in range(wt - 1):
+            p = nth_plane(n)
+
+            @pl.when((p < w) & (w < wt - 1))
+            def _():
+                slice_copy(j, p, True).wait_send()
+
+            @pl.when((p > w) & (w > 0))
+            def _():
+                slice_copy(j, p, False).wait_send()
+
     for m in range(weight_count):
         @pl.when(w < wt - 1)
         def _():
@@ -807,7 +840,7 @@
         dma((4 + count,)),
         dma((Spread.KINDS, units)),
         dma((Spread.KINDS, units)),
-        dma((3, geo.wt)),
+        dma((2, 3, geo.wt)),
         dma((3, geo.wt)),
         dma((2, max(count, 1) * geo.wt)),
         dma((max(count, 1) * geo.wt,)),

time: 279 us -> 262 us (0.939); the launches traced: 279 us -> 259 us
  Pallas kernels: 272 us -> 253 us
    pallas_call x1, Pallas kernels: 152 us -> 136 us  [forward_attention(): pl.pallas_call(functools.partial(forward_kernel, geo, inside, rank), out_...]
    pallas_call x1, Pallas kernels: 32 us -> 25.8 us  [backward_attention(): pl.pallas_call(functools.partial(backward_kernel, geo), out_shape=[jax.Sh...]
where the time goes in v5:
time: 262 us; the launch traced here: 259 us
  Pallas kernels  253 us (97%)
  local copies, waits for them, and re-layouts  5.86 us (2%)
    pallas_call x1, Pallas kernels, forward_attention(): pl.pallas_call(functools.partial(forward_kernel, geo, inside, rank), out_...  136 us
    pallas_call x1, Pallas kernels, closing(): pl.pallas_call(functools.partial(closing_kernel, geo, rank), out_shape=[j...  85.7 us
    pallas_call x1, Pallas kernels, backward_attention(): pl.pallas_call(functools.partial(backward_kernel, geo), out_shape=[jax.Sh...  25.8 us
    unnamed x10, local copies, waits for them, and re-layouts  5.86 us

profile of v5, /device:TPU:0, one launch (start us, length us, event | category | flops | bytes accessed | tf_op | source)
XLA Modules:
  0.0 259.1 jit_solution(2877130108153925878)
XLA Ops:
  0.7 136.4 %layer.1 = (bf16[2048,128]{1,0:T(8,128)(2,1)}, bf16[2048,128]{1,0:T(8,128)(2,1)}, bf16[2048,128]{1,0:T(8,128)(2,1)}, f32[2048,128]{1,0:T(8,128)}, f32[2048,128]{...) custom-call(s32[1,4]{1,0:T(1,128)} %len_ref.5, ...), custom_call_target="tpu_custom_call" | custom-call | tf_op jit(solution)/shard_map/layer/pallas_call | solution.py:883
  137.1 25.8 %attend_back.1 = (bf16[2048,128]{1,0:T(8,128)(2,1)}, bf16[2048,128]{1,0:T(8,128)(2,1)}, bf16[2048,128]{1,0:T(8,128)(2,1)}) custom-call(s32[1,4]{1,0:T(1,128)} %len_ref.5, s32[1,1]{1,0:T(1,128)} %bitcast.16.part_ref, bf16[2048,128]{1,0:T(8,128)(2,1)} %get-tuple-element.38.q_ref, bf16[2048,128]{1,0:T(8,128)(2,1)} %get-tuple-element.39.k_ref, ...), custom_call_target="tpu_custom_call" | custom-call | tf_op jit(solution)/shard_map/attend_back/pallas_call | solution.py:974
  162.9 85.7 %close.1 = (f32[256,1024]{1,0:T(8,128)}, bf16[8,128,1536]{2,1,0:T(8,128)(2,1)}, bf16[8,128,768]{2,1,0:T(8,128)(2,1)}, bf16[4,256,1152]{2,1,0:T(8,128)(2,1)}) custom-call(s32[1,4]{1,0:T(1,128)} %len_ref.5, s32[1,4]{1,0:T(1,128)} %id_ref.3, bf16[256,1024]{1,0:T(8,128)(2,1)} %tokens_ref.3, f32[256,1024]{1,0:T(8,128)} %get-tuple-element.37.first_ref, ...), custom_call_target="tpu_custom_call" | custom-call | tf_op jit(solution)/shard_map/close/pallas_call | solution.py:1443
  248.7 0.0 copy-start
  248.7 1.9 copy-done
  250.5 0.0 copy-start.1
  250.5 1.4 copy-done.1
  252.0 0.0 copy-start.2
  252.0 4.5 %unpack.1 = (f32[4,128,1024]{2,1,0:T(8,128)}, f32[4,128,1024]{2,1,0:T(8,128)}, f32[128,1024]{1,0:T(8,128)}, f32[128,1024]{1,0:T(8,128)}, f32[128,4096]{1,0:T(8,128)}, /*index=5*/f32[128,4096]{1,0:T(8,128)}) custom-call(bf16[8,128,1536]{2,1,0:T(8,128)(2,1)S(1)} %copy-done, bf16[8,128,768]{2,1,0:T(8,128)(2,1)S(1)} %copy-done.1), custom_call_target="tpu_custom_call" | custom-call | tf_op jit(solution)/shard_map/unpack/pallas_call | solution.py:1516
  256.5 0.0 copy-start.3
  256.5 0.0 copy-done.2
  256.5 1.0 copy.32
  257.5 0.6 copy-done.3
  258.1 1.0 copy.33
Async XLA Ops:
  248.7 1.9 copy-start
  250.5 1.4 copy-start.1
  252.0 4.5 %copy-start.2 = (f32[256,1024]{1,0:T(8,128)S(1)}, f32[256,1024]{1,0:T(8,128)}, u32[]{:S(2)}) copy-start(f32[256,1024]{1,0:T(8,128)} %get-tuple-element.72) | copy-start | bytes 3145732
  256.5 1.6 copy-start.3

commit v6 on v5

--- a/solution.py
+++ b/solution.py
@@ -72,6 +72,29 @@
         inside = (positions >= starts[i]) & (positions < ends[i]) & (owner == id_ref[0, i])
         picked = jnp.where(inside, 1.0, picked)
     return picked
+
+
+def placement(id_ref, docs, rank, lane_count):
+    a = lax.broadcasted_iota(jnp.int32, (lane_count, LANES), 0)
+    b = lax.broadcasted_iota(jnp.int32, (lane_count, LANES), 1)
+    every = jnp.zeros((lane_count, LANES), F32)
+    first = jnp.zeros((lane_count, LANES), F32)
+    for d in range(docs):
+        seen = jnp.bool_(False)
+        for e in range(d):
+            seen = seen | (id_ref[0, e] == id_ref[0, d])
+        hit = (a // rank == id_ref[0, d]) & (b // rank == d) & (a % rank == b % rank)
+        every = jnp.where(hit, 1.0, every)
+        first = jnp.where(hit, jnp.where(seen, 0.0, 1.0), first)
+    return every.astype(BF16), first.astype(BF16)
+
+
+def owner_columns(refs, owner, groups):
+    cols = []
+    for ref in refs:
+        wide = ref.shape[1] // groups
+        cols.append(ref[:, pl.ds(pl.multiple_of(owner * wide, LANES), wide)])
+    return jnp.concatenate(cols, axis=1).astype(F32)
 
 
 class Spread:
@@ -214,16 +237,14 @@
     "fc1_down", "fc1_up", "fc2_down", "fc2_up",
 )
 BASE_OUTPUTS = ("q", "k", "v", "o", "lse", "w_slice", "small")
-MLP_OUTPUTS = (
-    "output", "d_first", "d_heads", "g_out_down", "g_out_up", "g_fc1_down", "g_fc2_up", "g_fc1_up", "g_fc2_down",
-)
+MLP_OUTPUTS = ("output", "d_first", "d_heads", "g_out_down", "g_out_up", "g_fc1_down", "early_sum")
 BASE_SCRATCH = (
     "tok", "seg", "att_send_buf", "local_sem", "send_sem", "recv_sem", "slice_send", "slice_recv", "line_send",
     "line_recv", "att_send", "att_recv",
 )
 MLP_SCRATCH = (
     "att", "full_out", "full_fc1", "full_fc2", "unit1", "h1", "h1_low", "act", "slope", "d_pre", "y", "d_att_buf",
-    "back_send", "back_recv",
+    "back_send", "back_recv", "g_fc2_up", "g_fc1_up", "g_fc2_down", "set_out", "set_in", "set_far", "set_sems",
 )
 
 
@@ -602,7 +623,7 @@
         own_att.wait()
 
     if inside:
-        layer_rest(geo, rank, r, starts, ends, id_ref, down_ref, up_ref, att_arrivals, complete, tick, loop_ticks, tick_count)
+        layer_rest(geo, rank, r, starts, ends, id_ref, down_ref, up_ref, att_arrivals, complete, tick, loop_ticks, tick_count, len_ref.shape[1])
     else:
         att_arrivals()
 
@@ -653,7 +674,9 @@
         weight_spread(m, p).wait_sends()
 
 
-def layer_rest(geo, rank, r, starts, ends, id_ref, down_ref, up_ref, att_arrivals, complete, tick, ticked, tick_count):
+def layer_rest(
+    geo, rank, r, starts, ends, id_ref, down_ref, up_ref, att_arrivals, complete, tick, ticked, tick_count, docs
+):
     s, w = lax.axis_index("seq"), lax.axis_index("wt")
     rows, width, groups = geo.rows, geo.width, geo.groups
     part, g = s // groups, s % groups
@@ -667,8 +690,18 @@
     pos = s * rows + lax.broadcasted_iota(jnp.int32, (rows, LANES), 0)
     chosen = select_from(pos, starts, ends, id_ref, rank)
 
+    every = placement(id_ref, docs, rank, lane_count)[0]
+    doc_rows = docs * rank
+    in_doc = (lax.broadcasted_iota(jnp.int32, (rows, LANES), 1) // rank) == segment_from(pos, starts)
+
     def masked(value):
         return (value * chosen).astype(BF16)
+
+    def by_doc(low):
+        return jnp.where(in_doc, dot_nn(low, every), 0.0).astype(BF16)
+
+    def doc_grad(low_by_doc, value):
+        return dot_tn(low_by_doc, value)[:doc_rows].astype(BF16)
 
     def at_step(i):
         return pl.ds(pl.multiple_of(i * step, step), step)
@@ -738,19 +771,35 @@
     r.y[...] = d_second
     d_y = d_second.astype(BF16)
     low_fc2 = masked(dot_nt(d_y, r.fc2_up[...]))
-    r.g_fc2_up[...] = dot_tn(small_fc2, d_y).astype(BF16)
+    r.g_fc2_up[...] = doc_grad(by_doc(small_fc2), d_y)
+    low_fc2_doc, small_fc1_doc = by_doc(low_fc2), by_doc(small_fc1)
 
     def back_step(i, acc):
         cut = at_step(i)
         d_act = dot_nt(d_y, r.full_fc2[cut, :]) + dot_nn(low_fc2, r.fc2_down[:, cut])
         d_pre = (d_act * r.slope[:, cut]).astype(BF16)
         r.d_pre[:, cut] = d_pre
-        r.g_fc2_down[:, cut] = dot_tn(low_fc2, r.act[:, cut]).astype(BF16)
-        r.g_fc1_up[:, cut] = dot_tn(small_fc1, d_pre).astype(BF16)
+        r.g_fc2_down[:, cut] = doc_grad(low_fc2_doc, r.act[:, cut])
+        r.g_fc1_up[:, cut] = doc_grad(small_fc1_doc, d_pre)
         return acc + dot_nt(d_pre, r.fc1_up[:, cut])
 
     low_fc1 = masked(lax.fori_loop(0, steps, back_step, jnp.zeros((rows, lane_count), F32)))
-    r.g_fc1_down[...] = dot_tn(low_fc1, r.h1_low[...]).astype(BF16)
+
+    def make_early(chip, whose):
+        return owner_columns((r.g_fc2_up, r.g_fc1_up, r.g_fc2_down), chip * 2 + whose, groups)
+
+    early = PairSum(
+        groups // 2,
+        g // 2,
+        s % 2,
+        part * groups,
+        w,
+        (r.set_out, r.set_in, r.set_far),
+        [r.set_sems.at[i] for i in range(4)],
+        make_early,
+    )
+    early.run()
+    r.g_fc1_down[...] = doc_grad(by_doc(low_fc1), r.h1_low[...])
 
     def back_band(i, carry):
         cut = at_band(i)
@@ -794,8 +843,10 @@
         r.d_att_buf.at[g], r.d_heads.at[pl.ds(pl.multiple_of(g * rows, rows), rows)], r.local_sem.at[0]
     )
     own.start()
-    r.g_out_down[...] = dot_tn(low_out, r.att[...]).astype(BF16)
-    r.g_out_up[...] = dot_tn(small_out, d_z).astype(BF16)
+    r.g_out_down[...] = doc_grad(by_doc(low_out), r.att[...])
+    r.g_out_up[...] = doc_grad(by_doc(small_out), d_z)
+    r.early_sum[...] = early.finish().astype(BF16)
+    early.drain()
     for d in range(1, groups):
         other = (g + d) % groups
         here = r.d_heads.at[pl.ds(pl.multiple_of(other * rows, rows), rows)]
@@ -849,18 +900,19 @@
     ]
     if inside:
         hidden = mlp[1].shape[1]
+        doc_rows = lengths.shape[1] * rank
+        early = (width + 2 * hidden) // geo.groups
+        near = geo.groups // 2
         shapes += [
             struct((rows, width), F32),
             struct((rows, width), F32),
             struct((geo.queries, LANES), BF16),
-            struct((lane_count, width), BF16),
-            struct((lane_count, width), BF16),
-            struct((lane_count, width), BF16),
-            struct((lane_count, width), BF16),
-            struct((lane_count, hidden), BF16),
-            struct((lane_count, hidden), BF16),
+            struct((doc_rows, width), BF16),
+            struct((doc_rows, width), BF16),
+            struct((doc_rows, width), BF16),
+            struct((doc_rows, early), BF16),
         ]
-        specs += [vmem, vmem, any_spec] + [vmem] * 6
+        specs += [vmem, vmem, any_spec] + [vmem] * 4
         scratch += [
             pltpu.VMEM((rows, width), BF16),
             pltpu.VMEM((width, width), BF16),
@@ -876,6 +928,13 @@
             pltpu.VMEM((geo.groups, rows, LANES), BF16),
             dma((geo.groups,)),
             dma((geo.groups,)),
+            pltpu.VMEM((doc_rows, width), BF16),
+            pltpu.VMEM((doc_rows, hidden), BF16),
+            pltpu.VMEM((doc_rows, hidden), BF16),
+            pltpu.VMEM((near, doc_rows, early), BF16),
+            pltpu.VMEM((near, doc_rows, early), BF16),
+            pltpu.VMEM((near, doc_rows, early), BF16),
+            dma((4, near)),
         ]
     else:
         shapes += [struct((rows, width), BF16)]
@@ -894,7 +953,8 @@
 
 
 def backward_kernel(geo, len_ref, part_ref, q_ref, k_ref, v_ref, o_ref, lse_ref, g_ref, dq_ref, dk_ref, dv_ref, dk_acc, dv_acc):
-    rows = geo.rows
+    rows = min(512, geo.queries)
+    block = min(512, geo.keys)
     part = part_ref[0, 0]
     scale = HEAD_DIM ** (-0.5)
     starts, ends = doc_bounds(len_ref)
@@ -914,56 +974,41 @@
             found = jnp.where(index == i, values[i], found)
         return found
 
+    def both_heads(value):
+        zero = jnp.zeros_like(value)
+        return jnp.concatenate([jnp.where(first_head, value, zero), jnp.where(first_head, zero, value)], axis=0)
+
     def query_block(b, carry):
         at = pl.ds(pl.multiple_of(b * rows, rows), rows)
-        origin = (part * geo.groups + b) * rows
-        query = q_ref[at, :] * jnp.asarray(scale, BF16)
-        cot = g_ref[at, :]
-        lse = lse_ref[at, :]
-        both = cot.astype(F32) * o_ref[at, :]
+        origin = part * geo.queries + b * rows
+        query = both_heads(q_ref[at, :] * jnp.asarray(scale, BF16))
+        cot = both_heads(g_ref[at, :])
+        scaled = cot * jnp.asarray(scale, BF16)
+        lse = jnp.concatenate([lse_ref[at, h * HEAD_DIM : h * HEAD_DIM + 1] for h in range(PAIR)], axis=0)
+        out = o_ref[at, :]
+        dot = jnp.sum(scaled.astype(F32) * jnp.concatenate([out, out], axis=0), axis=1, keepdims=True)
         q_pos = origin + lax.broadcasted_iota(jnp.int32, (rows, 1), 0)
         q_seg = segment_from(q_pos, starts)
-        heads = []
-        for h in range(PAIR):
-            mask = first_head if h == 0 else jnp.logical_not(first_head)
-            zero = jnp.zeros_like(query)
-            heads.append(
-                (
-                    jnp.where(mask, query, zero),
-                    jnp.where(mask, cot, zero),
-                    lse[:, h * HEAD_DIM : h * HEAD_DIM + 1],
-                    jnp.sum(jnp.where(mask, both, 0.0), axis=1, keepdims=True),
-                )
-            )
-        low = pick(starts, seg_of(origin)) // rows
-        high = (pick(ends, seg_of(origin + rows - 1)) + rows - 1) // rows
-
-        def key_block(c, accs):
-            keys_at = pl.ds(pl.multiple_of(c * rows, rows), rows)
+        q_seg = jnp.concatenate([q_seg, q_seg], axis=0)
+        low = pick(starts, seg_of(origin)) // block
+        high = (pick(ends, seg_of(origin + rows - 1)) + block - 1) // block
+
+        def key_block(c, acc):
+            keys_at = pl.ds(pl.multiple_of(c * block, block), block)
             key, value = k_ref[keys_at, :], v_ref[keys_at, :]
-            k_pos = c * rows + lax.broadcasted_iota(jnp.int32, (1, rows), 1)
-            same = q_seg == segment_from(k_pos, starts)
-            new = []
-            dk_parts, dv_parts = [], []
-            for h in range(PAIR):
-                q_head, g_head, lse_head, dot_head = heads[h]
-                score = jnp.where(same, dot_nt(q_head, key), -1e30)
-                prob = jnp.exp(score - lse_head)
-                d_prob = dot_nt(g_head, value)
-                raw = (prob * (d_prob - dot_head) * scale).astype(BF16)
-                new.append(accs[h] + dot_nn(raw, key))
-                dk_parts.append(dot_tn(raw, q_head))
-                dv_parts.append(dot_tn(prob.astype(BF16), g_head))
-            dk_acc[keys_at, :] += dk_parts[0] + dk_parts[1]
-            dv_acc[keys_at, :] += dv_parts[0] + dv_parts[1]
-            return tuple(new)
-
-        zero = jnp.zeros((rows, LANES), F32)
-        accs = lax.fori_loop(low, high, key_block, (zero, zero))
-        dq_ref[at, :] = jnp.where(first_head, accs[0], accs[1]).astype(BF16)
+            k_pos = c * block + lax.broadcasted_iota(jnp.int32, (1, block), 1)
+            score = jnp.where(q_seg == segment_from(k_pos, starts), dot_nt(query, key), -1e30)
+            prob = jnp.exp(score - lse)
+            raw = (prob * (dot_nt(scaled, value) - dot)).astype(BF16)
+            dk_acc[keys_at, :] += dot_tn(raw, query)
+            dv_acc[keys_at, :] += dot_tn(prob.astype(BF16), cot)
+            return acc + dot_nn(raw, key)
+
+        acc = lax.fori_loop(low, high, key_block, jnp.zeros((PAIR * rows, LANES), F32))
+        dq_ref[at, :] = jnp.where(first_head, acc[:rows], acc[rows:]).astype(BF16)
         return carry
 
-    lax.fori_loop(0, geo.groups, query_block, 0)
+    lax.fori_loop(0, geo.queries // rows, query_block, 0)
     dk_ref[...] = (dk_acc[...] * HEAD_DIM**0.5).astype(BF16)
     dv_ref[...] = dv_acc[...].astype(BF16)
 
@@ -1035,8 +1080,8 @@
             device_id_type=MESH,
         )
 
-    def start(self):
-        def step(d, carry):
+    def run(self):
+        def start(d):
             chip = (self.me + 1 + d) % self.count
             if self.slots < self.count:
 
@@ -1046,20 +1091,21 @@
 
             self.near_out[d % self.slots] = self.make(chip, 1 - self.core).astype(BF16)
             self.near(chip).start()
-            return carry
-
-        lax.fori_loop(0, self.count, step, 0)
-
-    def send(self):
-        def step(d, carry):
+
+        def send(d):
             chip = (self.me + 1 + d) % self.count
             own = self.make(chip, self.core)
             self.near(chip).wait_recv()
             self.near_in[chip] = (own + self.near_in[chip].astype(F32)).astype(BF16)
             self.far(chip).start()
+
+        def step(d, carry):
+            start(d)
+            send(d - 1)
             return carry
 
-        lax.fori_loop(0, self.count - 1, step, 0)
+        start(0)
+        lax.fori_loop(1, self.count, step, 0)
 
     def finish(self):
         total = self.make(self.me, self.core)
@@ -1099,6 +1145,8 @@
 def closing_kernel(
     geo,
     rank,
+    single_count,
+    early,
     len_ref,
     id_ref,
     tokens_ref,
@@ -1110,48 +1158,47 @@
     down_ref,
     up_ref,
     small_ref,
-    out_down_ref,
-    out_up_ref,
-    fc1_down_ref,
-    fc2_up_ref,
-    fc1_up_ref,
-    fc2_down_ref,
-    grad_ref,
-    sum1_ref,
-    sum2_ref,
-    tok_far,
-    tok_out,
-    tok_in,
-    tok_stage,
-    small_buf,
-    set1_out,
-    set1_in,
-    set1_far,
-    set2_out,
-    set2_in,
-    set2_far,
-    down_acc,
-    up_acc,
-    mine1,
-    mine2,
-    place_buf,
-    fold_buf,
-    all1,
-    all2,
-    places,
-    done1,
-    done2,
-    tok_sems,
-    set1_sems,
-    set2_sems,
-    line_send,
-    line_recv,
-    spread_send,
-    spread_recv,
-    local_sem,
-    stage_sem,
-    small_sem,
+    *refs,
 ):
+    singles = refs[:single_count]
+    early_ref = refs[single_count] if early else None
+    (
+        grad_ref,
+        sum1_ref,
+        sum2_ref,
+        tok_far,
+        tok_out,
+        tok_in,
+        tok_stage,
+        small_buf,
+        set1_out,
+        set1_in,
+        set1_far,
+        set2_out,
+        set2_in,
+        set2_far,
+        down_acc,
+        up_acc,
+        mine1,
+        mine2,
+        place_buf,
+        fold_buf,
+        all1,
+        all2,
+        places,
+        done1,
+        done2,
+        tok_sems,
+        set1_sems,
+        set2_sems,
+        line_send,
+        line_recv,
+        spread_send,
+        spread_recv,
+        local_sem,
+        stage_sem,
+        small_sem,
+    ) = refs[single_count + early :]
     x, y, core, w = device_here(geo)
     s = lax.axis_index("seq")
     rows, width, wt, groups, parts = geo.rows, geo.width, geo.wt, geo.groups, geo.parts
@@ -1161,14 +1208,6 @@
     lane_count = down_ref.shape[0] // 4
     lanes = pl.ds(pl.multiple_of(g * LANES, LANES), LANES)
     starts, ends = doc_bounds(len_ref)
-    ids = [id_ref[0, d] for d in range(docs)]
-    fresh = []
-    for d in range(docs):
-        seen = jnp.bool_(False)
-        for e in range(d):
-            seen = seen | (ids[e] == ids[d])
-        fresh.append(jnp.where(seen, 0.0, 1.0))
-
     greet_all(geo)
 
     def iota(shape, dim):
@@ -1208,18 +1247,11 @@
         (tok_stage, stage_sem),
     )
 
-    singles = [out_down_ref, out_up_ref, fc1_down_ref, fc2_up_ref, fc1_up_ref, fc2_down_ref]
-
     def by_document(value):
         return dot_tn(fold_buf[...], value)[:doc_rows]
 
     def make_set1(chip, whose):
-        owner = chip * 2 + whose
-        cols = []
-        for ref in singles:
-            wide = ref.shape[1] // groups
-            cols.append(by_document(ref[:, pl.ds(pl.multiple_of(owner * wide, LANES), wide)]))
-        return jnp.concatenate(cols, axis=1)
+        return owner_columns(singles, chip * 2 + whose, groups)
 
     def make_set2(chip, whose):
         owner = chip * 2 + whose
@@ -1241,11 +1273,21 @@
 
     mine_at = part * wt + w
 
+    late = set1_out.shape[2]
+    whole = mine1.shape[1]
+
+    def cut_of(kind, ref):
+        if kind == 0:
+            return ref.at[:, pl.ds(0, late)]
+        if kind == 3:
+            return ref.at[:, pl.ds(late, whole - late)]
+        return ref
+
     def line_copy(kind, n, src, dst_all):
         device, plane, _ = peer(n)
         return pltpu.make_async_remote_copy(
-            src_ref=src,
-            dst_ref=dst_all.at[mine_at],
+            src_ref=cut_of(kind, src),
+            dst_ref=cut_of(kind, dst_all.at[mine_at]),
             send_sem=line_send.at[kind, n],
             recv_sem=line_recv.at[kind, mine_at],
             device_id=(device, plane),
@@ -1255,8 +1297,8 @@
     def line_arrival(kind, n, dst_all):
         device, plane, at = peer(n)
         return pltpu.make_async_remote_copy(
-            src_ref=dst_all.at[at],
-            dst_ref=dst_all.at[at],
+            src_ref=cut_of(kind, dst_all.at[at]),
+            dst_ref=cut_of(kind, dst_all.at[at]),
             send_sem=line_send.at[kind, n],
             recv_sem=line_recv.at[kind, at],
             device_id=(device, plane),
@@ -1291,6 +1333,8 @@
             line_arrival(kind, n, dst_all).wait_recv()
             if kind == 0:
                 line_arrival(2, n, places).wait_recv()
+                if early:
+                    line_arrival(3, n, dst_all).wait_recv()
             at = peer(n)[2]
             total = total + dot_nn(places[at][:, :doc_rows], dst_all[at])
         finals[kind][...] = total.astype(BF16)
@@ -1314,22 +1358,16 @@
         spread.wait(3)
         spread.go(8)
 
-    a, b = iota((lane_count, LANES), 0), iota((lane_count, LANES), 1)
-    places_all = jnp.zeros((lane_count, LANES), F32)
-    places_first = jnp.zeros((lane_count, LANES), F32)
-    for d in range(docs):
-        hit = (a // rank == ids[d]) & (b // rank == d) & (a % rank == b % rank)
-        places_all = jnp.where(hit, 1.0, places_all)
-        places_first = jnp.where(hit, fresh[d], places_first)
-    place_buf[...] = places_all.astype(BF16)
-    fold_buf[...] = places_first.astype(BF16)
+    place_buf[...], fold_buf[...] = placement(id_ref, docs, rank, lane_count)
     for n in peers:
         line_copy(2, n, place_buf, places).start()
-
-    set1.start()
-    tok.start()
-    set1.send()
-    tok.send()
+    if early:
+        mine1[:, late:] = early_ref[...]
+        for n in peers:
+            line_copy(3, n, mine1, all1).start()
+
+    set1.run()
+    tok.run()
 
     def small_copy(t):
         return pltpu.make_async_copy(
@@ -1361,7 +1399,7 @@
     small_copy(0).start()
     lax.fori_loop(0, geo.seq, add_up, 0)
 
-    mine1[...] = set1.finish().astype(BF16)
+    mine1[:, :late] = set1.finish().astype(BF16)
     for n in peers:
         line_copy(0, n, mine1, all1).start()
 
@@ -1381,9 +1419,8 @@
         by_doc = dot_nn(low, widen[:, :doc_rows])
         by_doc = jnp.where(in_doc, by_doc, 0.0).astype(BF16)
         down_acc[j * doc_rows : (j + 1) * doc_rows, :] = dot_tn(by_doc, tokens)
-    set2.start()
+    set2.run()
     grad_ref[...] = total
-    set2.send()
     place(0, mine1, all1)
     for j in range(3):
         mine2[:, (3 + j) * LANES : (4 + j) * LANES] = by_document(
@@ -1406,6 +1443,8 @@
         line_copy(0, n, mine1, all1).wait_send()
         line_copy(1, n, mine2, all2).wait_send()
         line_copy(2, n, place_buf, places).wait_send()
+        if early:
+            line_copy(3, n, mine1, all1).wait_send()
     tok.drain()
     set1.drain()
     set2.drain()
@@ -1426,12 +1465,14 @@
     pl.semaphore_wait(barrier, count)
 
 
-def closing(geo, rank, lengths, ids, tokens, d_first, dq, dk, dv, w_slice, down, up, small, grads):
+def closing(geo, rank, lengths, ids, tokens, d_first, dq, dk, dv, w_slice, down, up, small, grads, early_sum):
     rows, width = geo.rows, geo.width
     docs = lengths.shape[1]
     doc_rows = docs * rank
     lane_count = down.shape[0] // 4
-    set1 = sum(v.shape[1] for v in grads) // geo.groups
+    early = [] if early_sum is None else [early_sum]
+    late = sum(v.shape[1] for v in grads) // geo.groups
+    set1 = late + sum(v.shape[1] for v in early)
     set2 = 6 * LANES
     chips, near = geo.seq // 2, geo.groups // 2
     peers = geo.wt * geo.parts
@@ -1441,23 +1482,23 @@
     dma = pltpu.SemaphoreType.DMA
     wide = width + LANES
     return pl.pallas_call(
-        functools.partial(closing_kernel, geo, rank),
+        functools.partial(closing_kernel, geo, rank, len(grads), len(early)),
         out_shape=[
             jax.ShapeDtypeStruct((rows, width), F32),
             jax.ShapeDtypeStruct((geo.groups, lane_count, set1), BF16),
             jax.ShapeDtypeStruct((geo.groups, lane_count, set2), BF16),
             jax.ShapeDtypeStruct((chips, rows, wide), BF16),
         ],
-        in_specs=[smem, smem] + [vmem] * 8 + [any_spec] + [vmem] * len(grads),
+        in_specs=[smem, smem] + [vmem] * 8 + [any_spec] + [vmem] * (len(grads) + len(early)),
         out_specs=[vmem, any_spec, any_spec, any_spec],
         scratch_shapes=[
             pltpu.VMEM((min(chips, 4), rows, wide), BF16),
             pltpu.VMEM((chips, rows, wide), BF16),
             pltpu.VMEM((2, rows, wide), BF16),
             pltpu.VMEM((2, rows, 3 * lane_count), BF16),
-            pltpu.VMEM((near, doc_rows, set1), BF16),
-            pltpu.VMEM((near, doc_rows, set1), BF16),
-            pltpu.VMEM((near, doc_rows, set1), BF16),
+            pltpu.VMEM((near, doc_rows, late), BF16),
+            pltpu.VMEM((near, doc_rows, late), BF16),
+            pltpu.VMEM((near, doc_rows, late), BF16),
             pltpu.VMEM((near, doc_rows, 3 * LANES), BF16),
             pltpu.VMEM((near, doc_rows, 3 * LANES), BF16),
             pltpu.VMEM((near, doc_rows, 3 * LANES), BF16),
@@ -1475,8 +1516,8 @@
             dma((4, chips)),
             dma((4, near)),
             dma((4, near)),
-            dma((3, peers)),
-            dma((3, peers)),
+            dma((4, peers)),
+            dma((4, peers)),
             dma((Spread.KINDS, 2)),
             dma((Spread.KINDS, 2)),
             dma((2,)),
@@ -1487,7 +1528,7 @@
             collective_id=1, has_side_effects=True, vmem_limit_bytes=VMEM_LIMIT
         ),
         name="close",
-    )(lengths, ids, tokens, d_first, dq, dk, dv, w_slice, down, up, small, *grads)
+    )(lengths, ids, tokens, d_first, dq, dk, dv, w_slice, down, up, small, *grads, *early)
 
 
 def unpack_kernel(one_ref, two_ref, down_ref, up_ref, fc1_down_ref, fc2_up_ref, fc1_up_ref, fc2_down_ref):
@@ -1522,7 +1563,7 @@
             pl.BlockSpec((1,) + two.shape[1:], lambda i: (i, 0, 0)),
         ],
         out_specs=[four_spec, four_spec, flat(LANES), flat(LANES), flat(thick), flat(thick)],
-        compiler_params=pltpu.CompilerParams(vmem_limit_bytes=VMEM_LIMIT // 2),
+        compiler_params=pltpu.CompilerParams(vmem_limit_bytes=VMEM_LIMIT),
         name="unpack",
     )(one, two)
 
@@ -1577,7 +1618,15 @@
     doc_range = jnp.arange(lengths.shape[0], dtype=jnp.int32)
     chosen = jnp.sum(jnp.where(local_seg[:, None] == doc_range[None, :], ids[None, :], 0), axis=1)
     lane_owner = jnp.arange(lane_count, dtype=jnp.int32) // rank_size
-    return (chosen[:, None] == lane_owner[None, :]).astype(jnp.float32)
+    lane_rank = jnp.arange(lane_count, dtype=jnp.int32) % rank_size
+    doc_owner = jnp.repeat(doc_range, rank_size)
+    doc_rank = jnp.arange(doc_owner.shape[0], dtype=jnp.int32) % rank_size
+    to_doc = (lane_owner[:, None] == jnp.repeat(ids, rank_size)[None, :]) & (lane_rank[:, None] == doc_rank[None, :])
+    return (
+        (chosen[:, None] == lane_owner[None, :]).astype(jnp.float32),
+        to_doc.astype(jnp.bfloat16),
+        (local_seg[:, None] == doc_owner[None, :]).astype(jnp.float32),
+    )
 
 
 def feed_forward(
@@ -1589,6 +1638,11 @@
     out_down, out_up = attn_maps
     fc1_down_all, fc1_up_all = fc1_maps
     fc2_down_all, fc2_up_all = fc2_maps
+    select, to_doc, in_doc = select
+
+    def by_doc(low):
+        return (jnp.dot(low, to_doc, preferred_element_type=jnp.float32) * in_doc).astype(jnp.bfloat16)
+
     out_main = jnp.dot(attended_tok, full_out, preferred_element_type=jnp.float32)
     small_out = (
         jnp.dot(attended_tok, out_down, preferred_element_type=jnp.float32) * select
@@ -1623,21 +1677,21 @@
     d_act = times_transposed(d_y, full_fc2)
     low_fc2 = (times_transposed(d_y, fc2_up_all) * select).astype(jnp.bfloat16)
     d_act = d_act + times_transposed(low_fc2, fc2_down_all)
-    grad_fc2_up = left_inner(small_fc2, d_y)
-    grad_fc2_down = left_inner(low_fc2, act_low)
+    grad_fc2_up = left_inner(by_doc(small_fc2), d_y)
+    grad_fc2_down = left_inner(by_doc(low_fc2), act_low)
     d_pre = gelu_back(d_act)[0].astype(jnp.bfloat16)
     d_first_low = times_transposed(d_pre, full_fc1)
     low_fc1 = (times_transposed(d_pre, fc1_up_all) * select).astype(jnp.bfloat16)
     d_first_low = d_first_low + times_transposed(low_fc1, fc1_down_all)
-    grad_fc1_up = left_inner(small_fc1, d_pre)
-    grad_fc1_down = left_inner(low_fc1, first_low)
+    grad_fc1_up = left_inner(by_doc(small_fc1), d_pre)
+    grad_fc1_down = left_inner(by_doc(low_fc1), first_low)
     d_first = norm1_back(d_second + d_first_low)[0]
     d_z = d_first.astype(jnp.bfloat16)
     d_attended = times_transposed(d_z, full_out)
     low_out = (times_transposed(d_z, out_up) * select).astype(jnp.bfloat16)
     d_attended = (d_attended + times_transposed(low_out, out_down)).astype(jnp.bfloat16)
-    grad_out_up = left_inner(small_out, d_z)
-    grad_out_down = left_inner(low_out, attended_tok)
+    grad_out_up = left_inner(by_doc(small_out), d_z)
+    grad_out_down = left_inner(by_doc(low_out), attended_tok)
     blocks = [
         [p * geo.groups + i for i in range(geo.groups)] for p in range(geo.parts)
     ]
@@ -1705,8 +1759,9 @@
         geo, rank_size, doc_lengths, adapter_ids, tokens, w_qkv, down_rows, up_rows, qv_bias, mlp
     )
     if inside:
-        output, d_first, d_heads, *set1 = rest
+        output, d_first, d_heads, *set1, early_sum = rest
     else:
+        early_sum = None
         output, d_first, d_heads, set1 = feed_forward(
             geo,
             tokens,
@@ -1737,6 +1792,7 @@
         up_rows,
         small_all,
         set1,
+        early_sum,
     )
 
     down4, up4, fc1_down_sum, fc2_up_sum, fc1_up_sum, fc2_down_sum = unpack(geo, sum1, sum2, lane_count)

time: 262 us -> 245 us (0.935)
  Pallas kernels: 253 us -> 241 us
  local copies, waits for them, and re-layouts: 5.86 us -> 2.57 us
    pallas_call x1, Pallas kernels: 85.7 us -> 74.7 us  [closing(): pl.pallas_call(functools.partial(closing_kernel, geo, rank, len(grads), l...]
    pallas_call x1, Pallas kernels: 25.8 us -> 19.7 us  [backward_attention(): pl.pallas_call(functools.partial(backward_kernel, geo), out_shape=[jax.Sh...]
    unnamed x10 -> x6, local copies, waits for them, and re-layouts: 5.86 us -> 2.57 us
    pallas_call x1, Pallas kernels: 4.54 us -> 7.59 us  [unpack(): pl.pallas_call(unpack_kernel, grid=(groups,), out_shape=[four, four, whol...]
    pallas_call x1, Pallas kernels: 136 us -> 139 us  [forward_attention(): pl.pallas_call(functools.partial(forward_kernel, geo, inside, rank), out_...]
where the time goes in v6:
time: 245 us
  Pallas kernels  241 us (98%)
  local copies, waits for them, and re-layouts  2.57 us (1%)
    pallas_call x1, Pallas kernels, forward_attention(): pl.pallas_call(functools.partial(forward_kernel, geo, inside, rank), out_...  139 us
    pallas_call x1, Pallas kernels, closing(): pl.pallas_call(functools.partial(closing_kernel, geo, rank, len(grads), l...  74.7 us
    pallas_call x1, Pallas kernels, backward_attention(): pl.pallas_call(functools.partial(backward_kernel, geo), out_shape=[jax.Sh...  19.7 us
    pallas_call x1, Pallas kernels, unpack(): pl.pallas_call(unpack_kernel, grid=(groups,), out_shape=[four, four, whol...  7.59 us

profile of v6, /device:TPU:0, one launch (start us, length us, event | category | flops | bytes accessed | tf_op | source)
XLA Modules:
  0.0 244.5 jit_solution(3906265672230656187)
XLA Ops:
  0.7 139.3 %layer.1 = (bf16[2048,128]{1,0:T(8,128)(2,1)}, bf16[2048,128]{1,0:T(8,128)(2,1)}, bf16[2048,128]{1,0:T(8,128)(2,1)}, f32[2048,128]{1,0:T(8,128)}, f32[2048,128]{...) custom-call(s32[1,4]{1,0:T(1,128)} %len_ref.5, ...), custom_call_target="tpu_custom_call" | custom-call | tf_op jit(solution)/shard_map/layer/pallas_call | solution.py:942
  140.0 19.7 %attend_back.1 = (bf16[2048,128]{1,0:T(8,128)(2,1)}, bf16[2048,128]{1,0:T(8,128)(2,1)}, bf16[2048,128]{1,0:T(8,128)(2,1)}) custom-call(s32[1,4]{1,0:T(1,128)} %len_ref.5, s32[1,1]{1,0:T(1,128)} %bitcast.16.part_ref, bf16[2048,128]{1,0:T(8,128)(2,1)} %get-tuple-element.36.q_ref, bf16[2048,128]{1,0:T(8,128)(2,1)} %get-tuple-element.37.k_ref, ...), custom_call_target="tpu_custom_call" | custom-call | tf_op jit(solution)/shard_map/attend_back/pallas_call | solution.py:1019
  159.7 74.7 %close.1 = (f32[256,1024]{1,0:T(8,128)}, bf16[8,128,1536]{2,1,0:T(8,128)(2,1)}, bf16[8,128,768]{2,1,0:T(8,128)(2,1)}, bf16[4,256,1152]{2,1,0:T(8,128)(2,1)}) custom-call(s32[1,4]{1,0:T(1,128)} %len_ref.5, s32[1,4]{1,0:T(1,128)} %id_ref.3, bf16[256,1024]{1,0:T(8,128)(2,1)} %tokens_ref.3, f32[256,1024]{1,0:T(8,128)} %get-tuple-element.35.first_ref, ...), custom_call_target="tpu_custom_call" | custom-call | tf_op jit(solution)/shard_map/close/pallas_call | solution.py:1484
  234.4 0.0 copy-start
  234.4 7.6 %unpack.1 = (f32[4,128,1024]{2,1,0:T(8,128)}, f32[4,128,1024]{2,1,0:T(8,128)}, f32[128,1024]{1,0:T(8,128)}, f32[128,1024]{1,0:T(8,128)}, f32[128,4096]{1,0:T(8,128)}, /*index=5*/f32[128,4096]{1,0:T(8,128)}) custom-call(bf16[8,128,1536]{2,1,0:T(8,128)(2,1)} %get-tuple-element.52.one_ref, bf16[8,128,768]{2,1,0:T(8,128)(2,1)} %get-tuple-element.53.two_ref), custom_call_target="tpu_custom_call" | custom-call | tf_op jit(solution)/shard_map/unpack/pallas_call | solution.py:1557
  242.0 0.0 copy-start.1
  242.0 0.0 copy-done
  242.0 1.0 copy.32
  242.9 0.6 copy-done.1
  243.6 1.0 copy.33
Async XLA Ops:
  234.4 7.6 %copy-start = (f32[256,1024]{1,0:T(8,128)S(1)}, f32[256,1024]{1,0:T(8,128)}, u32[]{:S(2)}) copy-start(f32[256,1024]{1,0:T(8,128)} %get-tuple-element.68) | copy-start | bytes 3145732
  242.0 1.6 copy-start.1

commit v7 on v6

--- a/solution.py
+++ b/solution.py
@@ -1142,6 +1142,132 @@
                 self.far(chip).wait_send()
 
 
+class CrossSum(PairSum):
+    def with_corner(self, via, via_send, via_recv):
+        self.via, self.via_send, self.via_recv = via, via_send, via_recv
+        x, y = self.me % 2, self.me // 2
+        self.near_chips = [y * 2 + 1 - x, (1 - y) * 2 + x]
+        self.corner = (1 - y) * 2 + 1 - x
+        self.half = self.near_in.shape[1] // 2
+        return self
+
+    def part(self, ref, h):
+        return ref.at[pl.ds(h * self.half, self.half)]
+
+    def device(self, chip):
+        return (self.first + chip * 2 + self.core, self.w)
+
+    def corner_copy(self, h):
+        return pltpu.make_async_remote_copy(
+            src_ref=self.part(self.near_in.at[self.corner], h),
+            dst_ref=self.via.at[h],
+            send_sem=self.via_send.at[h],
+            recv_sem=self.via_recv.at[h],
+            device_id=self.device(self.near_chips[h]),
+            device_id_type=MESH,
+        )
+
+    def near_copy(self, which, h):
+        chip = self.near_chips[which]
+        return pltpu.make_async_remote_copy(
+            src_ref=self.part(self.near_in.at[chip], h),
+            dst_ref=self.part(self.far_in.at[self.me], h),
+            send_sem=self.far_send.at[which * 2 + h],
+            recv_sem=self.far_recv.at[which * 2 + h],
+            device_id=self.device(chip),
+            device_id_type=MESH,
+        )
+
+    def near_arrival(self, which, h):
+        here = self.part(self.far_in.at[self.near_chips[which]], h)
+        return pltpu.make_async_remote_copy(
+            src_ref=here,
+            dst_ref=here,
+            send_sem=self.far_send.at[which * 2 + h],
+            recv_sem=self.far_recv.at[which * 2 + h],
+            device_id=self.device(self.near_chips[which]),
+            device_id_type=MESH,
+        )
+
+    def run(self):
+        order = [self.corner] + self.near_chips + [self.me]
+
+        def chip_at(d):
+            chip = order[0]
+            for i in range(1, len(order)):
+                chip = jnp.where(d == i, order[i], chip)
+            return chip
+
+        def start(d):
+            chip = chip_at(d)
+            self.near_out[chip] = self.make(chip, 1 - self.core).astype(BF16)
+            self.near(chip).start()
+
+        start(0)
+
+        def step(d, carry):
+            start(d)
+            chip = chip_at(d - 1)
+            own = self.make(chip, self.core)
+            self.near(chip).wait_recv()
+            self.near_in[chip] = (own + self.near_in[chip].astype(F32)).astype(BF16)
+
+            @pl.when(d == 1)
+            def _():
+                self.corner_copy(0).start()
+                self.corner_copy(1).start()
+
+            @pl.when(d == 2)
+            def _():
+                self.near_copy(0, 0).start()
+
+            @pl.when(d == 3)
+            def _():
+                self.near_copy(1, 1).start()
+
+            return carry
+
+        lax.fori_loop(1, len(order), step, 0)
+        for which in range(2):
+            h = 1 - which
+            self.corner_copy(h).wait_recv()
+            chip = self.near_chips[which]
+            rows = pl.ds(h * self.half, self.half)
+            self.near_in[chip, rows, :] = (
+                self.near_in[chip, rows, :].astype(F32) + self.via[h].astype(F32)
+            ).astype(BF16)
+            self.near_copy(which, h).start()
+
+    def slot(self, chip):
+        return chip
+
+    def finish(self):
+        stage, sem = self.stage
+        total = self.make(self.me, self.core)
+        self.near(self.me).wait_recv()
+        total = total + self.near_in[self.me].astype(F32)
+        fetches = []
+        for which in range(2):
+            for h in range(2):
+                self.near_arrival(which, h).wait_recv()
+            fetches.append(
+                pltpu.make_async_copy(self.far_in.at[self.near_chips[which]], stage.at[which], sem.at[which])
+            )
+            fetches[-1].start()
+        for which in range(2):
+            fetches[which].wait()
+            total = total + stage[which].astype(F32)
+        return total
+
+    def drain(self):
+        for chip in [self.corner] + self.near_chips + [self.me]:
+            self.near(chip).wait_send()
+        for h in range(2):
+            self.corner_copy(h).wait_send()
+            for which in range(2):
+                self.near_copy(which, h).wait_send()
+
+
 def closing_kernel(
     geo,
     rank,
@@ -1198,6 +1324,8 @@
         local_sem,
         stage_sem,
         small_sem,
+        tok_via,
+        via_sems,
     ) = refs[single_count + early :]
     x, y, core, w = device_here(geo)
     s = lax.axis_index("seq")
@@ -1242,10 +1370,13 @@
             low = low + dot_nn((part_low * chosen).astype(BF16), fold(j))
         return jnp.concatenate([total, low], axis=1)
 
-    tok = PairSum(
+    square = geo.nx == 2 and geo.ny == 2
+    tok = (CrossSum if square else PairSum)(
         geo.seq // 2, s // 2, core, 0, w, (tok_out, tok_in, tok_far), [tok_sems.at[i] for i in range(4)], make_tokens,
         (tok_stage, stage_sem),
     )
+    if square:
+        tok.with_corner(tok_via, via_sems.at[0], via_sems.at[1])
 
     def by_document(value):
         return dot_tn(fold_buf[...], value)[:doc_rows]
@@ -1274,13 +1405,14 @@
     mine_at = part * wt + w
 
     late = set1_out.shape[2]
+    front = late + 3 * LANES
     whole = mine1.shape[1]
 
     def cut_of(kind, ref):
         if kind == 0:
-            return ref.at[:, pl.ds(0, late)]
+            return ref.at[:, pl.ds(0, front)]
         if kind == 3:
-            return ref.at[:, pl.ds(late, whole - late)]
+            return ref.at[:, pl.ds(front, whole - front)]
         return ref
 
     def line_copy(kind, n, src, dst_all):
@@ -1362,7 +1494,7 @@
     for n in peers:
         line_copy(2, n, place_buf, places).start()
     if early:
-        mine1[:, late:] = early_ref[...]
+        mine1[:, front:] = early_ref[...]
         for n in peers:
             line_copy(3, n, mine1, all1).start()
 
@@ -1399,6 +1531,10 @@
     small_copy(0).start()
     lax.fori_loop(0, geo.seq, add_up, 0)
 
+    for j in range(3):
+        mine1[:, late + j * LANES : late + (j + 1) * LANES] = by_document(
+            up_acc[j * lane_count : (j + 1) * lane_count, :].astype(BF16)
+        ).astype(BF16)
     mine1[:, :late] = set1.finish().astype(BF16)
     for n in peers:
         line_copy(0, n, mine1, all1).start()
@@ -1422,16 +1558,12 @@
     set2.run()
     grad_ref[...] = total
     place(0, mine1, all1)
-    for j in range(3):
-        mine2[:, (3 + j) * LANES : (4 + j) * LANES] = by_document(
-            up_acc[j * lane_count : (j + 1) * lane_count, :].astype(BF16)
-        ).astype(BF16)
-    mine2[:, : 3 * LANES] = set2.finish().astype(BF16)
+    mine2[...] = set2.finish().astype(BF16)
     for n in peers:
         line_copy(1, n, mine2, all2).start()
     pass_on(0)
+    place(1, mine2, all2)
     pass_last(0)
-    place(1, mine2, all2)
     pass_on(1)
     pass_last(1)
     for kind in range(2):
@@ -1472,8 +1604,8 @@
     lane_count = down.shape[0] // 4
     early = [] if early_sum is None else [early_sum]
     late = sum(v.shape[1] for v in grads) // geo.groups
-    set1 = late + sum(v.shape[1] for v in early)
-    set2 = 6 * LANES
+    set1 = late + 3 * LANES + sum(v.shape[1] for v in early)
+    set2 = 3 * LANES
     chips, near = geo.seq // 2, geo.groups // 2
     peers = geo.wt * geo.parts
     smem = pl.BlockSpec(memory_space=pltpu.SMEM)
@@ -1523,6 +1655,8 @@
             dma((2,)),
             dma((2,)),
             dma((2,)),
+            pltpu.VMEM((2, rows // 2, wide) if chips == 4 else (1, 16, LANES), BF16),
+            dma((2, 2)),
         ],
         compiler_params=pltpu.CompilerParams(
             collective_id=1, has_side_effects=True, vmem_limit_bytes=VMEM_LIMIT
@@ -1531,20 +1665,20 @@
     )(lengths, ids, tokens, d_first, dq, dk, dv, w_slice, down, up, small, *grads, *early)
 
 
-def unpack_kernel(one_ref, two_ref, down_ref, up_ref, fc1_down_ref, fc2_up_ref, fc1_up_ref, fc2_down_ref):
+def unpack_kernel(late, one_ref, two_ref, down_ref, up_ref, fc1_down_ref, fc2_up_ref, fc1_up_ref, fc2_down_ref):
     for j in range(3):
         down_ref[j] = two_ref[0, :, j * LANES : (j + 1) * LANES].astype(F32)
-        up_ref[j] = two_ref[0, :, (3 + j) * LANES : (4 + j) * LANES].astype(F32)
+    singles = [down_ref.at[3], up_ref.at[3], fc1_down_ref, fc2_up_ref, fc1_up_ref, fc2_down_ref]
     at = 0
-    for ref in (down_ref.at[3], up_ref.at[3], fc1_down_ref, fc2_up_ref, fc1_up_ref, fc2_down_ref):
+    for ref in singles[:late] + [up_ref.at[j] for j in range(3)] + singles[late:]:
         wide = ref.shape[1]
         ref[...] = one_ref[0, :, at : at + wide].astype(F32)
         at += wide
 
 
-def unpack(geo, one, two, lane_count):
+def unpack(geo, one, two, lane_count, late):
     groups = geo.groups
-    thick = (one.shape[2] - 4 * LANES) // 2
+    thick = (one.shape[2] - 7 * LANES) // 2
 
     def whole(wide):
         return jax.ShapeDtypeStruct((lane_count, wide * groups), F32)
@@ -1555,7 +1689,7 @@
     four = jax.ShapeDtypeStruct((4, lane_count, LANES * groups), F32)
     four_spec = pl.BlockSpec((4, lane_count, LANES), lambda i: (0, 0, i))
     return pl.pallas_call(
-        unpack_kernel,
+        functools.partial(unpack_kernel, late),
         grid=(groups,),
         out_shape=[four, four, whole(LANES), whole(LANES), whole(thick), whole(thick)],
         in_specs=[
@@ -1795,7 +1929,7 @@
         early_sum,
     )
 
-    down4, up4, fc1_down_sum, fc2_up_sum, fc1_up_sum, fc2_down_sum = unpack(geo, sum1, sum2, lane_count)
+    down4, up4, fc1_down_sum, fc2_up_sum, fc1_up_sum, fc2_down_sum = unpack(geo, sum1, sum2, lane_count, len(set1))
 
     def as_up(rows):
         return rows.reshape(rows.shape[:-2] + (adapter_count, rank_size, rows.shape[-1]))

time: 245 us -> 242 us (0.988)
  Pallas kernels: 241 us -> 237 us
    pallas_call x1, Pallas kernels: 74.7 us -> 70.5 us  [closing(): pl.pallas_call(functools.partial(closing_kernel, geo, rank, len(grads), l...]
where the time goes in v7:
time: 242 us; the launch traced here: 240 us
  Pallas kernels  237 us (98%)
  local copies, waits for them, and re-layouts  2.57 us (1%)
    pallas_call x1, Pallas kernels, forward_attention(): pl.pallas_call(functools.partial(forward_kernel, geo, inside, rank), out_...  139 us
    pallas_call x1, Pallas kernels, closing(): pl.pallas_call(functools.partial(closing_kernel, geo, rank, len(grads), l...  70.5 us
    pallas_call x1, Pallas kernels, backward_attention(): pl.pallas_call(functools.partial(backward_kernel, geo), out_shape=[jax.Sh...  19.7 us
    pallas_call x1, Pallas kernels, unpack(): pl.pallas_call(functools.partial(unpack_kernel, late), grid=(groups,), ou...  7.57 us

profile of v7, /device:TPU:0, one launch (start us, length us, event | category | flops | bytes accessed | tf_op | source)
XLA Modules:
  0.0 240.2 jit_solution(10468131890033294126)
XLA Ops:
  0.7 139.2 %layer.1 = (bf16[2048,128]{1,0:T(8,128)(2,1)}, bf16[2048,128]{1,0:T(8,128)(2,1)}, bf16[2048,128]{1,0:T(8,128)(2,1)}, f32[2048,128]{1,0:T(8,128)}, f32[2048,128]{...) custom-call(s32[1,4]{1,0:T(1,128)} %len_ref.5, ...), custom_call_target="tpu_custom_call" | custom-call | tf_op jit(solution)/shard_map/layer/pallas_call | solution.py:942
  139.9 19.7 %attend_back.1 = (bf16[2048,128]{1,0:T(8,128)(2,1)}, bf16[2048,128]{1,0:T(8,128)(2,1)}, bf16[2048,128]{1,0:T(8,128)(2,1)}) custom-call(s32[1,4]{1,0:T(1,128)} %len_ref.5, s32[1,1]{1,0:T(1,128)} %bitcast.16.part_ref, bf16[2048,128]{1,0:T(8,128)(2,1)} %get-tuple-element.36.q_ref, bf16[2048,128]{1,0:T(8,128)(2,1)} %get-tuple-element.37.k_ref, ...), custom_call_target="tpu_custom_call" | custom-call | tf_op jit(solution)/shard_map/attend_back/pallas_call | solution.py:1019
  159.5 70.5 %close.1 = (f32[256,1024]{1,0:T(8,128)}, bf16[8,128,1920]{2,1,0:T(8,128)(2,1)}, bf16[8,128,384]{2,1,0:T(8,128)(2,1)}, bf16[4,256,1152]{2,1,0:T(8,128)(2,1)}) custom-call(s32[1,4]{1,0:T(1,128)} %len_ref.5, s32[1,4]{1,0:T(1,128)} %id_ref.3, bf16[256,1024]{1,0:T(8,128)(2,1)} %tokens_ref.3, f32[256,1024]{1,0:T(8,128)} %get-tuple-element.35.first_ref, ...), custom_call_target="tpu_custom_call" | custom-call | tf_op jit(solution)/shard_map/close/pallas_call | solution.py:1616
  230.1 0.0 copy-start
  230.1 7.6 %unpack.1 = (f32[4,128,1024]{2,1,0:T(8,128)}, f32[4,128,1024]{2,1,0:T(8,128)}, f32[128,1024]{1,0:T(8,128)}, f32[128,1024]{1,0:T(8,128)}, f32[128,4096]{1,0:T(8,128)}, /*index=5*/f32[128,4096]{1,0:T(8,128)}) custom-call(bf16[8,128,1920]{2,1,0:T(8,128)(2,1)} %get-tuple-element.52.one_ref, bf16[8,128,384]{2,1,0:T(8,128)(2,1)} %get-tuple-element.53.two_ref), custom_call_target="tpu_custom_call" | custom-call | tf_op jit(solution)/shard_map/unpack/pallas_call | solution.py:1691
  237.6 0.0 copy-start.1
  237.6 0.0 copy-done
  237.6 1.0 copy.32
  238.6 0.6 copy-done.1
  239.2 1.0 copy.33
Async XLA Ops:
  230.1 7.6 %copy-start = (f32[256,1024]{1,0:T(8,128)S(1)}, f32[256,1024]{1,0:T(8,128)}, u32[]{:S(2)}) copy-start(f32[256,1024]{1,0:T(8,128)} %get-tuple-element.68) | copy-start | bytes 3145732
  237.6 1.6 copy-start.1

commit v8 on v7

--- a/solution.py
+++ b/solution.py
@@ -240,11 +240,13 @@
 MLP_OUTPUTS = ("output", "d_first", "d_heads", "g_out_down", "g_out_up", "g_fc1_down", "early_sum")
 BASE_SCRATCH = (
     "tok", "seg", "att_send_buf", "local_sem", "send_sem", "recv_sem", "slice_send", "slice_recv", "line_send",
-    "line_recv", "att_send", "att_recv",
+    "line_recv", "att_send", "att_recv", "q_buf", "k_buf", "v_buf", "o_buf", "lse_buf", "slice_buf", "small_buf", "flush_sem",
 )
+LATER = ("cotangent", "fc1_down", "fc1_up", "fc2_down", "fc2_up")
 MLP_SCRATCH = (
     "att", "full_out", "full_fc1", "full_fc2", "unit1", "h1", "h1_low", "act", "slope", "d_pre", "y", "d_att_buf",
     "back_send", "back_recv", "g_fc2_up", "g_fc1_up", "g_fc2_down", "set_out", "set_in", "set_far", "set_sems",
+    "load_sem", "cotangent_buf", "fc1_down_buf", "fc1_up_buf", "fc2_down_buf", "fc2_up_buf",
 )
 
 
@@ -257,8 +259,17 @@
     weights_out = (r.full_out, r.full_fc1, r.full_fc2) if inside else ()
     weight_count = len(weights_in)
     att_ref, q_ref, k_ref, v_ref, o_ref, lse_ref, slice_ref, small_ref = (
-        r.att, r.q, r.k, r.v, r.o, r.lse, r.w_slice, r.small
+        r.att, r.q_buf, r.k_buf, r.v_buf, r.o_buf, r.lse_buf, r.slice_buf, r.small_buf
     )
+    results = [r.q, r.k, r.v, r.o, r.lse, r.w_slice, r.small]
+    made = [q_ref, k_ref, v_ref, o_ref, lse_ref, slice_ref, small_ref]
+    flushes = [pltpu.make_async_copy(made[i], results[i], r.flush_sem.at[i]) for i in range(len(made))]
+    loads = []
+    if inside:
+        loads = [
+            pltpu.make_async_copy(getattr(r, name), getattr(r, name + "_buf"), r.load_sem.at[i])
+            for i, name in enumerate(LATER)
+        ]
     tok_buf, seg_buf, att_buf, local_sem = r.tok, r.seg, r.att_send_buf, r.local_sem
     send_sem, recv_sem, slice_send, slice_recv = r.send_sem, r.recv_sem, r.slice_send, r.slice_recv
     line_send, line_recv, att_send, att_recv = r.line_send, r.line_recv, r.att_send, r.att_recv
@@ -308,6 +319,9 @@
             device_id=(s, w + 1 if up else w - 1),
             device_id_type=MESH,
         )
+
+    for copy in loads:
+        copy.start()
 
     starts, ends = doc_bounds(len_ref)
     seg_buf[...] = segment_from(lax.broadcasted_iota(jnp.int32, seg_buf.shape, 1), starts)
@@ -605,6 +619,8 @@
         return carry
 
     lax.fori_loop(0, geo.groups, attend, 0)
+    for copy in flushes:
+        copy.start()
     own_att = pltpu.make_async_copy(att_buf.at[g], att_ref.at[:, lanes], local_sem.at[0])
     own_att.start()
 
@@ -623,10 +639,16 @@
         own_att.wait()
 
     if inside:
+        for copy in loads:
+            copy.wait()
+        for name in LATER:
+            setattr(r, name, getattr(r, name + "_buf"))
         layer_rest(geo, rank, r, starts, ends, id_ref, down_ref, up_ref, att_arrivals, complete, tick, loop_ticks, tick_count, len_ref.shape[1])
     else:
         att_arrivals()
 
+    for copy in flushes:
+        copy.wait()
     for d in range(1, geo.groups):
         att_copy((g + d) % geo.groups).wait_send()
     tok.wait_sends()
@@ -880,7 +902,7 @@
         struct((width, 3 * LANES), BF16),
         struct((geo.keys, 3 * LANES), BF16),
     ]
-    specs = [vmem] * 7
+    specs = [any_spec] * 7
     dma = pltpu.SemaphoreType.DMA
     count = 3 if inside else 0
     units = 1 + count * geo.wt
@@ -898,6 +920,7 @@
         dma((geo.groups,)),
         dma((geo.groups,)),
     ]
+    scratch += [pltpu.VMEM(v.shape, v.dtype) for v in shapes] + [dma((len(shapes),))]
     if inside:
         hidden = mlp[1].shape[1]
         doc_rows = lengths.shape[1] * rank
@@ -935,14 +958,18 @@
             pltpu.VMEM((near, doc_rows, early), BF16),
             pltpu.VMEM((near, doc_rows, early), BF16),
             dma((4, near)),
+            dma((len(LATER),)),
         ]
+        scratch += [pltpu.VMEM(v.shape, v.dtype) for name, v in zip(MLP_INPUTS, mlp) if name in LATER]
     else:
         shapes += [struct((rows, width), BF16)]
         specs += [any_spec]
     return pl.pallas_call(
         functools.partial(forward_kernel, geo, inside, rank),
         out_shape=shapes,
-        in_specs=[smem, smem, any_spec, any_spec, vmem, vmem, vmem] + [any_spec] * count + [vmem] * (len(mlp) - count),
+        in_specs=[smem, smem, any_spec, any_spec, vmem, vmem, vmem] + [
+            any_spec if i < count or name in LATER else vmem for i, name in enumerate(MLP_INPUTS[: len(mlp)])
+        ],
         out_specs=specs,
         scratch_shapes=scratch,
         compiler_params=pltpu.CompilerParams(
@@ -952,13 +979,19 @@
     )(lengths, ids, tokens, w_qkv, down, up, bias, *mlp)
 
 
-def backward_kernel(geo, len_ref, part_ref, q_ref, k_ref, v_ref, o_ref, lse_ref, g_ref, dq_ref, dk_ref, dv_ref, dk_acc, dv_acc):
+def backward_kernel(
+    geo, len_ref, part_ref, q_ref, k_ref, v_ref, o_ref, lse_ref, g_ref, pass_ref, dq_ref, dk_ref, dv_ref, passed_ref,
+    dk_acc, dv_acc, pass_buf, pass_sem,
+):
     rows = min(512, geo.queries)
     block = min(512, geo.keys)
     part = part_ref[0, 0]
     scale = HEAD_DIM ** (-0.5)
     starts, ends = doc_bounds(len_ref)
     first_head = lax.broadcasted_iota(jnp.int32, (rows, LANES), 1) < HEAD_DIM
+    fetch = pltpu.make_async_copy(pass_ref, pass_buf, pass_sem.at[0])
+    store = pltpu.make_async_copy(pass_buf, passed_ref, pass_sem.at[1])
+    fetch.start()
     dk_acc[...] = jnp.zeros_like(dk_acc)
     dv_acc[...] = jnp.zeros_like(dv_acc)
 
@@ -1008,12 +1041,17 @@
         dq_ref[at, :] = jnp.where(first_head, acc[:rows], acc[rows:]).astype(BF16)
         return carry
 
-    lax.fori_loop(0, geo.queries // rows, query_block, 0)
+    query_block(0, 0)
+    fetch.wait()
+    store.start()
+    lax.fori_loop(1, geo.queries // rows, query_block, 0)
     dk_ref[...] = (dk_acc[...] * HEAD_DIM**0.5).astype(BF16)
     dv_ref[...] = dv_acc[...].astype(BF16)
-
-
-def backward_attention(geo, lengths, part, q, k, v, o, lse, d_heads):
+    store.wait()
+
+
+def backward_attention(geo, lengths, part, q, k, v, o, lse, d_heads, output):
+    any_spec = pl.BlockSpec(memory_space=pl.ANY)
     smem = pl.BlockSpec(memory_space=pltpu.SMEM)
     vmem = pl.BlockSpec(memory_space=pltpu.VMEM)
     return pl.pallas_call(
@@ -1022,13 +1060,15 @@
             jax.ShapeDtypeStruct((geo.queries, LANES), BF16),
             jax.ShapeDtypeStruct((geo.keys, LANES), BF16),
             jax.ShapeDtypeStruct((geo.keys, LANES), BF16),
+            jax.ShapeDtypeStruct(output.shape, F32),
         ],
-        in_specs=[smem, smem] + [vmem] * 6,
-        out_specs=[vmem] * 3,
-        scratch_shapes=[pltpu.VMEM((geo.keys, LANES), F32)] * 2,
+        in_specs=[smem, smem] + [vmem] * 6 + [any_spec],
+        out_specs=[vmem] * 3 + [any_spec],
+        scratch_shapes=[pltpu.VMEM((geo.keys, LANES), F32)] * 2
+        + [pltpu.VMEM(output.shape, F32), pltpu.SemaphoreType.DMA((2,))],
         compiler_params=pltpu.CompilerParams(vmem_limit_bytes=VMEM_LIMIT),
         name="attend_back",
-    )(lengths, part, q, k, v, o, lse, d_heads)
+    )(lengths, part, q, k, v, o, lse, d_heads, output)
 
 
 class Block:
@@ -1908,8 +1948,8 @@
             (stack_down(fc2_down), stack_up(fc2_up)),
             select_local(tok_rows, lane_count, rank_size, doc_lengths[0], adapter_ids[0]),
         )
-    d_q, d_k, d_v = backward_attention(
-        geo, doc_lengths, part_index.reshape(1, 1), q_heads, k_heads, v_heads, o_heads, lse_heads, d_heads
+    d_q, d_k, d_v, output = backward_attention(
+        geo, doc_lengths, part_index.reshape(1, 1), q_heads, k_heads, v_heads, o_heads, lse_heads, d_heads, output
     )
     input_grad, sum1, sum2, _ = closing(
         geo,

time: 242 us -> 238 us (0.983)
  Pallas kernels: 237 us -> 234 us
    pallas_call x1, Pallas kernels: 139 us -> 137 us  [forward_attention(): pl.pallas_call(functools.partial(forward_kernel, geo, inside, rank), out_...]
where the time goes in v8:
time: 238 us; the launch traced here: 236 us
  Pallas kernels  234 us (98%)
    pallas_call x1, Pallas kernels, forward_attention(): pl.pallas_call(functools.partial(forward_kernel, geo, inside, rank), out_...  137 us
    pallas_call x1, Pallas kernels, closing(): pl.pallas_call(functools.partial(closing_kernel, geo, rank, len(grads), l...  70.4 us
    pallas_call x1, Pallas kernels, backward_attention(): pl.pallas_call(functools.partial(backward_kernel, geo), out_shape=[jax.Sh...  19.5 us
    pallas_call x1, Pallas kernels, unpack(): pl.pallas_call(functools.partial(unpack_kernel, late), grid=(groups,), ou...  7.57 us

profile of v8, /device:TPU:0, one launch (start us, length us, event | category | flops | bytes accessed | tf_op | source)
XLA Modules:
  0.0 235.9 jit_solution(15071711034712883041)
XLA Ops:
  0.7 136.7 %layer.1 = (bf16[2048,128]{1,0:T(8,128)(2,1)}, bf16[2048,128]{1,0:T(8,128)(2,1)}, bf16[2048,128]{1,0:T(8,128)(2,1)}, f32[2048,128]{1,0:T(8,128)}, f32[2048,128]{...) custom-call(s32[1,4]{1,0:T(1,128)} %len_ref.5, ...), custom_call_target="tpu_custom_call" | custom-call | tf_op jit(solution)/shard_map/layer/pallas_call | solution.py:967
  137.4 19.5 %attend_back.1 = (bf16[2048,128]{1,0:T(8,128)(2,1)}, bf16[2048,128]{1,0:T(8,128)(2,1)}, bf16[2048,128]{1,0:T(8,128)(2,1)}, f32[256,1024]{1,0:T(8,128)}) custom-call(s32[1,4]{1,0:T(1,128)} %len_ref.5, s32[1,1]{1,0:T(1,128)} %bitcast.part_ref, bf16[2048,128]{1,0:T(8,128)(2,1)} %get-tuple-element.35.q_ref, bf16[2048,128]{1,0:T(8,128)(2,1)} %get-tuple-element.36.k_ref, ...), custom_call_target="tpu_custom_call" | custom-call | tf_op jit(solution)/shard_map/attend_back/pallas_call | solution.py:1057
  156.9 70.4 %close.1 = (f32[256,1024]{1,0:T(8,128)}, bf16[8,128,1920]{2,1,0:T(8,128)(2,1)}, bf16[8,128,384]{2,1,0:T(8,128)(2,1)}, bf16[4,256,1152]{2,1,0:T(8,128)(2,1)}) custom-call(s32[1,4]{1,0:T(1,128)} %len_ref.5, s32[1,4]{1,0:T(1,128)} %id_ref.3, bf16[256,1024]{1,0:T(8,128)(2,1)} %tokens_ref.3, f32[256,1024]{1,0:T(8,128)} %get-tuple-element.43.first_ref, ...), custom_call_target="tpu_custom_call" | custom-call | tf_op jit(solution)/shard_map/close/pallas_call | solution.py:1656
  227.3 0.0 copy-start
  227.3 7.6 %unpack.1 = (f32[4,128,1024]{2,1,0:T(8,128)}, f32[4,128,1024]{2,1,0:T(8,128)}, f32[128,1024]{1,0:T(8,128)}, f32[128,1024]{1,0:T(8,128)}, f32[128,4096]{1,0:T(8,128)}, /*index=5*/f32[128,4096]{1,0:T(8,128)}) custom-call(bf16[8,128,1920]{2,1,0:T(8,128)(2,1)} %get-tuple-element.54.one_ref, bf16[8,128,384]{2,1,0:T(8,128)(2,1)} %get-tuple-element.55.two_ref), custom_call_target="tpu_custom_call" | custom-call | tf_op jit(solution)/shard_map/unpack/pallas_call | solution.py:1731
  234.9 0.0 copy-done
  234.9 1.0 copy.31
Async XLA Ops:
  227.3 7.6 %copy-start = (f32[256,1024]{1,0:T(8,128)S(1)}, f32[256,1024]{1,0:T(8,128)}, u32[]{:S(2)}) copy-start(f32[256,1024]{1,0:T(8,128)} %get-tuple-element.71) | copy-start | bytes 3145732
